TPU v7x, 32 devices: a whole 2x2x4 slice. The times are simulated.
32 devices in a mesh: dp: 4 (over x, core), context: 2 (over y), tensor: 4 (over z).
Axes of the slice: x: 2, y: 2, z: 4, core: 2. Of those that a mesh axis runs over, the one named last changes fastest.
Arguments:
- layer_input_hidden: bfloat16 [4, 2048, 2560], P('dp', 'context', 'tensor'), may hold values from -60 to 60
- cotangent: bfloat16 [4, 2048, 2560], P('dp', 'context', 'tensor'), may hold values from -6 to 6
- valid_mask: int32 [4, 2048], P('dp'), may hold values from 0 to 1, as said below
- span_starts: int32 [4, 2], P('dp'), may hold values from 769 to 1792, as said below
- gain_attn: float32 [2560], P('tensor'), may hold values from 0.5 to 1.5
- w_query: bfloat16 [2560, 2560], P(None, 'tensor'), may hold values from -0.125 to 0.125
- w_key: bfloat16 [2560, 640], P(None, 'tensor'), may hold values from -0.125 to 0.125
- w_value: bfloat16 [2560, 640], P(None, 'tensor'), may hold values from -0.125 to 0.125
- w_out: bfloat16 [2560, 2560], P('tensor'), may hold values from -0.75 to 0.75
- gain_mlp: float32 [2560], P('tensor'), may hold values from 0.5 to 1.5
- w_gate: bfloat16 [2560, 7168], P(None, 'tensor'), may hold values from -0.125 to 0.125
- w_up: bfloat16 [2560, 7168], P(None, 'tensor'), may hold values from -0.125 to 0.125
- w_down: bfloat16 [7168, 2560], P('tensor'), may hold values from -0.125 to 0.125
Outputs:
- layer_out: bfloat16 [4, 2048, 2560], P('dp', 'context', 'tensor')
- input_grad: bfloat16 [4, 2048, 2560], P('dp', 'context', 'tensor')
- attention_gain_gradient: float32 [2560], P('tensor')
- query_grad: float32 [2560, 2560], P(('dp', 'context'), 'tensor')
- key_grad: float32 [2560, 640], P(('dp', 'context'), 'tensor')
- value_grad: float32 [2560, 640], P(('dp', 'context'), 'tensor')
- out_grad: float32 [2560, 2560], P('tensor', ('dp', 'context'))
- gain_mlp_grad: float32 [2560], P('tensor')
- gate_grad: float32 [2560, 7168], P(('dp', 'context'), 'tensor')
- up_grad: float32 [2560, 7168], P(('dp', 'context'), 'tensor')
- down_grad: float32 [7168, 2560], P('tensor', ('dp', 'context'))
- stream_rms: float32 [], replicated
- attention_rms: float32 [], replicated
- feedforward_rms: float32 [], replicated
Inputs may be any that keep to these rules, and one draw needn't show every extreme that they name: `valid_mask`: A sequence's valid tokens are its first ones, 1536 of them or more; one sequence, drawn from the seed, is valid throughout. `span_starts`: the first span of a sequence contains positions 1023 and 1024; the second begins at 1280 or later and ends inside the sequence.
All inputs are finite; a program needn't handle non-finite values.
Results may differ from a plain program's by a relative error of at most 0.025.
Values may be sent and summed in bfloat16 or wider, within the bound.
A program may use at most 320 MiB of HBM per device.

v0:
```python
import jax
import jax.numpy as jnp
from jax import lax
from jax.sharding import PartitionSpec as P

D = 2560
HD = 80
LEN = 2048
PIC = 256


epsilon = 1e-05
rope_base = 1000000.0


def rope_tables(offset, count_rows):
    halves = jnp.arange(HD // 2, dtype=jnp.float32)
    inverse = rope_base ** (-2.0 * halves / HD)
    positions = (offset + jnp.arange(count_rows, dtype=jnp.int32)).astype(jnp.float32)
    angles = positions[:, None] * inverse[None, :]
    return (jnp.cos(angles), jnp.sin(angles))


def rotate(vectors, cos_tab, sin_tab):
    lower_half = vectors[..., : HD // 2]
    upper_half = vectors[..., HD // 2 :]
    cos_b = cos_tab[:, None, :]
    sin_b = sin_tab[:, None, :]
    return jnp.concatenate(
        [lower_half * cos_b - upper_half * sin_b, upper_half * cos_b + lower_half * sin_b], -1
    )


def span_index(span_starts):
    positions = jnp.arange(LEN, dtype=jnp.int32)
    inside = (positions[None, None, :] >= span_starts[:, :, None]) & (
        positions[None, None, :] < span_starts[:, :, None] + PIC
    )
    labels = jnp.arange(1, span_starts.shape[1] + 1, dtype=jnp.int32)[None, :, None]
    return jnp.sum(jnp.where(inside, labels, 0), axis=1) - 1


def project(left_operand, right_operand):
    return jnp.einsum(
        "scd,dx->scx", left_operand, right_operand, preferred_element_type=jnp.float32
    )


def row_sums(stacked):
    return lax.psum(stacked, "tensor")


def normalize(stream, gain, extras):
    square_sums = jnp.sum(stream * stream, -1)
    totals = row_sums(jnp.stack([square_sums] + extras))
    inverse = lax.rsqrt(totals[0] / D + epsilon)
    scaled = (stream * inverse[..., None] * gain).astype(jnp.bfloat16)
    gathered = lax.all_gather(scaled, "tensor", axis=2, tiled=True)
    return (gathered, inverse, totals)


def norm_back(gradient, stream, inverse, gain, extras):
    normed = stream * inverse[..., None]
    weighted = gradient * gain
    totals = row_sums(jnp.stack([jnp.sum(weighted * normed, -1)] + extras))
    through = inverse[..., None] * (weighted - normed * (totals[0] / D)[..., None])
    gain_grad = jnp.sum(gradient * normed, (0, 1))
    return (through, gain_grad, totals)


def branch_sum(partial_value):
    return lax.psum_scatter(
        partial_value.astype(jnp.bfloat16), "tensor", scatter_dimension=2, tiled=True
    ).astype(jnp.float32)


def gather_cot(gradient):
    return lax.all_gather(gradient.astype(jnp.bfloat16), "tensor", axis=2, tiled=True)


def input_sum(partial_value):
    return lax.psum_scatter(
        partial_value.astype(jnp.bfloat16), "tensor", scatter_dimension=2, tiled=True
    ).astype(jnp.float32)


def scores_for(query_block, key_seq, valid_row, span_row, block_positions):
    raw_scores = jnp.einsum(
        "bkgd,jkd->kgbj", query_block, key_seq, preferred_element_type=jnp.float32
    )
    columns = jnp.arange(key_seq.shape[0], dtype=jnp.int32)
    span_here = lax.dynamic_slice_in_dim(span_row, block_positions[0], block_positions.shape[0], 0)
    same_span = (span_here[:, None] >= 0) & (span_here[:, None] == span_row[None, :])
    allowed = (valid_row[None, :] > 0) & (
        (columns[None, :] <= block_positions[:, None]) | same_span
    )
    return jnp.where(allowed[None, None], raw_scores * HD ** (-0.5), -jnp.inf)


def attend_forward(query_seq, key_seq, value_seq, valid_row, span_row, offset):
    local_rows = query_seq.shape[0]
    block_rows = min(512, local_rows)
    blocks = local_rows // block_rows
    positions = (offset + jnp.arange(local_rows, dtype=jnp.int32)).reshape(blocks, block_rows)
    query_blocks = query_seq.reshape((blocks, block_rows) + query_seq.shape[1:])

    def one_block(pieces):
        query_block, block_positions = pieces
        scores = scores_for(query_block, key_seq, valid_row, span_row, block_positions)
        row_max = jnp.max(scores, -1, keepdims=True)
        shifted = jnp.exp(scores - row_max)
        row_total = jnp.sum(shifted, -1, keepdims=True)
        attn_probs = (shifted / row_total).astype(jnp.bfloat16)
        mixed = jnp.einsum(
            "kgbj,jkd->bkgd", attn_probs, value_seq, preferred_element_type=jnp.float32
        )
        return (mixed, row_max[..., 0] + jnp.log(row_total[..., 0]))

    mixed, logsum = lax.map(one_block, (query_blocks, positions))
    return (mixed.reshape(query_seq.shape), logsum)


def attend_backward(query_seq, key_seq, value_seq, grad_seq, logsum, valid_row, span_row, offset):
    local_rows = query_seq.shape[0]
    block_rows = min(512, local_rows)
    blocks = local_rows // block_rows
    positions = (offset + jnp.arange(local_rows, dtype=jnp.int32)).reshape(blocks, block_rows)
    query_blocks = query_seq.reshape((blocks, block_rows) + query_seq.shape[1:])
    grad_blocks = grad_seq.reshape((blocks, block_rows) + grad_seq.shape[1:])

    def one_block(accum, pieces):
        key_acc, value_acc = accum
        query_block, grad_block, block_logsum, block_positions = pieces
        scores = scores_for(query_block, key_seq, valid_row, span_row, block_positions)
        attn_probs = jnp.exp(scores - block_logsum[..., None])
        probs_low = attn_probs.astype(jnp.bfloat16)
        grad_probs = jnp.einsum(
            "bkgd,jkd->kgbj", grad_block, value_seq, preferred_element_type=jnp.float32
        )
        row_dot = jnp.sum(grad_probs * attn_probs, -1, keepdims=True)
        grad_scores = (HD ** (-0.5) * attn_probs * (grad_probs - row_dot)).astype(jnp.bfloat16)
        grad_query = jnp.einsum(
            "kgbj,jkd->bkgd", grad_scores, key_seq, preferred_element_type=jnp.float32
        )
        key_acc = key_acc + jnp.einsum(
            "kgbj,bkgd->jkd", grad_scores, query_block, preferred_element_type=jnp.float32
        )
        value_acc = value_acc + jnp.einsum(
            "kgbj,bkgd->jkd", probs_low, grad_block, preferred_element_type=jnp.float32
        )
        return ((key_acc, value_acc), grad_query)

    start_acc = (jnp.zeros(key_seq.shape, jnp.float32), jnp.zeros(value_seq.shape, jnp.float32))
    (key_acc, value_acc), grad_query = lax.scan(
        one_block, start_acc, (query_blocks, grad_blocks, logsum, positions)
    )
    return (grad_query.reshape(query_seq.shape), key_acc, value_acc)


def local(
    layer_input_hidden,
    cotangent,
    valid_mask,
    span_starts,
    gain_attn,
    w_query,
    w_key,
    w_value,
    w_out,
    gain_mlp,
    w_gate,
    w_up,
    w_down,
):
    seq_count, local_rows, feature_part = layer_input_hidden.shape
    kv_count = w_key.shape[1] // HD
    head_count = w_query.shape[1] // HD
    group_size = head_count // kv_count
    offset = lax.axis_index("context") * local_rows
    cos_tab, sin_tab = rope_tables(offset, local_rows)
    span_ids = span_index(span_starts)
    keep_mask = lax.dynamic_slice_in_dim(valid_mask, offset, local_rows, 1).astype(jnp.float32)
    keep_col = keep_mask[..., None]
    stream = layer_input_hidden.astype(jnp.float32)
    normed_a, inverse_a, totals_a = normalize(stream, gain_attn, [])
    query_pre = project(normed_a, w_query).reshape(seq_count, local_rows, head_count, HD)
    key_pre = project(normed_a, w_key).reshape(seq_count, local_rows, kv_count, HD)
    value_low = (
        project(normed_a, w_value).astype(jnp.bfloat16).reshape(seq_count, local_rows, kv_count, HD)
    )
    query_rot = (
        rotate(query_pre, cos_tab, sin_tab)
        .astype(jnp.bfloat16)
        .reshape(seq_count, local_rows, kv_count, group_size, HD)
    )
    key_rot = rotate(key_pre, cos_tab, sin_tab).astype(jnp.bfloat16)
    key_all, value_all = (
        lax.all_gather(key_rot, "context", axis=1, tiled=True),
        lax.all_gather(value_low, "context", axis=1, tiled=True),
    )
    mixed, logsum = lax.map(
        lambda pieces: attend_forward(*pieces, offset),
        (query_rot, key_all, value_all, valid_mask, span_ids),
    )
    attended = mixed.reshape(seq_count, local_rows, head_count * HD).astype(jnp.bfloat16)
    attn_out = keep_col * branch_sum(project(attended, w_out))
    middle = stream + attn_out
    normed_m, inverse_m, totals_m = normalize(middle, gain_mlp, [jnp.sum(attn_out * attn_out, -1)])
    gate_val = project(normed_m, w_gate)
    up_val = project(normed_m, w_up)
    gate_sig = jax.nn.sigmoid(gate_val)
    activated = (gate_val * gate_sig * up_val).astype(jnp.bfloat16)
    ffn_out = keep_col * branch_sum(project(activated, w_down))
    layer_out = (middle + ffn_out).astype(jnp.bfloat16)
    grad_out = cotangent.astype(jnp.float32)
    grad_ffn = gather_cot(keep_col * grad_out)
    down_grad = jnp.einsum("scf,scd->fd", activated, grad_ffn, preferred_element_type=jnp.float32)
    activation_gradient = jnp.einsum(
        "scd,fd->scf", grad_ffn, w_down, preferred_element_type=jnp.float32
    )
    grad_gate = (
        activation_gradient * up_val * gate_sig * (1.0 + gate_val * (1.0 - gate_sig))
    ).astype(jnp.bfloat16)
    grad_up = (activation_gradient * gate_val * gate_sig).astype(jnp.bfloat16)
    gate_grad = jnp.einsum("scd,scf->df", normed_m, grad_gate, preferred_element_type=jnp.float32)
    up_grad = jnp.einsum("scd,scf->df", normed_m, grad_up, preferred_element_type=jnp.float32)
    grad_normed_m = input_sum(
        jnp.einsum("scf,df->scd", grad_gate, w_gate, preferred_element_type=jnp.float32)
        + jnp.einsum("scf,df->scd", grad_up, w_up, preferred_element_type=jnp.float32)
    )
    through_m, gain_m_grad, back_m = norm_back(
        grad_normed_m, middle, inverse_m, gain_mlp, [jnp.sum(ffn_out * ffn_out, -1)]
    )
    grad_middle = grad_out + through_m
    grad_attn = gather_cot(keep_col * grad_middle)
    out_grad = jnp.einsum("scx,scd->xd", attended, grad_attn, preferred_element_type=jnp.float32)
    grad_attended = jnp.einsum(
        "scd,xd->scx", grad_attn, w_out, preferred_element_type=jnp.float32
    ).astype(jnp.bfloat16)
    grad_attended = grad_attended.reshape(seq_count, local_rows, kv_count, group_size, HD)
    grad_query_rot, grad_key_all, grad_value_all = lax.map(
        lambda pieces: attend_backward(*pieces, offset),
        (query_rot, key_all, value_all, grad_attended, logsum, valid_mask, span_ids),
    )
    grad_key_rot, grad_value_loc = (
        lax.psum_scatter(
            grad_key_all.astype(jnp.bfloat16), "context", scatter_dimension=1, tiled=True
        ).astype(jnp.float32),
        lax.psum_scatter(
            grad_value_all.astype(jnp.bfloat16), "context", scatter_dimension=1, tiled=True
        ).astype(jnp.float32),
    )
    grad_query = (
        rotate(grad_query_rot.reshape(seq_count, local_rows, head_count, HD), cos_tab, -sin_tab)
        .astype(jnp.bfloat16)
        .reshape(seq_count, local_rows, head_count * HD)
    )
    grad_key = (
        rotate(grad_key_rot, cos_tab, -sin_tab)
        .astype(jnp.bfloat16)
        .reshape(seq_count, local_rows, kv_count * HD)
    )
    grad_value = grad_value_loc.astype(jnp.bfloat16).reshape(seq_count, local_rows, kv_count * HD)
    query_grad = jnp.einsum("scd,scx->dx", normed_a, grad_query, preferred_element_type=jnp.float32)
    key_grad = jnp.einsum("scd,scx->dx", normed_a, grad_key, preferred_element_type=jnp.float32)
    value_grad = jnp.einsum("scd,scx->dx", normed_a, grad_value, preferred_element_type=jnp.float32)
    grad_partial = jnp.einsum(
        "scx,dx->scd", grad_query, w_query, preferred_element_type=jnp.float32
    )
    grad_partial = grad_partial + jnp.einsum(
        "scx,dx->scd", grad_key, w_key, preferred_element_type=jnp.float32
    )
    grad_partial = grad_partial + jnp.einsum(
        "scx,dx->scd", grad_value, w_value, preferred_element_type=jnp.float32
    )
    grad_normed_a = input_sum(grad_partial)
    through_a, gain_a_grad, back_a = norm_back(grad_normed_a, stream, inverse_a, gain_attn, [])
    input_grad = (grad_middle + through_a).astype(jnp.bfloat16)
    query_sum, key_sum, value_sum, out_sum, gate_sum, up_sum, down_sum = (
        lax.psum_scatter(
            query_grad.astype(jnp.bfloat16), ("dp", "context"), scatter_dimension=0, tiled=True
        ).astype(jnp.float32),
        lax.psum_scatter(
            key_grad.astype(jnp.bfloat16), ("dp", "context"), scatter_dimension=0, tiled=True
        ).astype(jnp.float32),
        lax.psum_scatter(
            value_grad.astype(jnp.bfloat16), ("dp", "context"), scatter_dimension=0, tiled=True
        ).astype(jnp.float32),
        lax.psum_scatter(
            out_grad.astype(jnp.bfloat16), ("dp", "context"), scatter_dimension=1, tiled=True
        ).astype(jnp.float32),
        lax.psum_scatter(
            gate_grad.astype(jnp.bfloat16), ("dp", "context"), scatter_dimension=0, tiled=True
        ).astype(jnp.float32),
        lax.psum_scatter(
            up_grad.astype(jnp.bfloat16), ("dp", "context"), scatter_dimension=0, tiled=True
        ).astype(jnp.float32),
        lax.psum_scatter(
            down_grad.astype(jnp.bfloat16), ("dp", "context"), scatter_dimension=1, tiled=True
        ).astype(jnp.float32),
    )
    statistics = jnp.stack(
        [
            jnp.sum(keep_mask * totals_a[0]),
            jnp.sum(keep_mask * totals_m[1]),
            jnp.sum(keep_mask * back_m[1]),
            jnp.sum(keep_mask),
        ]
    )
    attention_gain_total, gain_m_sum, reduced = lax.psum(
        (gain_a_grad, gain_m_grad, statistics), ("dp", "context")
    )
    denominator = reduced[3] * D
    stream_rms = jnp.sqrt(reduced[0] / denominator)
    attention_rms = jnp.sqrt(reduced[1] / denominator)
    feedforward_rms = jnp.sqrt(reduced[2] / denominator)
    return (
        layer_out,
        input_grad,
        attention_gain_total,
        query_sum,
        key_sum,
        value_sum,
        out_sum,
        gain_m_sum,
        gate_sum,
        up_sum,
        down_sum,
        stream_rms,
        attention_rms,
        feedforward_rms,
    )


def solution(mesh):
    placed = (
        P("dp", "context", "tensor"),
        P("dp", "context", "tensor"),
        P("dp", None),
        P("dp", None),
        P("tensor"),
        P(None, "tensor"),
        P(None, "tensor"),
        P(None, "tensor"),
        P("tensor", None),
        P("tensor"),
        P(None, "tensor"),
        P(None, "tensor"),
        P("tensor", None),
    )
    return jax.shard_map(
        local,
        mesh=mesh,
        in_specs=placed,
        out_specs=(
            P("dp", "context", "tensor"),
            P("dp", "context", "tensor"),
            P("tensor"),
            P(("dp", "context"), "tensor"),
            P(("dp", "context"), "tensor"),
            P(("dp", "context"), "tensor"),
            P("tensor", ("dp", "context")),
            P("tensor"),
            P(("dp", "context"), "tensor"),
            P(("dp", "context"), "tensor"),
            P("tensor", ("dp", "context")),
            P(),
            P(),
            P(),
        ),
        check_vma=False,
    )
```

profile of v0, /device:TPU:0, one launch (start us, length us, event | category | flops | bytes accessed | tf_op | source)
XLA Modules:
  0.0 1891.8 jit_solution(10953451772071269756)
XLA Ops:
  33.1 89.2 %all-gather.5.cloned.1.call-done = bf16[1,1024,2560]{2,1,0:T(8,128)(2,1)} async-done(((bf16[1,1024,640]{2,1,0:T(8,128)(2,1)}), bf16[1,1024,2560]{2,1,0:T(8,128)(2,1)}) %all-gather.5.cloned.1.call-update) | async-done | bytes 5242896 | tf_op jit(solution)/shard_map/all_gather | solution.py:58
  163.4 101.8 %while.47 = (s32[]{:T(128)}, bf16[2,512,2,4,80]{1,4,3,2,0:T(8,128)(2,1)}, f32[2,2,4,512]{3,2,1,0:T(4,128)S(1)}, s32[2048]{0:T(1024)S(1)}, s32[2,512]{1,0:T(2,128...) while((s32[]{:T(128)}, ...), condition=%wide.region_6.7_spmd, body=%wide.region_3.6_spmd.sunk | while | flops 2790259200 | bytes 112493784 | solution.py:119
  306.3 92.2 %reduce-scatter.40.cloned.1.call-done = bf16[640,1024]{1,0:T(8,128)(2,1)} async-done(((bf16[2560,1024]{1,0:T(8,128)(2,1)}), bf16[640,1024]{1,0:T(8,128)(2,1)}) %reduce-scatter.40.cloned.1.call-update) | async-done | bytes 1310736
  427.7 96.0 %all-gather.7.cloned.1.call-done = bf16[1,1024,2560]{2,1,0:T(8,128)(2,1)} async-done(((bf16[1,1024,640]{2,1,0:T(8,128)(2,1)}), bf16[1,1024,2560]{2,1,0:T(8,128)(2,1)}) %all-gather.7.cloned.1.call-update) | async-done | bytes 5242896 | tf_op jit(solution)/shard_map/all_gather | solution.py:58
  555.4 66.8 %all-gather.9.cloned.1.call-done = bf16[1,1024,2560]{2,1,0:T(8,128)(2,1)} async-done(((bf16[1,1024,640]{2,1,0:T(8,128)(2,1)}), bf16[1,1024,2560]{2,1,0:T(8,128)(2,1)}) %all-gather.9.cloned.1.call-update) | async-done | bytes 5242896 | tf_op jit(solution)/shard_map/all_gather | solution.py:78
  622.2 22.3 %multiply_convert_fusion = (bf16[1024,1792]{1,0:T(8,128)(2,1)}, bf16[1024,1792]{1,0:T(8,128)(2,1)}, bf16[1024,1792]{1,0:T(8,128)(2,1)}) fusion(f32[1024,1792]{1,0:T(8,128)} %fusion.62, f32[1024,1792]{1,0:T(8,128)} %fusion.60, bf16[1792,2560]{1,0:T(8,128)(2,1)} %param.29, bf16[1,1024,2560]{2,1,0:T(8,128)(2,1)} %all-gather.9.cloned.1.call-done), kind=kOutput, calls=%fused_computation.72 | convolution fusion | flops 9424601088 | bytes 40108032 | tf_op jit(solution)/shard_map/scd,fd->scf/dot_general | solution.py:218
  752.7 29.4 %reduce-scatter.42.cloned.1.call-done = bf16[640,1024]{1,0:T(8,128)(2,1)} async-done(((bf16[2560,1024]{1,0:T(8,128)(2,1)}), bf16[640,1024]{1,0:T(8,128)(2,1)}) %reduce-scatter.42.cloned.1.call-update) | async-done | bytes 1310736
  792.4 86.2 %reduce-scatter.44.cloned.1.call-done = bf16[640,1024]{1,0:T(8,128)(2,1)} async-done(((bf16[2560,1024]{1,0:T(8,128)(2,1)}), bf16[640,1024]{1,0:T(8,128)(2,1)}) %reduce-scatter.44.cloned.1.call-update) | async-done | bytes 1310736
  909.6 96.5 %all-gather.11.cloned.1.call-done = bf16[1,1024,2560]{2,1,0:T(8,128)(2,1)} async-done(((bf16[1,1024,640]{2,1,0:T(8,128)(2,1)}), bf16[1,1024,2560]{2,1,0:T(8,128)(2,1)}) %all-gather.11.cloned.1.call-update) | async-done | bytes 5242896 | tf_op jit(solution)/shard_map/all_gather | solution.py:78
  1024.5 261.6 %while.48 = (s32[]{:T(128)}, f32[2048,2,80]{0,2,1:T(8,128)S(1)}, f32[2048,2,80]{0,2,1:T(8,128)}, f32[2,512,2,4,80]{1,0,4,3,2:T(2,128)}, bf16[2,512,2,4,80]{1,4,3...) while((s32[]{:T(128)}, f32[2048,2,80]{0,2,1:T(8,128)S(1)}, ...), condition=%wide.region_18.19_spmd.clone, body=%wide.region_16.18_spmd.clone.sunk | while | flops 6851656192 | bytes 357844320 | solution.py:154
  1058.4 24.3 %fusion.197 = (f32[2,4,512]{2,1,0:T(4,128)S(1)}, f32[2,512,4,2048]{3,1,2,0:T(8,128)}) fusion(f32[2,512,4,2048]{3,1,2,0:T(8,128)} %fusion.195, f32[2,4,512]{2,1,0:T(4,128)S(1)} %dynamic-slice_bitcast_fusion.2, pred[512,2048]{1,0:T(8,128)(4,1)S(1)} %fusion.196, bf16[2048,2,80]{0,2,1:T(8,128)(2,1)S(1)} %copy-done.8, ...), kind=kOutput, calls=%fused_computation.27.clone.1 | convolution fusion | flops 1384116224 | bytes 69500928 | tf_op jit(solution)/shard_map/while/body/eval_jaxpr/while/body/eval_jaxpr/bkgd,jkd->kgbj/dot_general | solution.py:137
  1082.7 27.6 %fusion.198 = bf16[2,4,512,2048]{3,2,1,0:T(8,128)(2,1)} fusion(f32[2,512,4,2048]{3,1,2,0:T(8,128)} %get-tuple-element.510, f32[2,512,4,2048]{3,1,2,0:T(8,128)} %fusion.195, f32[2,4,512]{2,1,0:T(4,128)S(1)} %get-tuple-element.511, f32[2,4,512]{2,1,0:T(4,128)S(1)} %dynamic-slice_bitcast_fusion.2, pred[512,2048]{1,0:T(8,128)(4,1)S(1)} %fusion.196), kind=kLoop, calls=%fused_computation.29.clone.1 | loop fusion | flops 58720256 | bytes 84967424 | tf_op jit(solution)/shard_map/while/body/eval_jaxpr/while/body/eval_jaxpr/convert_element_type | solution.py:141
  1131.0 24.2 %dynamic_update_slice.32 = f32[2,512,2,4,80]{1,0,4,3,2:T(2,128)} dynamic-update-slice(f32[2,512,2,4,80]{1,0,4,3,2:T(2,128)} %get-tuple-element.566, f32[1,512,2,4,80]{1,0,4,3,2:T(1,128)} %copy.103, s32[]{:T(128)S(6)} %copy.121, s32[]{:T(128)} %constant.91.clone.1..sunk.1, s32[]{:T(128)} %constant.91.clone.1..sunk.1, s32[]{:T(128)} %constant.91.clone.1..sunk.1, s32[]{:T(128)} %constant.91.clone.1..sunk.1) | dynamic-update-slice | bytes 2621444 | tf_op jit(solution)/shard_map/while/body/eval_jaxpr/while/body/jit(dynamic_update_index_in_dim)/dynamic_update_slice | solution.py:119
  1188.9 24.3 %fusion.197 = (f32[2,4,512]{2,1,0:T(4,128)S(1)}, f32[2,512,4,2048]{3,1,2,0:T(8,128)}) fusion(f32[2,512,4,2048]{3,1,2,0:T(8,128)} %fusion.195, f32[2,4,512]{2,1,0:T(4,128)S(1)} %dynamic-slice_bitcast_fusion.2, pred[512,2048]{1,0:T(8,128)(4,1)S(1)} %fusion.196, bf16[2048,2,80]{0,2,1:T(8,128)(2,1)S(1)} %copy-done.8, ...), kind=kOutput, calls=%fused_computation.27.clone.1 | convolution fusion | flops 1384116224 | bytes 69500928 | tf_op jit(solution)/shard_map/while/body/eval_jaxpr/while/body/eval_jaxpr/bkgd,jkd->kgbj/dot_general | solution.py:137
  1213.2 27.6 %fusion.198 = bf16[2,4,512,2048]{3,2,1,0:T(8,128)(2,1)} fusion(f32[2,512,4,2048]{3,1,2,0:T(8,128)} %get-tuple-element.510, f32[2,512,4,2048]{3,1,2,0:T(8,128)} %fusion.195, f32[2,4,512]{2,1,0:T(4,128)S(1)} %get-tuple-element.511, f32[2,4,512]{2,1,0:T(4,128)S(1)} %dynamic-slice_bitcast_fusion.2, pred[512,2048]{1,0:T(8,128)(4,1)S(1)} %fusion.196), kind=kLoop, calls=%fused_computation.29.clone.1 | loop fusion | flops 58720256 | bytes 84967424 | tf_op jit(solution)/shard_map/while/body/eval_jaxpr/while/body/eval_jaxpr/convert_element_type | solution.py:141
  1261.6 24.2 %dynamic_update_slice.32 = f32[2,512,2,4,80]{1,0,4,3,2:T(2,128)} dynamic-update-slice(f32[2,512,2,4,80]{1,0,4,3,2:T(2,128)} %get-tuple-element.566, f32[1,512,2,4,80]{1,0,4,3,2:T(1,128)} %copy.103, s32[]{:T(128)S(6)} %copy.121, s32[]{:T(128)} %constant.91.clone.1..sunk.1, s32[]{:T(128)} %constant.91.clone.1..sunk.1, s32[]{:T(128)} %constant.91.clone.1..sunk.1, s32[]{:T(128)} %constant.91.clone.1..sunk.1) | dynamic-update-slice | bytes 2621444 | tf_op jit(solution)/shard_map/while/body/eval_jaxpr/while/body/jit(dynamic_update_index_in_dim)/dynamic_update_slice | solution.py:119
  1388.2 21.9 %copy.67 = bf16[1,1024,2560]{1,0,2:T(2,128)(2,1)} copy(bf16[1,1024,2560]{2,1,0:T(8,128)(2,1)} %fusion.79) | data formatting | bytes 10485760
  1427.0 52.6 %reduce-scatter.36.cloned.1.call-done = bf16[320,1792]{1,0:T(8,128)(2,1)} async-done(((bf16[2560,1792]{1,0:T(8,128)(2,1)}), bf16[320,1792]{1,0:T(8,128)(2,1)}) %reduce-scatter.36.cloned.1.call-update) | async-done | bytes 1146896 | tf_op jit(solution)/shard_map/reduce_scatter | solution.py:295
  1482.4 75.7 %reduce-scatter.34.cloned.1.call-done = bf16[320,1792]{1,0:T(8,128)(2,1)} async-done(((bf16[2560,1792]{1,0:T(8,128)(2,1)}), bf16[320,1792]{1,0:T(8,128)(2,1)}) %reduce-scatter.34.cloned.1.call-update) | async-done | bytes 1146896 | tf_op jit(solution)/shard_map/reduce_scatter | solution.py:292
  1560.9 38.1 %reduce-scatter.50.cloned.1.call-done = bf16[320,160]{1,0:T(8,128)(2,1)} async-done(((bf16[2560,160]{1,0:T(8,128)(2,1)}), bf16[320,160]{1,0:T(8,128)(2,1)}) %reduce-scatter.50.cloned.1.call-update) | async-done | bytes 102416
  1600.8 39.0 %reduce-scatter.48.cloned.1.call-done = bf16[320,160]{1,0:T(8,128)(2,1)} async-done(((bf16[2560,160]{1,0:T(8,128)(2,1)}), bf16[320,160]{1,0:T(8,128)(2,1)}) %reduce-scatter.48.cloned.1.call-update) | async-done | bytes 102416
  1641.6 48.8 %reduce-scatter.32.cloned.1.call-done = bf16[640,320]{0,1:T(8,128)(2,1)} async-done(((bf16[640,2560]{0,1:T(8,128)(2,1)}), bf16[640,320]{0,1:T(8,128)(2,1)}) %reduce-scatter.32.cloned.1.call-update) | async-done | bytes 409616 | tf_op jit(solution)/shard_map/reduce_scatter | solution.py:289
  1692.3 48.6 %reduce-scatter.30.cloned.1.call-done = bf16[320,640]{1,0:T(8,128)(2,1)} async-done(((bf16[2560,640]{1,0:T(8,128)(2,1)}), bf16[320,640]{1,0:T(8,128)(2,1)}) %reduce-scatter.30.cloned.1.call-update) | async-done | bytes 409616 | tf_op jit(solution)/shard_map/reduce_scatter | solution.py:280
  1742.9 94.1 %reduce-scatter.46.cloned.1.call-done = bf16[640,1024]{1,0:T(8,128)(2,1)} async-done(((bf16[2560,1024]{1,0:T(8,128)(2,1)}), bf16[640,1024]{1,0:T(8,128)(2,1)}) %reduce-scatter.46.cloned.1.call-update) | async-done | bytes 1310736
  (300 shorter events, 712.2 us)
Async XLA Ops:
  7.2 262.1 %copy-start = (bf16[640,2560]{1,0:T(8,128)(2,1)S(1)}, bf16[640,2560]{1,0:T(8,128)(2,1)}, u32[]{:S(2)}) copy-start(bf16[640,2560]{1,0:T(8,128)(2,1)} %param.25) | copy-start | bytes 9830404
  7.2 115.1 %all-gather.5.cloned.1.call-start = ((), (), s32[]{:S(2)}) async-start(), calls=%async_computation.13 | async-start | bytes 6553600 | tf_op jit(solution)/shard_map/all_gather | solution.py:58
  25.9 372.7 %reduce-scatter.40.cloned.1.call-start = ((), (), s32[]{:S(2)}) async-start(), calls=%async_computation.24 | async-start | bytes 6553600
  33.1 119.4 %copy-start.12 = (f32[1024,40]{0,1:T(8,128)}, f32[1024,40]{0,1:T(8,128)S(1)}, u32[]{:S(2)}) copy-start(f32[1024,40]{0,1:T(8,128)S(1)} %get-tuple-element.359) | copy-start | bytes 491524
  306.2 217.4 %all-gather.7.cloned.1.call-start = ((), (), s32[]{:S(2)}) async-start(), calls=%async_computation.14 | async-start | bytes 6553600 | tf_op jit(solution)/shard_map/all_gather | solution.py:58
  306.3 598.7 %copy-start.33 = (f32[1,1024]{1,0:T(1,128)}, f32[1,1024]{1,0:T(1,128)S(1)}, u32[]{:S(2)}) copy-start(f32[1,1024]{1,0:T(1,128)S(1)} %dynamic-slice_convert_fusion) | copy-start | bytes 12292
  422.7 482.3 %copy-start.35 = (f32[1,1,1024]{2,1,0:T(1,128)}, f32[1,1,1024]{2,1,0:T(1,128)S(1)}, u32[]{:S(2)}) copy-start(f32[1,1,1024]{2,1,0:T(1,128)S(1)} %fusion.127) | copy-start | bytes 12292
  427.1 195.1 %all-gather.9.cloned.1.call-start = ((), (), s32[]{:S(2)}) async-start(), calls=%async_computation.15 | async-start | bytes 6553600 | tf_op jit(solution)/shard_map/all_gather | solution.py:78
  427.7 354.4 %reduce-scatter.42.cloned.1.call-start = ((), (), s32[]{:S(2)}) async-start(), calls=%async_computation.25 | async-start | bytes 6553600
  689.8 188.8 %reduce-scatter.44.cloned.1.call-start = ((), (), s32[]{:S(2)}) async-start(), calls=%async_computation.26 | async-start | bytes 6553600
  752.7 253.5 %all-gather.11.cloned.1.call-start = ((), (), s32[]{:S(2)}) async-start(), calls=%async_computation.16 | async-start | bytes 6553600 | tf_op jit(solution)/shard_map/all_gather | solution.py:78
  909.6 425.7 %reduce-scatter.28.cloned.1.call-start = ((), (), s32[]{:S(2)}) async-start(), calls=%async_computation.18 | async-start | bytes 983040 | tf_op jit(solution)/shard_map/reduce_scatter | solution.py:249
  1058.4 24.3 %copy-start.22 = (f32[2048,2,80]{0,2,1:T(8,128)}, f32[2048,2,80]{0,2,1:T(8,128)S(1)}, u32[]{:S(2)}) copy-start(f32[2048,2,80]{0,2,1:T(8,128)S(1)} %fusion.200) | copy-start | bytes 3932164 | tf_op jit(solution)/shard_map/while/body/eval_jaxpr/while
  1188.9 24.3 %copy-start.22 = (f32[2048,2,80]{0,2,1:T(8,128)}, f32[2048,2,80]{0,2,1:T(8,128)S(1)}, u32[]{:S(2)}) copy-start(f32[2048,2,80]{0,2,1:T(8,128)S(1)} %fusion.200) | copy-start | bytes 3932164 | tf_op jit(solution)/shard_map/while/body/eval_jaxpr/while
  1288.4 53.1 %reduce-scatter.26.cloned.1.call-start = ((), (), s32[]{:S(2)}) async-start(), calls=%async_computation.17 | async-start | bytes 983040 | tf_op jit(solution)/shard_map/reduce_scatter | solution.py:246
  1289.4 134.8 %reduce-scatter.38.cloned.1.call-start = ((), (), s32[]{:S(2)}) async-start(), calls=%async_computation.23 | async-start | bytes 10321920 | tf_op jit(solution)/shard_map/reduce_scatter | solution.py:298
  1304.3 175.2 %reduce-scatter.36.cloned.1.call-start = ((), (), s32[]{:S(2)}) async-start(), calls=%async_computation.22 | async-start | bytes 10321920 | tf_op jit(solution)/shard_map/reduce_scatter | solution.py:295
  1319.3 238.8 %reduce-scatter.34.cloned.1.call-start = ((), (), s32[]{:S(2)}) async-start(), calls=%async_computation.21 | async-start | bytes 10321920 | tf_op jit(solution)/shard_map/reduce_scatter | solution.py:292
  1335.1 263.9 %reduce-scatter.50.cloned.1.call-start = ((), (), s32[]{:S(2)}) async-start(), calls=%async_computation.29 | async-start | bytes 1474560
  1341.4 298.4 %reduce-scatter.48.cloned.1.call-start = ((), (), s32[]{:S(2)}) async-start(), calls=%async_computation.28 | async-start | bytes 1474560
  1347.7 342.7 %reduce-scatter.32.cloned.1.call-start = ((), (), s32[]{:S(2)}) async-start(), calls=%async_computation.20 | async-start | bytes 3686400 | tf_op jit(solution)/shard_map/reduce_scatter | solution.py:289
  1356.3 384.7 %reduce-scatter.30.cloned.1.call-start = ((), (), s32[]{:S(2)}) async-start(), calls=%async_computation.19 | async-start | bytes 3686400 | tf_op jit(solution)/shard_map/reduce_scatter | solution.py:280
  1369.4 467.7 %reduce-scatter.46.cloned.1.call-start = ((), (), s32[]{:S(2)}) async-start(), calls=%async_computation.27 | async-start | bytes 6553600
  1858.3 23.2 %copy-start.1 = (bf16[640,2560]{1,0:T(8,128)(2,1)S(1)}, bf16[640,2560]{1,0:T(8,128)(2,1)}, u32[]{:S(2)}) copy-start(bf16[640,2560]{1,0:T(8,128)(2,1)} %param.25) | copy-start | bytes 9830404
  (53 other events, 455.2 us)
Sparse Core Ops, SparseCore 0:
  26.0 96.2 all-gather.4
  306.4 92.1 reduce-scatter.39
  427.2 96.4 all-gather.6
  525.7 96.4 all-gather.8
  689.9 92.1 reduce-scatter.41
  784.3 94.2 reduce-scatter.43
  909.7 96.4 all-gather.10
  1288.5 14.3 reduce-scatter.27
  1305.8 15.9 reduce-scatter.25
  1325.3 75.0 reduce-scatter.37
  1404.5 75.0 reduce-scatter.35
  1483.0 75.0 reduce-scatter.33
  1561.7 37.2 reduce-scatter.49
  1602.5 37.2 reduce-scatter.47
  1643.5 46.8 reduce-scatter.31
  1694.0 46.8 reduce-scatter.29
  1743.2 93.7 reduce-scatter.45
where the time goes:
time: 1910 us; the launch traced here: 1890 us
  waiting for transfers between devices  954 us (50%)
  matrix products  417 us (22%)
  local copies, waits for them, and re-layouts  265 us (14%)
  other arithmetic  144 us (8%)
  blocking collectives  81.6 us (4%)
  between operations  21.2 us (1%)
    unnamed x23, waiting for transfers between devices  380 us
    all_gather x2, waiting for transfers between devices, normalize(): gathered = lax.all_gather(scaled, 'tensor', axis=2, tiled=True)  185 us
    unnamed x120, local copies, waits for them, and re-layouts  183 us
    all_gather x2, waiting for transfers between devices, gather_cot(): lax.all_gather(gradient.astype(jnp.bfloat16), 'tensor', axis=2, tiled=True)  163 us
    reduce_scatter x1, waiting for transfers between devices, local(): lax.psum_scatter(gate_grad.astype(jnp.bfloat16), ('dp', 'context'), scatt...  75.7 us
    dot_general x7, matrix products, project(): jnp.einsum('scd,dx->scx', left_operand, right_operand, preferred_element_...  63.5 us
    dot_general x4, matrix products, scores_for(): jnp.einsum('bkgd,jkd->kgbj', query_block, key_seq, preferred_element_type...  59.1 us
    dynamic_update_slice x4, local copies, waits for them, and re-layouts, attend_forward(): mixed, logsum = lax.map(one_block, (query_blocks, positions))  55.8 us
  transfers between devices with their start and end apart: 17, of which 14 were waited for; matrix products, arithmetic and copies ran while one was open for 14% of the time, Pallas kernels for 0%

commit v1 on v0

v1 whole, which is shorter than its diff:
```python
import functools
import math

import jax
import jax.numpy as jnp
from jax import lax
from jax.experimental import pallas as pl
from jax.experimental.pallas import tpu as pltpu
from jax.sharding import PartitionSpec as P

HD = 80
PIC = 256
F32 = jnp.float32
BF = jnp.bfloat16
SCALE = HD**-0.5
SCALE2 = SCALE * math.log2(math.e)
LOWEST = -1e30
GROUP_ROWS = 256
HOP_ROWS = 64
VMEM_LIMIT = 60 << 20
KEY_ROWS_FWD = 1024
KEY_ROWS_BWD = 512

epsilon = 1e-05
rope_base = 1000000.0


def dot(a, b):
    return jnp.dot(a, b, preferred_element_type=F32)


def dot_nt(a, b):
    return lax.dot_general(a, b, (((1,), (1,)), ((), ())), preferred_element_type=F32)


def ein(spec, a, b):
    return jnp.einsum(spec, a, b, preferred_element_type=F32)


def forward_kernel(
    group, key_rows, lim_ref, kend_ref, q_ref, k_ref, vt_ref, o_ref, lse_ref, acc, mx, sm
):
    rows = q_ref.shape[-1]
    acc[...] = jnp.zeros_like(acc)
    sm[...] = jnp.zeros_like(sm)
    mx[...] = jnp.full_like(mx, LOWEST)
    kend = kend_ref[...]

    def step(masked, i, _):
        at = pl.multiple_of(i * key_rows, key_rows)
        k_blk = k_ref[0, pl.ds(at, key_rows), :]
        v_blk = vt_ref[0, :, pl.ds(at, key_rows)]
        if masked:
            keep = (lax.broadcasted_iota(jnp.int32, (key_rows, rows), 0) + at) < kend
        for h in range(group):
            s = dot(k_blk, q_ref[h])
            if masked:
                s = jnp.where(keep, s, LOWEST)
            old = mx[h]
            new = jnp.maximum(old, jnp.max(s, 0, keepdims=True))
            p = jnp.exp2(s * SCALE2 - new * SCALE2)
            alpha = jnp.exp2((old - new) * SCALE2)
            mx[h] = new
            sm[h] = sm[h] * alpha + jnp.sum(p, 0, keepdims=True)
            acc[h] = acc[h] * alpha + dot(v_blk, p.astype(BF))
        return 0

    lax.fori_loop(0, lim_ref[pl.program_id(1), 0], functools.partial(step, False), 0)
    lax.fori_loop(lim_ref[pl.program_id(1), 0], lim_ref[pl.program_id(1), 1], functools.partial(step, True), 0)
    for h in range(group):
        o_ref[h] = (acc[h] / sm[h]).astype(BF)
        lse_ref[h] = mx[h] * SCALE2 + jnp.log2(sm[h])


def key_limits(kend, key_rows):
    by_group = kend.reshape(-1, GROUP_ROWS)
    return jnp.stack(
        [jnp.min(by_group, 1) // key_rows, -(-jnp.max(by_group, 1) // key_rows)], 1
    ).astype(jnp.int32)


def attend_forward(q, k, vt, kend):
    heads, _, total = q.shape
    rows = GROUP_ROWS
    kvs, keys, _ = k.shape
    group = heads // kvs
    key_rows = min(KEY_ROWS_FWD, keys)
    return pl.pallas_call(
        functools.partial(forward_kernel, group, key_rows),
        grid=(kvs, total // rows),
        in_specs=[
            pl.BlockSpec(memory_space=pltpu.SMEM),
            pl.BlockSpec((1, rows), lambda g, i: (0, i)),
            pl.BlockSpec((group, HD, rows), lambda g, i: (g, 0, i)),
            pl.BlockSpec((1, keys, HD), lambda g, i: (g, 0, 0)),
            pl.BlockSpec((1, HD, keys), lambda g, i: (g, 0, 0)),
        ],
        out_specs=[
            pl.BlockSpec((group, HD, rows), lambda g, i: (g, 0, i)),
            pl.BlockSpec((group, 1, rows), lambda g, i: (g, 0, i)),
        ],
        out_shape=[
            jax.ShapeDtypeStruct((heads, HD, total), BF),
            jax.ShapeDtypeStruct((heads, 1, total), F32),
        ],
        scratch_shapes=[
            pltpu.VMEM((group, HD, rows), F32),
            pltpu.VMEM((group, 1, rows), F32),
            pltpu.VMEM((group, 1, rows), F32),
        ],
        compiler_params=pltpu.CompilerParams(vmem_limit_bytes=32 << 20),
        cost_estimate=pl.CostEstimate(
            flops=10 * heads * total * keys * HD,
            bytes_accessed=8 << 20,
            transcendentals=heads * total * keys,
        ),
        name="attend_fwd",
    )(key_limits(kend, key_rows), kend, q, k, vt)


def backward_kernel(
    group, key_rows, lim_ref, kend_ref, q_ref, do_ref, o_ref, lse_ref, k_ref, kt_ref, v_ref,
    dq_ref, dk_ref, dv_ref, ds_all, p_all, q_all, do_all,
):
    @pl.when(pl.program_id(1) == 0)
    def _():
        dk_ref[...] = jnp.zeros_like(dk_ref)
        dv_ref[...] = jnp.zeros_like(dv_ref)

    rows = q_ref.shape[-1]
    dq_ref[...] = jnp.zeros_like(dq_ref)
    kend = kend_ref[...]
    delta = []
    for h in range(group):
        q_all[:, h * rows : (h + 1) * rows] = q_ref[h]
        do_all[:, h * rows : (h + 1) * rows] = do_ref[h]
        delta.append(jnp.sum(do_ref[h].astype(F32) * o_ref[h].astype(F32), 0, keepdims=True))

    def step(masked, i, _):
        at = pl.multiple_of(i * key_rows, key_rows)
        k_blk = k_ref[0, pl.ds(at, key_rows), :]
        v_blk = v_ref[0, pl.ds(at, key_rows), :]
        kt_blk = kt_ref[0, :, pl.ds(at, key_rows)]
        if masked:
            keep = (lax.broadcasted_iota(jnp.int32, (key_rows, rows), 0) + at) < kend
        for h in range(group):
            s = dot(k_blk, q_ref[h])
            p = jnp.exp2(s * SCALE2 - lse_ref[h])
            if masked:
                p = jnp.where(keep, p, 0.0)
            dp = dot(v_blk, do_ref[h])
            ds = (p * (dp - delta[h])).astype(BF)
            p_all[:, h * rows : (h + 1) * rows] = p.astype(BF)
            ds_all[:, h * rows : (h + 1) * rows] = ds
            dq_ref[h] += dot(kt_blk, ds)
        dk_ref[0, pl.ds(at, key_rows), :] += dot_nt(ds_all[...], q_all[...])
        dv_ref[0, pl.ds(at, key_rows), :] += dot_nt(p_all[...], do_all[...])
        return 0

    lax.fori_loop(0, lim_ref[pl.program_id(1), 0], functools.partial(step, False), 0)
    lax.fori_loop(lim_ref[pl.program_id(1), 0], lim_ref[pl.program_id(1), 1], functools.partial(step, True), 0)


def attend_backward(q, do, o, lse, k, kt, v, kend):
    heads, _, total = q.shape
    rows = GROUP_ROWS
    kvs, keys, _ = k.shape
    group = heads // kvs
    key_rows = min(KEY_ROWS_BWD, keys)
    by_head = pl.BlockSpec((group, HD, rows), lambda g, i: (g, 0, i))
    by_key = pl.BlockSpec((1, keys, HD), lambda g, i: (g, 0, 0))
    return pl.pallas_call(
        functools.partial(backward_kernel, group, key_rows),
        grid=(kvs, total // rows),
        in_specs=[
            pl.BlockSpec(memory_space=pltpu.SMEM),
            pl.BlockSpec((1, rows), lambda g, i: (0, i)),
            by_head,
            by_head,
            by_head,
            pl.BlockSpec((group, 1, rows), lambda g, i: (g, 0, i)),
            by_key,
            pl.BlockSpec((1, HD, keys), lambda g, i: (g, 0, 0)),
            by_key,
        ],
        out_specs=[by_head, by_key, by_key],
        out_shape=[
            jax.ShapeDtypeStruct((heads, HD, total), F32),
            jax.ShapeDtypeStruct(k.shape, F32),
            jax.ShapeDtypeStruct(k.shape, F32),
        ],
        scratch_shapes=[
            pltpu.VMEM((key_rows, group * rows), BF),
            pltpu.VMEM((key_rows, group * rows), BF),
            pltpu.VMEM((HD, group * rows), BF),
            pltpu.VMEM((HD, group * rows), BF),
        ],
        compiler_params=pltpu.CompilerParams(vmem_limit_bytes=40 << 20),
        cost_estimate=pl.CostEstimate(
            flops=16 * heads * total * keys * HD,
            bytes_accessed=16 << 20,
            transcendentals=heads * total * keys,
        ),
        name="attend_bwd",
    )(key_limits(kend, key_rows), kend, q, do, o, lse, k, kt, v)


MESH_ID = pl.DeviceIdType.MESH
RING = 8
SENT = 4


def add_low(a, b):
    return (a.astype(F32) + b.astype(F32)).astype(BF)


class Sums:
    def __init__(self, size, count, part, low, high, sent, sems):
        self.size, self.count, self.part = size, count, part
        self.low, self.high, self.sent = low, high, sent
        self.low_send, self.low_recv, self.high_send, self.high_recv = sems
        self.here = lax.axis_index("tensor")

    def barrier(self):
        here, size = self.here, self.size
        barrier = pltpu.get_barrier_semaphore()

        @pl.when(here > 0)
        def _():
            pl.semaphore_signal(
                barrier, inc=1, device_id={"tensor": here - 1}, device_id_type=MESH_ID
            )

        @pl.when(here < size - 1)
        def _():
            pl.semaphore_signal(
                barrier, inc=1, device_id={"tensor": here + 1}, device_id_type=MESH_ID
            )

        @pl.when((here > 0) & (here < size - 1))
        def _():
            pl.semaphore_wait(barrier, 2)

        @pl.when((here == 0) | (here == size - 1))
        def _():
            pl.semaphore_wait(barrier, 1)

    def up(self, c):
        slot = lax.rem(c, RING)
        return pltpu.make_async_remote_copy(
            src_ref=self.low.at[slot],
            dst_ref=self.low.at[slot],
            send_sem=self.low_send.at[slot],
            recv_sem=self.low_recv.at[slot],
            device_id={"tensor": self.here + 1},
            device_id_type=MESH_ID,
        )

    def down(self, c):
        slot, mine = lax.rem(c, RING), lax.rem(c, SENT)
        return pltpu.make_async_remote_copy(
            src_ref=self.sent.at[mine],
            dst_ref=self.high.at[slot],
            send_sem=self.high_send.at[mine],
            recv_sem=self.high_recv.at[slot],
            device_id={"tensor": self.here - 1},
            device_id_type=MESH_ID,
        )

    def tick(self, k):
        here, size, count = self.here, self.size, self.count
        bottom, top = here == 0, here == size - 1
        c = k - here

        @pl.when((c >= 0) & (c < count))
        def _():
            slot = lax.rem(c, RING)

            @pl.when(bottom)
            def _():
                self.low[slot] = self.part(c)

            @pl.when(jnp.logical_not(bottom))
            def _():
                self.up(c).wait_recv()
                self.low[slot] = add_low(self.low[slot], self.part(c))

            @pl.when(jnp.logical_not(top))
            def _():
                self.up(c).start()

        d = k - (size - 1 - here)

        @pl.when((d >= 0) & (d < count))
        def _():
            slot, mine = lax.rem(d, RING), lax.rem(d, SENT)

            @pl.when(top)
            def _():
                self.sent[mine] = self.part(d)

            @pl.when(jnp.logical_not(top))
            def _():
                self.down(d).wait_recv()

                @pl.when(jnp.logical_not(bottom))
                def _():
                    self.sent[mine] = add_low(self.high[slot], self.part(d))

            @pl.when(jnp.logical_not(bottom))
            def _():
                self.down(d).start()

        @pl.when((c >= 2) & (c < count + 2) & jnp.logical_not(top))
        def _():
            self.up(c - 2).wait_send()

        @pl.when((d >= 2) & (d < count + 2) & jnp.logical_not(bottom))
        def _():
            self.down(d - 2).wait_send()

    def total(self, c, then):
        slot = lax.rem(c, RING)
        top = self.here == self.size - 1

        @pl.when(top)
        def _():
            then(self.low[slot].astype(F32))

        @pl.when(jnp.logical_not(top))
        def _():
            then(self.low[slot].astype(F32) + self.high[slot].astype(F32))


def sum_scratch(hop, features):
    return [
        pltpu.VMEM((RING, hop, features), BF),
        pltpu.VMEM((RING, hop, features), BF),
        pltpu.VMEM((SENT, hop, features), BF),
        pltpu.SemaphoreType.DMA((RING,)),
        pltpu.SemaphoreType.DMA((RING,)),
        pltpu.SemaphoreType.DMA((SENT,)),
        pltpu.SemaphoreType.DMA((RING,)),
    ]


def tile_of(n, most):
    for tile in range(most, 0, -128):
        if n % tile == 0:
            return tile
    return n


def ffn_kernel(
    size, hop, chunk,
    mixed, keep, gain, w_out, w_gate, w_up, w_down, x, cot,
    normed_o, act_o, gg_o, gu_o, ffn_o, back_o, middle_o, square_o,
    low, high, sent, low_send, low_recv, high_send, high_recv,
    wo, wg, wu, wd, parts, normed, xs, cots, mids, act, gg, gu, ffn, back,
    w_sem, x_sem, cot_sem, normed_sem, mid_sem, act_sem, ffn_sem,
):
    rows, features = x.shape
    hidden = w_gate.shape[1]
    count, per, groups = rows // hop, chunk // hop, rows // chunk
    tile_f, tile_d = tile_of(hidden, 256), tile_of(features, 256)
    tiles_f, tiles_d = hidden // tile_f, features // tile_d
    half_f, half_d = -(-tiles_f // 2), -(-tiles_d // 2)
    lag = size - 1 + per - 1
    ticks = max(per * groups + lag, count + size)

    def part(c):
        return parts[lax.rem(lax.div(c, per), 2), pl.ds(pl.multiple_of(lax.rem(c, per) * hop, hop), hop), :]

    sums = Sums(size, count, part, low, high, sent, (low_send, low_recv, high_send, high_recv))
    loads = [
        pltpu.make_async_copy(a, b, w_sem.at[i])
        for i, (a, b) in enumerate(((w_out, wo), (w_gate, wg), (w_up, wu), (w_down, wd)))
    ]
    for load in loads:
        load.start()

    def load_x(c):
        slot = lax.rem(c, 2)
        return pltpu.make_async_copy(x.at[pl.ds(c * hop, hop)], xs.at[slot], x_sem.at[slot])

    def load_cot(g):
        return pltpu.make_async_copy(cot.at[pl.ds(g * chunk, chunk)], cots, cot_sem)

    def save_normed(c):
        at, q = lax.rem(lax.div(c, per), 2), lax.rem(c, per)
        return pltpu.make_async_copy(
            normed.at[at, pl.ds(q * hop, hop)], normed_o.at[pl.ds(c * hop, hop)], normed_sem.at[at, q]
        )

    def save_mid(c):
        slot = lax.rem(c, 2)
        return pltpu.make_async_copy(mids.at[slot], middle_o.at[pl.ds(c * hop, hop)], mid_sem.at[slot])

    def save_act(g):
        return [
            pltpu.make_async_copy(a, b.at[pl.ds(g * chunk, chunk)], act_sem.at[i])
            for i, (a, b) in enumerate(((act, act_o), (gg, gg_o), (gu, gu_o)))
        ]

    def save_ffn(g):
        return [
            pltpu.make_async_copy(a, b.at[pl.ds(g * chunk, chunk)], ffn_sem.at[i])
            for i, (a, b) in enumerate(((ffn, ffn_o), (back, back_o)))
        ]

    def project(g):
        at = lax.rem(g, 2)
        lhs = mixed[:, pl.ds(pl.multiple_of(g * chunk, chunk), chunk)]

        def one(j, _):
            cols = pl.ds(pl.multiple_of(j * tile_d, tile_d), tile_d)
            parts[at, :, cols] = lax.dot_general(
                lhs, wo[:, cols], (((0,), (0,)), ((), ())), preferred_element_type=F32
            ).astype(BF)
            return 0

        lax.fori_loop(0, tiles_d, one, 0)

    load_x(0).start()
    load_cot(0).start()
    square_o[...] = jnp.zeros_like(square_o)
    loads[0].wait()
    project(0)
    sums.barrier()

    def finish(c):
        slot = lax.rem(c, 2)
        load_x(c).wait()

        @pl.when(c + 1 < count)
        def _():
            load_x(c + 1).start()

        @pl.when(c >= 2)
        def _():
            save_mid(c - 2).wait()

        @pl.when(c >= 2 * per)
        def _():
            save_normed(c - 2 * per).wait()

        kept = keep[pl.ds(pl.multiple_of(c * hop, hop), hop), :]

        def then(total):
            out = kept * total
            square_o[...] += jnp.sum(out * out, 0, keepdims=True)
            mids[slot] = xs[slot].astype(F32) + out

        sums.total(c, then)
        mid = mids[slot]
        inv = lax.rsqrt(jnp.sum(mid * mid, 1, keepdims=True) / features + epsilon)
        at = lax.rem(lax.div(c, per), 2)
        normed[at, pl.ds(pl.multiple_of(lax.rem(c, per) * hop, hop), hop), :] = (
            mid * inv * gain[...]
        ).astype(BF)
        save_mid(c).start()
        save_normed(c).start()

    def inner(g, lo, hi):
        at = lax.rem(g, 2)
        kept = keep[pl.ds(pl.multiple_of(g * chunk, chunk), chunk), :]

        def one(j, _):
            cols = pl.ds(pl.multiple_of(j * tile_f, tile_f), tile_f)
            gate = dot(normed[at], wg[:, cols])
            up = dot(normed[at], wu[:, cols])
            grad = dot_nt(cots[...], wd[cols, :]) * kept
            sig = jax.nn.sigmoid(gate)
            silu = gate * sig
            act[:, cols] = (silu * up * kept).astype(BF)
            gg[:, cols] = (grad * up * (sig + silu * (1.0 - sig))).astype(BF)
            gu[:, cols] = (grad * silu).astype(BF)
            return 0

        lax.fori_loop(lo, hi, one, 0)

    def outer(g, lo, hi):
        def one(j, _):
            cols = pl.ds(pl.multiple_of(j * tile_d, tile_d), tile_d)
            ffn[:, cols] = dot(act[...], wd[:, cols]).astype(BF)
            back[:, cols] = (dot_nt(gg[...], wg[cols, :]) + dot_nt(gu[...], wu[cols, :])).astype(BF)
            return 0

        lax.fori_loop(lo, hi, one, 0)

    def tick(k, _):
        sums.tick(k)
        c = k - (size - 1)

        @pl.when((c >= 0) & (c < count))
        def _():
            finish(c)

        ahead = k + 2

        @pl.when((lax.rem(ahead, per) == 0) & (ahead < count))
        def _():
            project(lax.div(ahead, per))

        s = k - lag
        g, stage = lax.div(s, per), lax.rem(s, per)
        going = (s >= 0) & (g < groups)

        @pl.when(going & (stage == 0))
        def _():
            @pl.when(g == 0)
            def _():
                for load in loads[1:]:
                    load.wait()

            load_cot(g).wait()

            @pl.when(g > 0)
            def _():
                for copy in save_act(g - 1):
                    copy.wait()

            inner(g, 0, half_f)

        @pl.when(going & (stage == 1))
        def _():
            inner(g, half_f, tiles_f)
            for copy in save_act(g):
                copy.start()

            @pl.when(g + 1 < groups)
            def _():
                load_cot(g + 1).start()

        @pl.when(going & (stage == 2))
        def _():
            @pl.when(g > 0)
            def _():
                for copy in save_ffn(g - 1):
                    copy.wait()

            outer(g, 0, half_d)

        @pl.when(going & (stage == 3))
        def _():
            outer(g, half_d, tiles_d)
            for copy in save_ffn(g):
                copy.start()

        return 0

    lax.fori_loop(0, ticks, tick, 0)
    for copy in save_act(groups - 1) + save_ffn(groups - 1):
        copy.wait()
    for c in range(count - 2, count):
        save_mid(c).wait()
    for c in range(count - 2 * per, count):
        save_normed(c).wait()


def feed_forward(size, mixed, keep, gain, w_out, w_gate, w_up, w_down, x, cot, chunk, hop):
    rows, features = x.shape
    hidden = w_gate.shape[1]
    per = chunk // hop
    assert per == 4
    anywhere, vmem = pl.BlockSpec(memory_space=pl.ANY), pl.BlockSpec(memory_space=pltpu.VMEM)
    shape = jax.ShapeDtypeStruct
    return pl.pallas_call(
        functools.partial(ffn_kernel, size, hop, chunk),
        in_specs=[vmem] * 3 + [anywhere] * 6,
        out_specs=[anywhere] * 7 + [vmem],
        out_shape=[
            shape((rows, features), BF),
            shape((rows, hidden), BF),
            shape((rows, hidden), BF),
            shape((rows, hidden), BF),
            shape((rows, features), BF),
            shape((rows, features), BF),
            shape((rows, features), F32),
            shape((1, features), F32),
        ],
        scratch_shapes=sum_scratch(hop, features)
        + [
            pltpu.VMEM(w_out.shape, BF),
            pltpu.VMEM(w_gate.shape, BF),
            pltpu.VMEM(w_up.shape, BF),
            pltpu.VMEM(w_down.shape, BF),
            pltpu.VMEM((2, chunk, features), BF),
            pltpu.VMEM((2, chunk, features), BF),
            pltpu.VMEM((2, hop, features), BF),
            pltpu.VMEM((chunk, features), BF),
            pltpu.VMEM((2, hop, features), F32),
            pltpu.VMEM((chunk, hidden), BF),
            pltpu.VMEM((chunk, hidden), BF),
            pltpu.VMEM((chunk, hidden), BF),
            pltpu.VMEM((chunk, features), BF),
            pltpu.VMEM((chunk, features), BF),
            pltpu.SemaphoreType.DMA((4,)),
            pltpu.SemaphoreType.DMA((2,)),
            pltpu.SemaphoreType.DMA,
            pltpu.SemaphoreType.DMA((2, per)),
            pltpu.SemaphoreType.DMA((2,)),
            pltpu.SemaphoreType.DMA((3,)),
            pltpu.SemaphoreType.DMA((2,)),
        ],
        compiler_params=pltpu.CompilerParams(
            collective_id=1, has_side_effects=True, vmem_limit_bytes=VMEM_LIMIT
        ),
        cost_estimate=pl.CostEstimate(
            flops=2 * rows * features * (6 * hidden + w_out.shape[0]),
            bytes_accessed=80 << 20,
            transcendentals=rows * hidden,
        ),
        name="feed_forward",
    )(mixed, keep, gain, w_out, w_gate, w_up, w_down, x, cot)


def back_kernel(
    size, hop, chunk,
    parts, keep, gain, w_out, middle, cot,
    grad_o, grad_low_o, mixed_o, gain_o,
    low, high, sent, low_send, low_recv, high_send, high_recv,
    wo, mids, cots, grads, grads_low,
    w_sem, mid_sem, cot_sem, grad_sem, grad_low_sem,
):
    rows, features = middle.shape
    count, per, groups = rows // hop, chunk // hop, rows // chunk
    ticks = max(count + size, per * (groups - 1) + size - 1 + per)

    def part(c):
        return parts[pl.ds(pl.multiple_of(c * hop, hop), hop), :]

    sums = Sums(size, count, part, low, high, sent, (low_send, low_recv, high_send, high_recv))
    load_w = pltpu.make_async_copy(w_out, wo, w_sem)
    load_w.start()

    def load_row(c):
        slot = lax.rem(c, 2)
        return [
            pltpu.make_async_copy(middle.at[pl.ds(c * hop, hop)], mids.at[slot], mid_sem.at[slot]),
            pltpu.make_async_copy(cot.at[pl.ds(c * hop, hop)], cots.at[slot], cot_sem.at[slot]),
        ]

    def save_grad(c):
        slot = lax.rem(c, 2)
        return pltpu.make_async_copy(grads.at[slot], grad_o.at[pl.ds(c * hop, hop)], grad_sem.at[slot])

    def save_low(c):
        q = lax.rem(c, per)
        return pltpu.make_async_copy(
            grads_low.at[pl.ds(q * hop, hop)], grad_low_o.at[pl.ds(c * hop, hop)], grad_low_sem.at[q]
        )

    for copy in load_row(0):
        copy.start()
    gain_o[...] = jnp.zeros_like(gain_o)
    sums.barrier()

    def finish(c):
        slot = lax.rem(c, 2)
        for copy in load_row(c):
            copy.wait()

        @pl.when(c + 1 < count)
        def _():
            for copy in load_row(c + 1):
                copy.start()

        @pl.when(c >= 2)
        def _():
            save_grad(c - 2).wait()

        @pl.when(c >= per)
        def _():
            save_low(c - per).wait()

        kept = keep[pl.ds(pl.multiple_of(c * hop, hop), hop), :]
        mid = mids[slot]
        inv = lax.rsqrt(jnp.sum(mid * mid, 1, keepdims=True) / features + epsilon)
        hat = mid * inv

        def then(total):
            gain_o[...] += jnp.sum(total * hat, 0, keepdims=True)
            weighted = total * gain[...]
            mean = jnp.sum(weighted * hat, 1, keepdims=True) / features
            grads[slot] = cots[slot].astype(F32) + inv * (weighted - hat * mean)

        sums.total(c, then)
        grads_low[pl.ds(pl.multiple_of(lax.rem(c, per) * hop, hop), hop), :] = (
            kept * grads[slot]
        ).astype(BF)
        save_grad(c).start()
        save_low(c).start()

    def tick(k, _):
        sums.tick(k)
        c = k - (size - 1)

        @pl.when((c >= 0) & (c < count))
        def _():
            finish(c)

            @pl.when(lax.rem(c, per) == per - 1)
            def _():
                g = lax.div(c, per)

                @pl.when(g == 0)
                def _():
                    load_w.wait()

                mixed_o[:, pl.ds(pl.multiple_of(g * chunk, chunk), chunk)] = dot_nt(
                    wo[...], grads_low[...]
                ).astype(BF)

        return 0

    lax.fori_loop(0, ticks, tick, 0)
    for c in range(count - 2, count):
        save_grad(c).wait()
    for c in range(count - per, count):
        save_low(c).wait()


def norm_back(size, parts, keep, gain, w_out, middle, cot, chunk, hop):
    rows, features = middle.shape
    per = chunk // hop
    anywhere, vmem = pl.BlockSpec(memory_space=pl.ANY), pl.BlockSpec(memory_space=pltpu.VMEM)
    shape = jax.ShapeDtypeStruct
    return pl.pallas_call(
        functools.partial(back_kernel, size, hop, chunk),
        in_specs=[vmem] * 3 + [anywhere] * 3,
        out_specs=[anywhere] * 2 + [vmem] * 2,
        out_shape=[
            shape((rows, features), F32),
            shape((rows, features), BF),
            shape((w_out.shape[0], rows), BF),
            shape((1, features), F32),
        ],
        scratch_shapes=sum_scratch(hop, features)
        + [
            pltpu.VMEM(w_out.shape, BF),
            pltpu.VMEM((2, hop, features), F32),
            pltpu.VMEM((2, hop, features), BF),
            pltpu.VMEM((2, hop, features), F32),
            pltpu.VMEM((chunk, features), BF),
            pltpu.SemaphoreType.DMA,
            pltpu.SemaphoreType.DMA((2,)),
            pltpu.SemaphoreType.DMA((2,)),
            pltpu.SemaphoreType.DMA((2,)),
            pltpu.SemaphoreType.DMA((per,)),
        ],
        compiler_params=pltpu.CompilerParams(
            collective_id=2, has_side_effects=True, vmem_limit_bytes=VMEM_LIMIT
        ),
        cost_estimate=pl.CostEstimate(
            flops=2 * rows * features * w_out.shape[0],
            bytes_accessed=40 << 20,
            transcendentals=rows,
        ),
        name="norm_back",
    )(parts, keep, gain, w_out, middle, cot)


class Line:
    def __init__(self, size):
        self.size = size
        self.here = lax.axis_index("tensor")
        self.up = [(i, i + 1) for i in range(size - 1)]
        self.down = [(i + 1, i) for i in range(size - 1)]

    def gather(self, own):
        size, here, width = self.size, self.here, own.shape[1]
        full = jnp.zeros((own.shape[0], size * width), own.dtype)
        full = lax.dynamic_update_slice(full, own, (0, here * width))
        rising, falling = [], []
        a = b = own
        for _ in range(size - 1):
            a = lax.ppermute(a, "tensor", self.up)
            b = lax.ppermute(b, "tensor", self.down)
            rising.append(a)
            falling.append(b)
        for s in range(size - 1):
            slot = lax.rem(here - 1 - s + size, size)
            block = jnp.where(here > s, rising[s], falling[size - 2 - s])
            full = lax.dynamic_update_slice(full, block, (0, slot * width))
        return full

    def gather_small(self, own):
        size, here, width = self.size, self.here, own.shape[1]
        full = jnp.zeros((own.shape[0], size * width), own.dtype)
        full = lax.dynamic_update_slice(full, own, (0, here * width))
        for s in range(1, size):
            block = lax.ppermute(own, "tensor", [(i, (i + s) % size) for i in range(size)])
            slot = lax.rem(here - s + size, size)
            full = lax.dynamic_update_slice(full, block, (0, slot * width))
        return full

    def scatter(self, partial_value, width):
        size, here = self.size, self.here

        def block(index):
            start = jnp.clip(index, 0, size - 1) * width
            return lax.dynamic_slice_in_dim(partial_value, start, width, 1)

        a = b = None
        for s in range(size - 1):
            up = block(here + (size - 1 - s))
            down = block(here - (size - 1 - s))
            if s:
                up = (up.astype(F32) + a.astype(F32)).astype(BF)
                down = (down.astype(F32) + b.astype(F32)).astype(BF)
            a = lax.ppermute(up, "tensor", self.up)
            b = lax.ppermute(down, "tensor", self.down)
        return block(here).astype(F32) + a.astype(F32) + b.astype(F32)


def rotate(vectors, cos_tab, sin_tab):
    lower = vectors[:, : HD // 2]
    upper = vectors[:, HD // 2 :]
    return jnp.concatenate([lower * cos_tab - upper * sin_tab, upper * cos_tab + lower * sin_tab], 1)


def local(
    axes,
    layer_input_hidden,
    cotangent,
    valid_mask,
    span_starts,
    gain_attn,
    w_query,
    w_key,
    w_value,
    w_out,
    gain_mlp,
    w_gate,
    w_up,
    w_down,
):
    line = Line(axes["tensor"])
    here = line.here
    _, rows, width = layer_input_hidden.shape
    features = width * line.size
    kvs = w_key.shape[1] // HD
    heads = w_query.shape[1] // HD
    place = lax.axis_index("context")
    offset = place * rows
    own_columns = here * width

    def own(a):
        return lax.dynamic_slice_in_dim(a, own_columns, width, 1)

    position = offset + jnp.arange(rows, dtype=jnp.int32)
    length = jnp.sum(valid_mask[0])
    starts = span_starts[0]
    last = position
    for k in range(starts.shape[0]):
        inside = (position >= starts[k]) & (position < starts[k] + PIC)
        last = jnp.maximum(last, jnp.where(inside, starts[k] + PIC - 1, 0))
    kend = jnp.minimum(last + 1, length)[None, :]
    keep = (position < length).astype(F32)[:, None]
    inverse_freq = rope_base ** (-2.0 * jnp.arange(HD // 2, dtype=F32) / HD)
    angles = inverse_freq[:, None] * position.astype(F32)[None, :]
    cos_tab, sin_tab = jnp.cos(angles), jnp.sin(angles)

    gains = line.gather_small(jnp.stack([gain_attn, gain_mlp]))
    gain_a, gain_m = gains[:1], gains[1:]

    x_low = line.gather(layer_input_hidden[0])
    stream = x_low.astype(F32)
    square_a = jnp.sum(stream * stream, 1, keepdims=True)
    inv_a = lax.rsqrt(square_a / features + epsilon)
    normed_a = (stream * inv_a * gain_a).astype(BF)
    key_t = rotate(ein("sd,dx->xs", normed_a, w_key).reshape(kvs, HD, rows), cos_tab, sin_tab)
    value_t = ein("sd,dx->xs", normed_a, w_value).reshape(kvs, HD, rows)
    mine = jnp.concatenate([key_t, value_t]).astype(BF)
    if axes["context"] == 2:
        other = lax.ppermute(mine, "context", [(0, 1), (1, 0)])
        first = place == 0
        both = jnp.concatenate(
            [jnp.where(first, mine, other), jnp.where(first, other, mine)], axis=2
        )
    else:
        both = lax.all_gather(mine, "context", axis=2, tiled=True)
    kt_all, vt_all = both[:kvs], both[kvs:]
    k_all, v_all = jnp.swapaxes(kt_all, 1, 2), jnp.swapaxes(vt_all, 1, 2)
    query_t = rotate(
        ein("sd,dx->xs", normed_a, w_query).reshape(heads, HD, rows), cos_tab, sin_tab
    ).astype(BF)

    cot = line.gather(jnp.where(square_a[0, 0] >= 0.0, cotangent[0], 0.0))

    mixed, lse = attend_forward(query_t, k_all, vt_all, kend)
    mixed_t = mixed.reshape(heads * HD, rows)
    normed_m, act, gg, gu, down_part, back_part, middle, attn_square = feed_forward(
        line.size, mixed_t, keep, gain_m, w_out, w_gate, w_up, w_down, x_low, cot, GROUP_ROWS, HOP_ROWS
    )
    grad_middle, grad_attn, grad_mixed, gain_m_rows = norm_back(
        line.size, back_part, keep, gain_m, w_out, middle, cot, GROUP_ROWS, HOP_ROWS
    )
    middle_own, grad_middle_own = own(middle), own(grad_middle)
    grad_q, grad_k, grad_v = attend_backward(
        query_t, grad_mixed.reshape(heads, HD, rows), mixed, lse, k_all, kt_all, v_all, kend
    )

    def shard(grad, dim):
        return lax.psum_scatter(
            grad.astype(BF), ("dp", "context"), scatter_dimension=dim, tiled=True
        ).astype(F32)

    down_sum = shard(ein("sf,sd->fd", act, cot), 1)
    gate_sum = shard(ein("sd,sf->df", normed_m, gg), 0)
    up_sum = shard(ein("sd,sf->df", normed_m, gu), 0)
    out_sum = shard(ein("xs,sd->xd", mixed_t, grad_attn), 1)

    ffn_out = line.scatter(down_part, width)
    layer_out = (middle_own + ffn_out).astype(BF)

    def halves(a):
        return a.astype(BF).reshape(kvs, axes["context"], rows, HD)

    dkv = jnp.concatenate([halves(grad_k), halves(grad_v)])
    dkv_own = lax.dynamic_index_in_dim(dkv, place, 1, False).astype(F32)
    if axes["context"] == 2:
        sent = lax.ppermute(
            lax.dynamic_index_in_dim(dkv, 1 - place, 1, False), "context", [(0, 1), (1, 0)]
        )
        dkv_own = dkv_own + sent.astype(F32)
    else:
        dkv_own = lax.psum_scatter(dkv, "context", scatter_dimension=1, tiled=False).astype(F32)
    dkv_t = jnp.swapaxes(dkv_own, 1, 2)
    grad_query = (
        rotate(grad_q * SCALE, cos_tab, -sin_tab).astype(BF).reshape(-1, rows)
    )
    grad_key = rotate(dkv_t[:kvs] * SCALE, cos_tab, -sin_tab).astype(BF).reshape(-1, rows)
    grad_value = dkv_t[kvs:].astype(BF).reshape(-1, rows)

    query_sum = shard(ein("sd,xs->dx", normed_a, grad_query), 0)
    key_sum = shard(ein("sd,xs->dx", normed_a, grad_key), 0)
    value_sum = shard(ein("sd,xs->dx", normed_a, grad_value), 0)

    partial_a = (
        ein("xs,dx->sd", grad_query, w_query)
        + ein("xs,dx->sd", grad_key, w_key)
        + ein("xs,dx->sd", grad_value, w_value)
    )
    hat_a = x_low.astype(F32) * inv_a
    row_dot = lax.psum(jnp.sum(partial_a * (hat_a * gain_a), 1), "tensor")[:, None]
    gain_a_part = jnp.sum(partial_a * hat_a, 0)
    grad_a = line.scatter(partial_a.astype(BF), width)
    hat_own = layer_input_hidden[0].astype(F32) * inv_a
    through = inv_a * (grad_a * gain_attn[None, :] - hat_own * (row_dot / features))
    input_grad = (grad_middle_own + through).astype(BF)

    gain_m_part = lax.dynamic_update_slice(
        jnp.zeros((1, features), F32), own(gain_m_rows), (0, own_columns)
    )[0]
    numbers = jnp.stack(
        [
            jnp.sum(keep * square_a) / line.size,
            jnp.sum(attn_square) / line.size,
            jnp.sum(ffn_out * ffn_out),
            jnp.sum(keep) / line.size,
        ]
    )
    total = lax.psum(
        jnp.concatenate([gain_a_part, gain_m_part, numbers]), ("dp", "context", "tensor")
    )
    gain_a_sum = lax.dynamic_slice_in_dim(total, own_columns, width, 0)
    gain_m_sum = lax.dynamic_slice_in_dim(total, features + own_columns, width, 0)
    numbers = total[2 * features :]
    rms = jnp.sqrt(numbers[:3] / (numbers[3] * features))
    return (
        layer_out[None],
        input_grad[None],
        gain_a_sum,
        query_sum,
        key_sum,
        value_sum,
        out_sum,
        gain_m_sum,
        gate_sum,
        up_sum,
        down_sum,
        rms[0],
        rms[1],
        rms[2],
    )


def solution(mesh):
    token = P("dp", "context", "tensor")
    by_rows = P(("dp", "context"), "tensor")
    by_columns = P("tensor", ("dp", "context"))
    cols, rows, vec = P(None, "tensor"), P("tensor", None), P("tensor")
    return jax.shard_map(
        functools.partial(local, dict(mesh.shape)),
        mesh=mesh,
        in_specs=(
            token,
            token,
            P("dp", None),
            P("dp", None),
            vec,
            cols,
            cols,
            cols,
            rows,
            vec,
            cols,
            cols,
            rows,
        ),
        out_specs=(
            token,
            token,
            vec,
            by_rows,
            by_rows,
            by_rows,
            by_columns,
            vec,
            by_rows,
            by_rows,
            by_columns,
            P(),
            P(),
            P(),
        ),
        check_vma=False,
    )
```

time: 1910 us -> 1110 us (0.58)
  waiting for transfers between devices: 954 us -> 218 us
  Pallas kernels: 0 us -> 366 us
  matrix products: 417 us -> 108 us
  local copies, waits for them, and re-layouts: 265 us -> 70.4 us
  starting transfers between devices: 0.71 us -> 137 us
  other arithmetic: 144 us -> 104 us
    unnamed x23 -> x9, waiting for transfers between devices: 380 us -> 0.12 us
    pallas_call x0 -> x4, Pallas kernels: none -> 366 us  [the longest x1 167 us: feed_forward(): pl.pallas_call(functools.partial(ffn_kernel, size, hop, chunk), in_specs=...]
    all_gather x4 -> x0, waiting for transfers between devices: 348 us -> none  [the longest x2 185 us: normalize(): gathered = lax.all_gather(scaled, 'tensor', axis=2, tiled=True)]
    dot_general x35 -> x13, matrix products: 417 us -> 108 us  [ein(): return jnp.einsum(spec, a, b, preferred_element_type=F32)]
    reduce_scatter x7 -> x5, waiting for transfers between devices: 226 us -> 66.4 us  [shard(): lax.psum_scatter(grad.astype(BF), ('dp', 'context'), scatter_dimension=di...]
    unnamed x120 -> x98, local copies, waits for them, and re-layouts: 183 us -> 30.6 us
    ppermute x0 -> x29, waiting for transfers between devices: none -> 151 us  [the longest x6 51.6 us: gather(): b = lax.ppermute(b, 'tensor', self.down)]
    ppermute x0 -> x29, starting transfers between devices: none -> 136 us  [the longest x1 47.3 us: local(): lax.ppermute(lax.dynamic_index_in_dim(dkv, 1 - place, 1, False), 'context...]
  transfers between devices with their start and end apart: 17 -> 36, of which waited for: 14 -> 13; matrix products, arithmetic and copies ran while one was open for 14% -> 21% of each run, Pallas kernels for 0% -> 3%
where the time goes in v1:
time: 1110 us; the launch traced here: 1100 us
  Pallas kernels  366 us (33%)
  waiting for transfers between devices  218 us (20%)
  starting transfers between devices  137 us (12%)
  matrix products  108 us (10%)
  other arithmetic  104 us (9%)
  blocking collectives  75.2 us (7%)
  local copies, waits for them, and re-layouts  70.4 us (6%)
  between operations  21 us (2%)
    pallas_call x1, Pallas kernels, feed_forward(): pl.pallas_call(functools.partial(ffn_kernel, size, hop, chunk), in_specs=...  167 us
    pallas_call x1, Pallas kernels, norm_back(): pl.pallas_call(functools.partial(back_kernel, size, hop, chunk), in_specs...  139 us
    dot_general x13, matrix products, ein(): return jnp.einsum(spec, a, b, preferred_element_type=F32)  108 us
    reduce_scatter x5, waiting for transfers between devices, shard(): lax.psum_scatter(grad.astype(BF), ('dp', 'context'), scatter_dimension=di...  66.4 us
    ppermute x6, waiting for transfers between devices, gather(): b = lax.ppermute(b, 'tensor', self.down)  51.6 us
    ppermute x1, starting transfers between devices, local(): lax.ppermute(lax.dynamic_index_in_dim(dkv, 1 - place, 1, False), 'context...  47.3 us
    ppermute x6, waiting for transfers between devices, scatter(): a = lax.ppermute(up, 'tensor', self.up)  43.2 us
    psum x1, blocking collectives, local(): lax.psum(jnp.concatenate([gain_a_part, gain_m_part, numbers]), ('dp', 'co...  41.5 us
  transfers between devices with their start and end apart: 36, of which 13 were waited for; matrix products, arithmetic and copies ran while one was open for 21% of the time, Pallas kernels for 3%

profile of v1, /device:TPU:0, one launch (start us, length us, event | category | flops | bytes accessed | tf_op | source)
XLA Modules:
  0.0 1100.4 jit_solution(2196464280717127125)
XLA Ops:
  15.5 26.1 %collective-permute-done.1 = bf16[1024,640]{1,0:T(8,128)(2,1)} collective-permute-done((bf16[1024,640]{1,0:T(8,128)(2,1)}, bf16[1024,640]{1,0:T(8,128)(2,1)}, u32[]{:S(2)}, u32[]{:S(2)}) %collective-permute-start.1) | collective-permute-done | bytes 1310752 | tf_op jit(solution)/shard_map/ppermute | solution.py:779
  78.1 12.5 %collective-permute-done.4 = bf16[1024,640]{1,0:T(8,128)(2,1)} collective-permute-done((bf16[1024,640]{1,0:T(8,128)(2,1)}, bf16[1024,640]{1,0:T(8,128)(2,1)}, u32[]{:S(2)}, u32[]{:S(2)}) %collective-permute-start.4) | collective-permute-done | bytes 1310752 | tf_op jit(solution)/shard_map/ppermute | solution.py:778
  110.4 10.0 collective-permute-done.5
  182.0 15.6 %collective-permute-done.12 = bf16[1024,640]{1,0:T(8,128)(2,1)} collective-permute-done((bf16[1024,640]{1,0:T(8,128)(2,1)}, bf16[1024,640]{1,0:T(8,128)(2,1)}, u32[]{:S(2)}, u32[]{:S(2)}) %collective-permute-start.12) | collective-permute-done | bytes 1310752 | tf_op jit(solution)/shard_map/ppermute | solution.py:779
  213.1 32.4 %attend_fwd.1 = (bf16[8,80,1024]{2,1,0:T(8,128)(2,1)S(1)}, f32[8,1,1024]{2,1,0:T(1,128)S(1)}) custom-call(s32[4,2]{1,0:T(4,128)S(1)} %pad_add_fusion.lim_ref, s32[1,1024]{1,0:T(1,128)S(1)} %fusion.20.kend_ref, bf16[8,80,1024]{2,1,0:T(8,128)(2,1)S(1)} %copy-done.5, bf16[2,2048,80]{2,1,0:T(8,128)(2,1)S(1)} %bitcast.82, bf16[2,80,2048]{2,1,0:T(8,128)(2,1)S(1)} %copy-done.8), custom_call_target="tpu_custom_call" | custom-call | flops 13421772800 | bytes 8388608 | tf_op jit(solution)/shard_map/attend_fwd/pallas_call | solution.py:88
  254.8 167.1 %feed_forward.1 = (bf16[1024,2560]{1,0:T(8,128)(2,1)}, bf16[1024,1792]{1,0:T(8,128)(2,1)}, bf16[1024,1792]{1,0:T(8,128)(2,1)}, bf16[1024,1792]{1,0:T(8,128)(2,1)...) custom-call(bf16[640,1024]{1,0:T(8,128)(2,1)} %bitcast.85, ...), custom_call_target="tpu_custom_call" | custom-call | flops 59726888960 | bytes 83886080 | tf_op jit(solution)/shard_map/feed_forward/pallas_call | solution.py:568
  421.9 138.6 %norm_back.1 = (f32[1024,2560]{1,0:T(8,128)}, bf16[1024,2560]{1,0:T(8,128)(2,1)}, bf16[640,1024]{1,0:T(8,128)(2,1)}, f32[1,2560]{1,0:T(1,128)}) custom-call(bf16[1024,2560]{1,0:T(8,128)(2,1)} %get-tuple-element.34.parts, f32[1024,1]{1,0:T(8,128)} %fusion.15.keep, f32[1,2560]{1,0:T(1,128)} %get-tuple-element.79.gain, bf16[640,2560]{1,0:T(8,128)(2,1)} %w_out.3, ...), custom_call_target="tpu_custom_call" | custom-call | flops 3355443200 | bytes 41943040 | tf_op jit(solution)/shard_map/norm_back/pallas_call | solution.py:729
  567.0 28.4 %attend_bwd.1 = (f32[8,80,1024]{2,1,0:T(8,128)S(1)}, f32[2,2048,80]{2,1,0:T(8,128)S(1)}, f32[2,2048,80]{2,1,0:T(8,128)S(1)}) custom-call(s32[4,2]{1,0:T(4,128)S(1)} %pad_add_fusion.1.lim_ref, s32[1,1024]{1,0:T(1,128)S(1)} %fusion.20.kend_ref, bf16[8,80,1024]{2,1,0:T(8,128)(2,1)S(1)} %copy-done.6, bf16[8,80,1024]{2,1,0:T(8,128)(2,1)S(1)} %bitcast.84, ...), custom_call_target="tpu_custom_call" | custom-call | flops 21474836480 | bytes 16777216 | tf_op jit(solution)/shard_map/attend_bwd/pallas_call | solution.py:172
  601.1 47.3 %collective-permute-start.22 = (bf16[4,1024,80]{1,2,0:T(8,128)(2,1)}, bf16[4,1024,80]{1,2,0:T(8,128)(2,1)}, u32[]{:S(2)}, u32[]{:S(2)}) collective-permute-start(bf16[4,1024,80]{1,2,0:T(8,128)(2,1)} %bitcast.104), channel_id=1, source_target_pairs={{0,4},{4,0},{1,5},{5,1},{2,6},{6,2},{3,7},{7,3},{8,12},{12,8},{9,1... | collective-permute-start | bytes 1966088 | tf_op jit(solution)/shard_map/ppermute | solution.py:924
  691.2 8.5 convolution_convert_fusion.4
  699.8 9.0 convolution_convert_fusion.3
  709.2 14.9 %convolution_convert_fusion = bf16[1792,2560]{0,1:T(8,128)(2,1)} fusion(bf16[1024,1792]{1,0:T(8,128)(2,1)} %get-tuple-element.47, bf16[1024,2560]{1,0:T(8,128)(2,1)} %select_dynamic-update-slice_fusion.cot), kind=kOutput, calls=%fused_computation.6 | convolution fusion | flops 9399828480 | bytes 18087936 | tf_op jit(solution)/shard_map/sf,sd->fd/dot_general | solution.py:37
  724.2 15.1 %convolution_convert_fusion.1 = bf16[2560,1792]{1,0:T(8,128)(2,1)} fusion(bf16[1024,2560]{1,0:T(8,128)(2,1)} %get-tuple-element.44, bf16[1024,1792]{1,0:T(8,128)(2,1)} %get-tuple-element.46), kind=kOutput, calls=%fused_computation.7 | convolution fusion | flops 9399828480 | bytes 18087936 | tf_op jit(solution)/shard_map/sd,sf->df/dot_general | solution.py:37
  739.6 15.0 %convolution_convert_fusion.2 = bf16[2560,1792]{1,0:T(8,128)(2,1)} fusion(bf16[1024,2560]{1,0:T(8,128)(2,1)} %get-tuple-element.44, bf16[1024,1792]{1,0:T(8,128)(2,1)} %get-tuple-element.45), kind=kOutput, calls=%fused_computation.8 | convolution fusion | flops 9399828480 | bytes 18087936 | tf_op jit(solution)/shard_map/sd,sf->df/dot_general | solution.py:37
  760.7 8.3 fusion.47
  774.6 9.8 fusion.5
  803.2 15.5 %collective-permute-done.23 = bf16[1024,640]{1,0:T(8,128)(2,1)} collective-permute-done((bf16[1024,640]{1,0:T(8,128)(2,1)}, bf16[1024,640]{1,0:T(8,128)(2,1)}, u32[]{:S(2)}, u32[]{:S(2)}) %collective-permute-start.23) | collective-permute-done | bytes 1310752 | tf_op jit(solution)/shard_map/ppermute | solution.py:812
  829.5 15.8 %collective-permute-done.17 = bf16[1024,640]{1,0:T(8,128)(2,1)} collective-permute-done((bf16[1024,640]{1,0:T(8,128)(2,1)}, bf16[1024,640]{1,0:T(8,128)(2,1)}, u32[]{:S(2)}, u32[]{:S(2)}) %collective-permute-start.17) | collective-permute-done | bytes 1310752 | tf_op jit(solution)/shard_map/ppermute | solution.py:812
  851.2 11.9 %collective-permute-done.24 = bf16[1024,640]{1,0:T(8,128)(2,1)} collective-permute-done((bf16[1024,640]{1,0:T(8,128)(2,1)}, bf16[1024,640]{1,0:T(8,128)(2,1)}, u32[]{:S(2)}, u32[]{:S(2)}) %collective-permute-start.24) | collective-permute-done | bytes 1310752 | tf_op jit(solution)/shard_map/ppermute | solution.py:812
  876.3 8.0 collective-permute-done.20
  894.4 18.0 %collective-permute-done.27 = bf16[1024,640]{1,0:T(8,128)(2,1)} collective-permute-done((bf16[1024,640]{1,0:T(8,128)(2,1)}, bf16[1024,640]{1,0:T(8,128)(2,1)}, u32[]{:S(2)}, u32[]{:S(2)}) %collective-permute-start.27) | collective-permute-done | bytes 1310752 | tf_op jit(solution)/shard_map/ppermute | solution.py:813
  921.6 33.7 %psum.14 = f32[1024]{0:T(1024)S(1)} all-reduce(f32[1024]{0:T(1024)S(1)} %get-tuple-element.49), channel_id=1, replica_groups=mesh['dp'=4,'context'=2,'tensor'=4] {'tensor'}, use_global_device_ids=true, to_apply=%region_5.6 | all-reduce | flops 1024 | bytes 8192 | tf_op jit(solution)/shard_map/psum | solution.py:947
  968.9 41.5 %psum.15 = f32[5124]{0:T(1024)S(1)} all-reduce(f32[5124]{0:T(1024)S(1)} %concatenate.36), channel_id=1, replica_groups=mesh['dp'=4,'context'=2,'tensor'=4] {'dp','context','tensor'}, use_global_device_ids=true, to_apply=%region_11.12 | all-reduce | flops 5124 | bytes 40992 | tf_op jit(solution)/shard_map/psum | solution.py:965
  1024.2 66.4 %reduce-scatter.16.cloned.1.call-done = bf16[320,1792]{1,0:T(8,128)(2,1)} async-done(((bf16[2560,1792]{1,0:T(8,128)(2,1)}), bf16[320,1792]{1,0:T(8,128)(2,1)}) %reduce-scatter.16.cloned.1.call-update) | async-done | bytes 1146896 | tf_op jit(solution)/shard_map/reduce_scatter | solution.py:906
  (268 shorter events, 310.2 us)
Async XLA Ops:
  7.2 948.1 %reduce-scatter.22.cloned.1.call-start = ((), (), s32[]{:S(2)}) async-start(), calls=%async_computation.12 | async-start | bytes 1474560
  8.8 52.7 %collective-permute-start = (bf16[1024,640]{1,0:T(8,128)(2,1)}, bf16[1024,640]{1,0:T(8,128)(2,1)}, u32[]{:S(2)}, u32[]{:S(2)}) collective-permute-start(bf16[1024,640]{1,0:T(8,128)(2,1)} %bitcast.96), channel_id=1, source_target_pairs={{0,1},{1,2},{2,3},{4,5},{5,6},{6,7},{8,9},{9,10},{10,11},{12,13},{... | collective-permute-start | bytes 3932168 | tf_op jit(solution)/shard_map/ppermute | solution.py:778
  44.2 54.9 %collective-permute-start.7 = (f32[2,640]{1,0:T(2,128)S(1)}, f32[2,640]{1,0:T(2,128)S(1)}, u32[]{:S(2)}, u32[]{:S(2)}) collective-permute-start(f32[2,640]{1,0:T(2,128)S(1)} %get-tuple-element.81), channel_id=1, source_target_pairs={{0,2},{1,3},{2,0},{3,1},{4,6},{5,7},{6,4},{7,5},{8,10},{9,11},{10,... | collective-permute-start | bytes 15368 | tf_op jit(solution)/shard_map/ppermute | solution.py:793
  48.1 51.0 %collective-permute-start.6 = (f32[2,640]{1,0:T(2,128)S(1)}, f32[2,640]{1,0:T(2,128)S(1)}, u32[]{:S(2)}, u32[]{:S(2)}) collective-permute-start(f32[2,640]{1,0:T(2,128)S(1)} %get-tuple-element.81), channel_id=1, source_target_pairs={{0,1},{1,2},{2,3},{3,0},{4,5},{5,6},{6,7},{7,4},{8,9},{9,10},{10,1... | collective-permute-start | bytes 15368 | tf_op jit(solution)/shard_map/ppermute | solution.py:793
  50.8 48.3 %collective-permute-start.8 = (f32[2,640]{1,0:T(2,128)S(1)}, f32[2,640]{1,0:T(2,128)S(1)}, u32[]{:S(2)}, u32[]{:S(2)}) collective-permute-start(f32[2,640]{1,0:T(2,128)S(1)} %get-tuple-element.81), channel_id=1, source_target_pairs={{0,3},{1,0},{2,1},{3,2},{4,7},{5,4},{6,5},{7,6},{8,11},{9,8},{10,9... | collective-permute-start | bytes 15368 | tf_op jit(solution)/shard_map/ppermute | solution.py:793
  163.0 41.9 %collective-permute-start.14 = (bf16[1024,640]{1,0:T(8,128)(2,1)}, bf16[1024,640]{1,0:T(8,128)(2,1)}, u32[]{:S(2)}, u32[]{:S(2)}) collective-permute-start(bf16[1024,640]{1,0:T(8,128)(2,1)} %collective-permute-done.10), channel_id=1, source_target_pairs={{0,1},{1,2},{2,3},{4,5},{5,6},{6,7},{8,9},{9,10},{10,11},{12,13},{... | collective-permute-start | bytes 3932168 | tf_op jit(solution)/shard_map/ppermute | solution.py:778
  197.5 49.0 %collective-permute-start.13 = (bf16[1024,640]{1,0:T(8,128)(2,1)}, bf16[1024,640]{1,0:T(8,128)(2,1)}, u32[]{:S(2)}, u32[]{:S(2)}) collective-permute-start(bf16[1024,640]{1,0:T(8,128)(2,1)} %collective-permute-done.12), channel_id=1, source_target_pairs={{1,0},{2,1},{3,2},{5,4},{6,5},{7,6},{9,8},{10,9},{11,10},{13,12},{... | collective-permute-start | bytes 3932168 | tf_op jit(solution)/shard_map/ppermute | solution.py:779
  204.9 47.2 %collective-permute-start.15 = (bf16[1024,640]{1,0:T(8,128)(2,1)}, bf16[1024,640]{1,0:T(8,128)(2,1)S(1)}, u32[]{:S(2)}, u32[]{:S(2)}) collective-permute-start(bf16[1024,640]{1,0:T(8,128)(2,1)} %collective-permute-done.14), channel_id=1, source_target_pairs={{0,1},{1,2},{2,3},{4,5},{5,6},{6,7},{8,9},{9,10},{10,11},{12,13},{... | collective-permute-start | bytes 3932168 | tf_op jit(solution)/shard_map/ppermute | solution.py:778
  601.1 56.2 %collective-permute-start.22 = (bf16[4,1024,80]{1,2,0:T(8,128)(2,1)}, bf16[4,1024,80]{1,2,0:T(8,128)(2,1)}, u32[]{:S(2)}, u32[]{:S(2)}) collective-permute-start(bf16[4,1024,80]{1,2,0:T(8,128)(2,1)} %bitcast.104), channel_id=1, source_target_pairs={{0,4},{4,0},{1,5},{5,1},{2,6},{6,2},{3,7},{7,3},{8,12},{12,8},{9,1... | collective-permute-start | bytes 1966088 | tf_op jit(solution)/shard_map/ppermute | solution.py:924
  672.7 284.4 %reduce-scatter.24.cloned.1.call-start = ((), (), s32[]{:S(2)}) async-start(), calls=%async_computation.13 | async-start | bytes 1474560
  687.6 271.2 %reduce-scatter.12.cloned.1.call-start = ((), (), s32[]{:S(2)}) async-start(), calls=%async_computation.7 | async-start | bytes 3686400 | tf_op jit(solution)/shard_map/reduce_scatter | solution.py:906
  699.7 261.0 %reduce-scatter.14.cloned.1.call-start = ((), (), s32[]{:S(2)}) async-start(), calls=%async_computation.8 | async-start | bytes 3686400 | tf_op jit(solution)/shard_map/reduce_scatter | solution.py:906
  708.8 309.6 %reduce-scatter.20.cloned.1.call-start = ((), (), s32[]{:S(2)}) async-start(), calls=%async_computation.11 | async-start | bytes 10321920 | tf_op jit(solution)/shard_map/reduce_scatter | solution.py:906
  724.1 297.1 %reduce-scatter.18.cloned.1.call-start = ((), (), s32[]{:S(2)}) async-start(), calls=%async_computation.10 | async-start | bytes 10321920 | tf_op jit(solution)/shard_map/reduce_scatter | solution.py:906
  739.4 351.2 %reduce-scatter.16.cloned.1.call-start = ((), (), s32[]{:S(2)}) async-start(), calls=%async_computation.9 | async-start | bytes 10321920 | tf_op jit(solution)/shard_map/reduce_scatter | solution.py:906
  790.3 39.2 %collective-permute-start.19 = (bf16[1024,640]{1,0:T(8,128)(2,1)}, bf16[1024,640]{1,0:T(8,128)(2,1)}, u32[]{:S(2)}, u32[]{:S(2)}) collective-permute-start(bf16[1024,640]{1,0:T(8,128)(2,1)} %get-tuple-element.62), channel_id=1, source_target_pairs={{1,0},{2,1},{3,2},{5,4},{6,5},{7,6},{9,8},{10,9},{11,10},{13,12},{... | collective-permute-start | bytes 3932168 | tf_op jit(solution)/shard_map/ppermute | solution.py:813
  794.7 50.6 %collective-permute-start.17 = (bf16[1024,640]{1,0:T(8,128)(2,1)}, bf16[1024,640]{1,0:T(8,128)(2,1)}, u32[]{:S(2)}, u32[]{:S(2)}) collective-permute-start(bf16[1024,640]{1,0:T(8,128)(2,1)} %add_convert_fusion.9), channel_id=1, source_target_pairs={{0,1},{1,2},{2,3},{4,5},{5,6},{6,7},{8,9},{9,10},{10,11},{12,13},{... | collective-permute-start | bytes 3932168 | tf_op jit(solution)/shard_map/ppermute | solution.py:812
  801.9 49.3 %collective-permute-start.26 = (bf16[1024,640]{1,0:T(8,128)(2,1)}, bf16[1024,640]{1,0:T(8,128)(2,1)}, u32[]{:S(2)}, u32[]{:S(2)}) collective-permute-start(bf16[1024,640]{1,0:T(8,128)(2,1)} %get-tuple-element.58), channel_id=1, source_target_pairs={{1,0},{2,1},{3,2},{5,4},{6,5},{7,6},{9,8},{10,9},{11,10},{13,12},{... | collective-permute-start | bytes 3932168 | tf_op jit(solution)/shard_map/ppermute | solution.py:813
  821.9 41.2 %collective-permute-start.24 = (bf16[1024,640]{1,0:T(8,128)(2,1)}, bf16[1024,640]{1,0:T(8,128)(2,1)}, u32[]{:S(2)}, u32[]{:S(2)}) collective-permute-start(bf16[1024,640]{1,0:T(8,128)(2,1)} %add_convert_fusion.4), channel_id=1, source_target_pairs={{0,1},{1,2},{2,3},{4,5},{5,6},{6,7},{8,9},{9,10},{10,11},{12,13},{... | collective-permute-start | bytes 3932168 | tf_op jit(solution)/shard_map/ppermute | solution.py:812
  868.8 43.6 %collective-permute-start.27 = (bf16[1024,640]{1,0:T(8,128)(2,1)}, bf16[1024,640]{1,0:T(8,128)(2,1)}, u32[]{:S(2)}, u32[]{:S(2)}) collective-permute-start(bf16[1024,640]{1,0:T(8,128)(2,1)} %get-tuple-element.56), channel_id=1, source_target_pairs={{1,0},{2,1},{3,2},{5,4},{6,5},{7,6},{9,8},{10,9},{11,10},{13,12},{... | collective-permute-start | bytes 3932168 | tf_op jit(solution)/shard_map/ppermute | solution.py:813
  870.1 92.7 %collective-permute-start.18 = (bf16[1024,640]{1,0:T(8,128)(2,1)}, bf16[1024,640]{1,0:T(8,128)(2,1)}, u32[]{:S(2)}, u32[]{:S(2)}) collective-permute-start(bf16[1024,640]{1,0:T(8,128)(2,1)} %get-tuple-element.59), channel_id=1, source_target_pairs={{0,1},{1,2},{2,3},{4,5},{5,6},{6,7},{8,9},{9,10},{10,11},{12,13},{... | collective-permute-start | bytes 3932168 | tf_op jit(solution)/shard_map/ppermute | solution.py:812
  887.4 75.4 %collective-permute-start.21 = (bf16[1024,640]{1,0:T(8,128)(2,1)}, bf16[1024,640]{1,0:T(8,128)(2,1)}, u32[]{:S(2)}, u32[]{:S(2)}) collective-permute-start(bf16[1024,640]{1,0:T(8,128)(2,1)} %add_convert_fusion.6), channel_id=1, source_target_pairs={{1,0},{2,1},{3,2},{5,4},{6,5},{7,6},{9,8},{10,9},{11,10},{13,12},{... | collective-permute-start | bytes 3932168 | tf_op jit(solution)/shard_map/ppermute | solution.py:813
  888.8 124.1 %collective-permute-start.25 = (bf16[1024,640]{1,0:T(8,128)(2,1)}, bf16[1024,640]{1,0:T(8,128)(2,1)}, u32[]{:S(2)}, u32[]{:S(2)}) collective-permute-start(bf16[1024,640]{1,0:T(8,128)(2,1)} %get-tuple-element.55), channel_id=1, source_target_pairs={{0,1},{1,2},{2,3},{4,5},{5,6},{6,7},{8,9},{9,10},{10,11},{12,13},{... | collective-permute-start | bytes 3932168 | tf_op jit(solution)/shard_map/ppermute | solution.py:812
  915.5 97.5 %collective-permute-start.28 = (bf16[1024,640]{1,0:T(8,128)(2,1)}, bf16[1024,640]{1,0:T(8,128)(2,1)}, u32[]{:S(2)}, u32[]{:S(2)}) collective-permute-start(bf16[1024,640]{1,0:T(8,128)(2,1)} %add_convert_fusion.1), channel_id=1, source_target_pairs={{1,0},{2,1},{3,2},{5,4},{6,5},{7,6},{9,8},{10,9},{11,10},{13,12},{... | collective-permute-start | bytes 3932168 | tf_op jit(solution)/shard_map/ppermute | solution.py:813
  (58 other events, 1129.3 us)
Sparse Core Ops, SparseCore 0:
  672.8 39.0 reduce-scatter.21
  715.1 37.3 reduce-scatter.23
  755.9 46.8 reduce-scatter.11
  806.1 46.8 reduce-scatter.13
  856.5 75.0 reduce-scatter.19
  935.5 76.3 reduce-scatter.17
  1015.5 75.0 reduce-scatter.15

commit v2 on v1

--- a/solution.py
+++ b/solution.py
@@ -161,7 +161,7 @@
     lax.fori_loop(lim_ref[pl.program_id(1), 0], lim_ref[pl.program_id(1), 1], functools.partial(step, True), 0)
 
 
-def attend_backward(q, do, o, lse, k, kt, v, kend):
+def attend_backward(q, do, o, lse, k, kt, v, kend, after):
     heads, _, total = q.shape
     rows = GROUP_ROWS
     kvs, keys, _ = k.shape
@@ -169,8 +169,12 @@
     key_rows = min(KEY_ROWS_BWD, keys)
     by_head = pl.BlockSpec((group, HD, rows), lambda g, i: (g, 0, i))
     by_key = pl.BlockSpec((1, keys, HD), lambda g, i: (g, 0, 0))
+
+    def kernel(*refs):
+        backward_kernel(group, key_rows, *refs[:9], *refs[9 + len(after) :])
+
     return pl.pallas_call(
-        functools.partial(backward_kernel, group, key_rows),
+        kernel,
         grid=(kvs, total // rows),
         in_specs=[
             pl.BlockSpec(memory_space=pltpu.SMEM),
@@ -182,7 +186,8 @@
             by_key,
             pl.BlockSpec((1, HD, keys), lambda g, i: (g, 0, 0)),
             by_key,
-        ],
+        ]
+        + [pl.BlockSpec(memory_space=pl.ANY)] * len(after),
         out_specs=[by_head, by_key, by_key],
         out_shape=[
             jax.ShapeDtypeStruct((heads, HD, total), F32),
@@ -202,7 +207,7 @@
             transcendentals=heads * total * keys,
         ),
         name="attend_bwd",
-    )(key_limits(kend, key_rows), kend, q, do, o, lse, k, kt, v)
+    )(key_limits(kend, key_rows), kend, q, do, o, lse, k, kt, v, *after)
 
 
 MESH_ID = pl.DeviceIdType.MESH
@@ -721,14 +726,18 @@
         save_low(c).wait()
 
 
-def norm_back(size, parts, keep, gain, w_out, middle, cot, chunk, hop):
+def norm_back(size, parts, keep, gain, w_out, middle, cot, chunk, hop, after):
     rows, features = middle.shape
     per = chunk // hop
     anywhere, vmem = pl.BlockSpec(memory_space=pl.ANY), pl.BlockSpec(memory_space=pltpu.VMEM)
     shape = jax.ShapeDtypeStruct
+
+    def kernel(*refs):
+        back_kernel(size, hop, chunk, *refs[:6], *refs[6 + len(after) :])
+
     return pl.pallas_call(
-        functools.partial(back_kernel, size, hop, chunk),
-        in_specs=[vmem] * 3 + [anywhere] * 3,
+        kernel,
+        in_specs=[vmem] * 3 + [anywhere] * (3 + len(after)),
         out_specs=[anywhere] * 2 + [vmem] * 2,
         out_shape=[
             shape((rows, features), F32),
@@ -758,7 +767,513 @@
             transcendentals=rows,
         ),
         name="norm_back",
-    )(parts, keep, gain, w_out, middle, cot)
+    )(parts, keep, gain, w_out, middle, cot, *after)
+
+
+def greet(peers):
+    barrier = pltpu.get_barrier_semaphore()
+    for peer in peers:
+        pl.semaphore_signal(barrier, inc=1, device_id=peer, device_id_type=MESH_ID)
+    pl.semaphore_wait(barrier, len(peers))
+
+
+def others(axis, size):
+    here = lax.axis_index(axis)
+    return [lax.rem(here + i, size) for i in range(1, size)]
+
+
+def project_kernel(
+    size, contexts, chunk,
+    own, gain_own, cos_tab, sin_tab, w_query, w_key, w_value,
+    x_o, normed_o, inv_o, gain_o, query_o, kv_o,
+    xs, gains, full, normed, kv, wq, wk, wv,
+    up_send, up_recv, down_send, down_recv, gain_send, gain_recv, kv_send, kv_recv,
+    own_sem, w_sem, out_sem, kv_sem,
+):
+    here, place = lax.axis_index("tensor"), lax.axis_index("context")
+    rows, width = own.shape
+    features = size * width
+    groups, steps = rows // chunk, size - 1
+    heads, kvs = w_query.shape[1] // HD, w_key.shape[1] // HD
+    bottom, top = here == 0, here == size - 1
+
+    loads = [
+        pltpu.make_async_copy(a, b, w_sem.at[i])
+        for i, (a, b) in enumerate(((w_query, wq), (w_key, wk), (w_value, wv)))
+    ]
+
+    def load_own(g):
+        part = pl.ds(g * chunk, chunk)
+        return pltpu.make_async_copy(own.at[part], xs.at[here, part], own_sem.at[g])
+
+    for g in range(groups):
+        load_own(g).start()
+    for load in loads:
+        load.start()
+    gains[here] = gain_own[...]
+
+    def block(owner, g):
+        return xs.at[owner, pl.ds(g * chunk, chunk)]
+
+    def up(g, s):
+        owner = jnp.clip(here - s, 0, size - 1)
+        return pltpu.make_async_remote_copy(
+            src_ref=block(owner, g),
+            dst_ref=block(owner, g),
+            send_sem=up_send.at[g, s],
+            recv_sem=up_recv.at[g, s],
+            device_id={"tensor": here + 1},
+            device_id_type=MESH_ID,
+        )
+
+    def down(g, s):
+        owner = jnp.clip(here + s, 0, size - 1)
+        return pltpu.make_async_remote_copy(
+            src_ref=block(owner, g),
+            dst_ref=block(owner, g),
+            send_sem=down_send.at[g, s],
+            recv_sem=down_recv.at[g, s],
+            device_id={"tensor": here - 1},
+            device_id_type=MESH_ID,
+        )
+
+    def send(g, s):
+        @pl.when((here >= s) & jnp.logical_not(top))
+        def _():
+            up(g, s).start()
+
+        @pl.when((here + s < size) & jnp.logical_not(bottom))
+        def _():
+            down(g, s).start()
+
+    def sent(g, s):
+        @pl.when((here >= s) & jnp.logical_not(top))
+        def _():
+            up(g, s).wait_send()
+
+        @pl.when((here + s < size) & jnp.logical_not(bottom))
+        def _():
+            down(g, s).wait_send()
+
+    def receive(g, s):
+        @pl.when(here - 1 - s >= 0)
+        def _():
+            up(g, s).wait_recv()
+
+        @pl.when(here + 1 + s < size)
+        def _():
+            down(g, s).wait_recv()
+
+    tensor_peers = [{"tensor": i} for i in others("tensor", size)]
+    context_peers = [{"context": i} for i in others("context", contexts)]
+    greet(tensor_peers + context_peers)
+
+    def gain_copy(i):
+        return pltpu.make_async_remote_copy(
+            src_ref=gains.at[here],
+            dst_ref=gains.at[here],
+            send_sem=gain_send.at[i],
+            recv_sem=gain_recv.at[i],
+            device_id=tensor_peers[i],
+            device_id_type=MESH_ID,
+        )
+
+    def kv_copy(g, i):
+        part = kv.at[:, :, pl.ds(pl.multiple_of(place * rows + g * chunk, chunk), chunk)]
+        return pltpu.make_async_remote_copy(
+            src_ref=part,
+            dst_ref=part,
+            send_sem=kv_send.at[g, i],
+            recv_sem=kv_recv.at[g, i],
+            device_id=context_peers[i],
+            device_id_type=MESH_ID,
+        )
+
+    load_own(0).wait()
+    send(0, 0)
+    for i in range(size - 1):
+        gain_copy(i).start()
+
+    def save(g):
+        part = pl.ds(g * chunk, chunk)
+        return [
+            pltpu.make_async_copy(full, x_o.at[part], out_sem.at[0]),
+            pltpu.make_async_copy(normed, normed_o.at[part], out_sem.at[1]),
+        ]
+
+    def turn(u, cos_t, sin_t):
+        lower, upper = u[: HD // 2], u[HD // 2 :]
+        return jnp.concatenate([lower * cos_t - upper * sin_t, upper * cos_t + lower * sin_t], 0)
+
+    def compute(g):
+        part = pl.ds(pl.multiple_of(g * chunk, chunk), chunk)
+
+        @pl.when(g == 0)
+        def _():
+            for load in loads:
+                load.wait()
+            for i in range(size - 1):
+                gain_copy(i).wait_recv()
+            gain_o[...] = jnp.concatenate([gains[j] for j in range(size)], 1)
+
+        @pl.when(g > 0)
+        def _():
+            for copy in save(g - 1):
+                copy.wait()
+
+        full[...] = jnp.concatenate([xs[j, part, :] for j in range(size)], 1)
+        stream = full[...].astype(F32)
+        inv = lax.rsqrt(jnp.sum(stream * stream, 1, keepdims=True) / features + epsilon)
+        inv_o[part, :] = inv
+        normed[...] = (stream * inv * gain_o[0:1, :]).astype(BF)
+        for copy in save(g):
+            copy.start()
+        cos_t, sin_t = cos_tab[:, part], sin_tab[:, part]
+        mine = pl.ds(pl.multiple_of(place * rows + g * chunk, chunk), chunk)
+        key = dot(normed[...], wk[...]).T
+        value = dot(normed[...], wv[...]).T
+        for h in range(kvs):
+            kv[h, :, mine] = turn(key[h * HD : (h + 1) * HD], cos_t, sin_t).astype(BF)
+            kv[kvs + h, :, mine] = value[h * HD : (h + 1) * HD].astype(BF)
+        for i in range(contexts - 1):
+            kv_copy(g, i).start()
+        query = dot(normed[...], wq[...]).T
+        for h in range(heads):
+            query_o[h, :, part] = turn(query[h * HD : (h + 1) * HD], cos_t, sin_t).astype(BF)
+
+    def tick(k, _):
+        g, s = lax.div(k, steps), lax.rem(k, steps)
+
+        @pl.when(s > 0)
+        def _():
+            receive(g, s - 1)
+            send(g, s)
+
+        @pl.when((s == steps - 1) & (g + 1 < groups))
+        def _():
+            load_own(g + 1).wait()
+            send(g + 1, 0)
+
+        @pl.when((s == 0) & (g > 0))
+        def _():
+            receive(g - 1, steps - 1)
+            compute(g - 1)
+
+        return 0
+
+    lax.fori_loop(0, groups * steps + 1, tick, 0)
+    for copy in save(groups - 1):
+        copy.wait()
+    for i in range(size - 1):
+        gain_copy(i).wait_send()
+    for g in range(groups):
+        for s in range(steps):
+            sent(g, s)
+        for i in range(contexts - 1):
+            kv_copy(g, i).wait()
+    out = pltpu.make_async_copy(kv, kv_o, kv_sem)
+    out.start()
+    out.wait()
+
+
+def project(axes, own, gain_own, cos_tab, sin_tab, w_query, w_key, w_value, chunk):
+    size, contexts = axes["tensor"], axes["context"]
+    rows, width = own.shape
+    features, groups = size * width, rows // chunk
+    heads, kvs = w_query.shape[1] // HD, w_key.shape[1] // HD
+    anywhere, vmem = pl.BlockSpec(memory_space=pl.ANY), pl.BlockSpec(memory_space=pltpu.VMEM)
+    shape, dma = jax.ShapeDtypeStruct, pltpu.SemaphoreType.DMA
+    return pl.pallas_call(
+        functools.partial(project_kernel, size, contexts, chunk),
+        in_specs=[anywhere] + [vmem] * 3 + [anywhere] * 3,
+        out_specs=[anywhere] * 2 + [vmem] * 3 + [anywhere],
+        out_shape=[
+            shape((rows, features), BF),
+            shape((rows, features), BF),
+            shape((rows, 1), F32),
+            shape((8, features), F32),
+            shape((heads, HD, rows), BF),
+            shape((2 * kvs, HD, contexts * rows), BF),
+        ],
+        scratch_shapes=[
+            pltpu.VMEM((size, rows, width), BF),
+            pltpu.VMEM((size, 8, width), F32),
+            pltpu.VMEM((chunk, features), BF),
+            pltpu.VMEM((chunk, features), BF),
+            pltpu.VMEM((2 * kvs, HD, contexts * rows), BF),
+            pltpu.VMEM(w_query.shape, BF),
+            pltpu.VMEM(w_key.shape, BF),
+            pltpu.VMEM(w_value.shape, BF),
+            dma((groups, size - 1)),
+            dma((groups, size - 1)),
+            dma((groups, size - 1)),
+            dma((groups, size - 1)),
+            dma((size - 1,)),
+            dma((size - 1,)),
+            dma((groups, max(contexts - 1, 1))),
+            dma((groups, max(contexts - 1, 1))),
+            dma((groups,)),
+            dma((3,)),
+            dma((2,)),
+            dma,
+        ],
+        compiler_params=pltpu.CompilerParams(
+            collective_id=3, has_side_effects=True, vmem_limit_bytes=VMEM_LIMIT
+        ),
+        cost_estimate=pl.CostEstimate(
+            flops=2 * rows * features * (heads + 2 * kvs) * HD,
+            bytes_accessed=20 << 20,
+            transcendentals=rows,
+        ),
+        name="project",
+    )(own, gain_own, cos_tab, sin_tab, w_query, w_key, w_value)
+
+
+def input_kernel(
+    size, chunk,
+    grads, inv, gain, w_query, w_key, w_value, x,
+    out_o, dot_o, gain_o,
+    parts, ups, downs, xs, wq, wk, wv, dots, cols,
+    up_send, up_recv, down_send, down_recv, dot_send, dot_recv, col_send, col_recv, w_sem, x_sem,
+):
+    here = lax.axis_index("tensor")
+    rows, features = x.shape
+    width, groups = features // size, rows // chunk
+    count = (size - 1) * groups
+    bottom, top = here == 0, here == size - 1
+    nq, nk = w_query.shape[1], w_key.shape[1]
+
+    loads = [
+        pltpu.make_async_copy(a, b, w_sem.at[i])
+        for i, (a, b) in enumerate(((w_query, wq), (w_key, wk), (w_value, wv)))
+    ]
+
+    def load_x(c):
+        slot = lax.rem(c, 2)
+        return pltpu.make_async_copy(x.at[pl.ds(c * chunk, chunk)], xs.at[slot], x_sem.at[slot])
+
+    for load in loads:
+        load.start()
+    load_x(0).start()
+    peers = [{"tensor": i} for i in others("tensor", size)]
+    greet(peers)
+    for load in loads:
+        load.wait()
+
+    def compute(c):
+        slot = lax.rem(c, 2)
+        part = pl.ds(pl.multiple_of(c * chunk, chunk), chunk)
+        load_x(c).wait()
+
+        @pl.when(c + 1 < groups)
+        def _():
+            load_x(c + 1).start()
+
+        g = grads[:, part].astype(F32).T.astype(BF)
+        whole = (
+            dot_nt(g[:, :nq], wq[...])
+            + dot_nt(g[:, nq : nq + nk], wk[...])
+            + dot_nt(g[:, nq + nk :], wv[...])
+        )
+        hat = xs[slot].astype(F32) * inv[part, :]
+        moved = whole * hat
+        rowsum = jnp.sum(moved * gain[0:1, :], 1, keepdims=True)
+        dots[here, :, part] = jnp.broadcast_to(rowsum, (chunk, 128)).T[:8]
+        colsum = jnp.sum(moved, 0, keepdims=True)
+        low = whole.astype(BF)
+        for j in range(size):
+            parts[j, part, :] = low[:, j * width : (j + 1) * width]
+            piece = jnp.broadcast_to(colsum[:, j * width : (j + 1) * width], (8, width))
+
+            @pl.when(c == 0)
+            def _():
+                cols[j] = piece
+
+            @pl.when(c > 0)
+            def _():
+                cols[j] += piece
+
+    def rows_of(m):
+        return pl.ds(pl.multiple_of(lax.rem(m, groups) * chunk, chunk), chunk)
+
+    def up(m, first):
+        owner = size - 1 - lax.div(m, groups)
+        return pltpu.make_async_remote_copy(
+            src_ref=parts.at[owner, rows_of(m)] if first else ups.at[m],
+            dst_ref=ups.at[m],
+            send_sem=up_send.at[m],
+            recv_sem=up_recv.at[m],
+            device_id={"tensor": here + 1},
+            device_id_type=MESH_ID,
+        )
+
+    def down(m, first):
+        owner = lax.div(m, groups)
+        return pltpu.make_async_remote_copy(
+            src_ref=parts.at[owner, rows_of(m)] if first else downs.at[m],
+            dst_ref=downs.at[m],
+            send_sem=down_send.at[m],
+            recv_sem=down_recv.at[m],
+            device_id={"tensor": here - 1},
+            device_id_type=MESH_ID,
+        )
+
+    def dot_copy(i):
+        return pltpu.make_async_remote_copy(
+            src_ref=dots.at[here],
+            dst_ref=dots.at[here],
+            send_sem=dot_send.at[i],
+            recv_sem=dot_recv.at[i],
+            device_id=peers[i],
+            device_id_type=MESH_ID,
+        )
+
+    def col_copy(i):
+        return pltpu.make_async_remote_copy(
+            src_ref=cols.at[peers[i]["tensor"]],
+            dst_ref=cols.at[size + i],
+            send_sem=col_send.at[i],
+            recv_sem=col_recv.at[i],
+            device_id=peers[i],
+            device_id_type=MESH_ID,
+        )
+
+    def tick(k, _):
+        @pl.when(k < groups)
+        def _():
+            compute(k)
+
+        m = k - here
+        owner = size - 1 - lax.div(m, groups)
+
+        @pl.when((m >= 0) & (owner > here))
+        def _():
+            @pl.when(bottom)
+            def _():
+                up(m, True).start()
+
+            @pl.when(jnp.logical_not(bottom))
+            def _():
+                up(m, False).wait_recv()
+                ups[m] = add_low(ups[m], parts[owner, rows_of(m), :])
+                up(m, False).start()
+
+        n = k - (size - 1 - here)
+        below = lax.div(n, groups)
+
+        @pl.when((n >= 0) & (below < here))
+        def _():
+            @pl.when(top)
+            def _():
+                down(n, True).start()
+
+            @pl.when(jnp.logical_not(top))
+            def _():
+                down(n, False).wait_recv()
+                downs[n] = add_low(downs[n], parts[below, rows_of(n), :])
+                down(n, False).start()
+
+        @pl.when(k == groups)
+        def _():
+            for i in range(size - 1):
+                dot_copy(i).start()
+                col_copy(i).start()
+
+        return 0
+
+    lax.fori_loop(0, max(count, groups + 1), tick, 0)
+
+    for i in range(size - 1):
+        dot_copy(i).wait()
+        col_copy(i).wait()
+    total = dots[0]
+    for j in range(1, size):
+        total = total + dots[j]
+    dot_o[...] = total
+    column = cols[here]
+    for j in range(size - 1):
+        column = column + cols[size + j]
+    gain_o[...] = column
+
+    def last(c, _):
+        part = pl.ds(pl.multiple_of(c * chunk, chunk), chunk)
+        m, n = (size - 1 - here) * groups + c, here * groups + c
+        out_o[part, :] = parts[here, part, :].astype(F32)
+
+        @pl.when(jnp.logical_not(bottom))
+        def _():
+            up(m, False).wait_recv()
+            out_o[part, :] += ups[m].astype(F32)
+
+        @pl.when(jnp.logical_not(top))
+        def _():
+            down(n, False).wait_recv()
+            out_o[part, :] += downs[n].astype(F32)
+
+        return 0
+
+    lax.fori_loop(0, groups, last, 0)
+
+    def drain(m, _):
+        @pl.when(size - 1 - lax.div(m, groups) > here)
+        def _():
+            up(m, False).wait_send()
+
+        @pl.when(lax.div(m, groups) < here)
+        def _():
+            down(m, False).wait_send()
+
+        return 0
+
+    lax.fori_loop(0, count, drain, 0)
+
+
+def input_gradient(size, grads, inv, gain, w_query, w_key, w_value, x, chunk, after):
+    rows, features = x.shape
+    width, groups = features // size, rows // chunk
+    count = (size - 1) * groups
+    anywhere, vmem = pl.BlockSpec(memory_space=pl.ANY), pl.BlockSpec(memory_space=pltpu.VMEM)
+    shape, dma = jax.ShapeDtypeStruct, pltpu.SemaphoreType.DMA
+
+    def kernel(*refs):
+        input_kernel(size, chunk, *refs[:7], *refs[7 + len(after) :])
+
+    return pl.pallas_call(
+        kernel,
+        in_specs=[vmem] * 3 + [anywhere] * (4 + len(after)),
+        out_specs=[vmem] * 3,
+        out_shape=[shape((rows, width), F32), shape((8, rows), F32), shape((8, width), F32)],
+        scratch_shapes=[
+            pltpu.VMEM((size, rows, width), BF),
+            pltpu.VMEM((count, chunk, width), BF),
+            pltpu.VMEM((count, chunk, width), BF),
+            pltpu.VMEM((2, chunk, features), BF),
+            pltpu.VMEM(w_query.shape, BF),
+            pltpu.VMEM(w_key.shape, BF),
+            pltpu.VMEM(w_value.shape, BF),
+            pltpu.VMEM((size, 8, rows), F32),
+            pltpu.VMEM((2 * size - 1, 8, width), F32),
+            dma((count,)),
+            dma((count,)),
+            dma((count,)),
+            dma((count,)),
+            dma((size - 1,)),
+            dma((size - 1,)),
+            dma((size - 1,)),
+            dma((size - 1,)),
+            dma((3,)),
+            dma((2,)),
+        ],
+        compiler_params=pltpu.CompilerParams(
+            collective_id=4, has_side_effects=True, vmem_limit_bytes=VMEM_LIMIT
+        ),
+        cost_estimate=pl.CostEstimate(
+            flops=2 * rows * features * grads.shape[0],
+            bytes_accessed=20 << 20,
+            transcendentals=rows,
+        ),
+        name="input_gradient",
+    )(grads, inv, gain, w_query, w_key, w_value, x, *after)
 
 
 class Line:
@@ -782,16 +1297,6 @@
         for s in range(size - 1):
             slot = lax.rem(here - 1 - s + size, size)
             block = jnp.where(here > s, rising[s], falling[size - 2 - s])
-            full = lax.dynamic_update_slice(full, block, (0, slot * width))
-        return full
-
-    def gather_small(self, own):
-        size, here, width = self.size, self.here, own.shape[1]
-        full = jnp.zeros((own.shape[0], size * width), own.dtype)
-        full = lax.dynamic_update_slice(full, own, (0, here * width))
-        for s in range(1, size):
-            block = lax.ppermute(own, "tensor", [(i, (i + s) % size) for i in range(size)])
-            slot = lax.rem(here - s + size, size)
             full = lax.dynamic_update_slice(full, block, (0, slot * width))
         return full
 
@@ -862,55 +1367,42 @@
     angles = inverse_freq[:, None] * position.astype(F32)[None, :]
     cos_tab, sin_tab = jnp.cos(angles), jnp.sin(angles)
 
-    gains = line.gather_small(jnp.stack([gain_attn, gain_mlp]))
-    gain_a, gain_m = gains[:1], gains[1:]
-
-    x_low = line.gather(layer_input_hidden[0])
-    stream = x_low.astype(F32)
-    square_a = jnp.sum(stream * stream, 1, keepdims=True)
-    inv_a = lax.rsqrt(square_a / features + epsilon)
-    normed_a = (stream * inv_a * gain_a).astype(BF)
-    key_t = rotate(ein("sd,dx->xs", normed_a, w_key).reshape(kvs, HD, rows), cos_tab, sin_tab)
-    value_t = ein("sd,dx->xs", normed_a, w_value).reshape(kvs, HD, rows)
-    mine = jnp.concatenate([key_t, value_t]).astype(BF)
-    if axes["context"] == 2:
-        other = lax.ppermute(mine, "context", [(0, 1), (1, 0)])
-        first = place == 0
-        both = jnp.concatenate(
-            [jnp.where(first, mine, other), jnp.where(first, other, mine)], axis=2
-        )
-    else:
-        both = lax.all_gather(mine, "context", axis=2, tiled=True)
+    x_own = layer_input_hidden[0]
+    gain_own = jnp.concatenate([gain_attn[None], gain_mlp[None], jnp.zeros((6, width), F32)])
+    x_low, normed_a, inv_a, gains, query_t, both = project(
+        axes, x_own, gain_own, cos_tab, sin_tab, w_query, w_key, w_value, GROUP_ROWS
+    )
+    gain_m = gains[1:2]
     kt_all, vt_all = both[:kvs], both[kvs:]
     k_all, v_all = jnp.swapaxes(kt_all, 1, 2), jnp.swapaxes(vt_all, 1, 2)
-    query_t = rotate(
-        ein("sd,dx->xs", normed_a, w_query).reshape(heads, HD, rows), cos_tab, sin_tab
-    ).astype(BF)
-
-    cot = line.gather(jnp.where(square_a[0, 0] >= 0.0, cotangent[0], 0.0))
+    cot = line.gather(jnp.where(inv_a[0, 0] >= 0.0, cotangent[0], 0.0))
 
     mixed, lse = attend_forward(query_t, k_all, vt_all, kend)
     mixed_t = mixed.reshape(heads * HD, rows)
     normed_m, act, gg, gu, down_part, back_part, middle, attn_square = feed_forward(
         line.size, mixed_t, keep, gain_m, w_out, w_gate, w_up, w_down, x_low, cot, GROUP_ROWS, HOP_ROWS
     )
+    grad_down = ein("sf,sd->fd", act, cot).astype(BF)
+    grad_gate = ein("sd,sf->df", normed_m, gg).astype(BF)
+    grad_up = ein("sd,sf->df", normed_m, gu).astype(BF)
     grad_middle, grad_attn, grad_mixed, gain_m_rows = norm_back(
-        line.size, back_part, keep, gain_m, w_out, middle, cot, GROUP_ROWS, HOP_ROWS
+        line.size,
+        back_part,
+        keep,
+        gain_m,
+        w_out,
+        middle,
+        cot,
+        GROUP_ROWS,
+        HOP_ROWS,
+        (grad_down, grad_gate, grad_up),
+    )
+    grad_out = ein("xs,sd->xd", mixed_t, grad_attn).astype(BF)
+    grad_mixed = grad_mixed.reshape(heads, HD, rows)
+    grad_q, grad_k, grad_v = attend_backward(
+        query_t, grad_mixed, mixed, lse, k_all, kt_all, v_all, kend, (grad_out,)
     )
     middle_own, grad_middle_own = own(middle), own(grad_middle)
-    grad_q, grad_k, grad_v = attend_backward(
-        query_t, grad_mixed.reshape(heads, HD, rows), mixed, lse, k_all, kt_all, v_all, kend
-    )
-
-    def shard(grad, dim):
-        return lax.psum_scatter(
-            grad.astype(BF), ("dp", "context"), scatter_dimension=dim, tiled=True
-        ).astype(F32)
-
-    down_sum = shard(ein("sf,sd->fd", act, cot), 1)
-    gate_sum = shard(ein("sd,sf->df", normed_m, gg), 0)
-    up_sum = shard(ein("sd,sf->df", normed_m, gu), 0)
-    out_sum = shard(ein("xs,sd->xd", mixed_t, grad_attn), 1)
 
     ffn_out = line.scatter(down_part, width)
     layer_out = (middle_own + ffn_out).astype(BF)
@@ -928,46 +1420,55 @@
     else:
         dkv_own = lax.psum_scatter(dkv, "context", scatter_dimension=1, tiled=False).astype(F32)
     dkv_t = jnp.swapaxes(dkv_own, 1, 2)
-    grad_query = (
-        rotate(grad_q * SCALE, cos_tab, -sin_tab).astype(BF).reshape(-1, rows)
+    grads = jnp.concatenate(
+        [
+            rotate(grad_q * SCALE, cos_tab, -sin_tab).astype(BF),
+            rotate(dkv_t[:kvs] * SCALE, cos_tab, -sin_tab).astype(BF),
+            dkv_t[kvs:].astype(BF),
+        ]
+    ).reshape(-1, rows)
+
+    def shard(grad, dim):
+        return lax.psum_scatter(grad, ("dp", "context"), scatter_dimension=dim, tiled=True)
+
+    grad_project = ein("sd,xs->dx", normed_a, grads).astype(BF)
+    down_sum = shard(grad_down, 1).astype(F32)
+    gate_sum = shard(grad_gate, 0).astype(F32)
+    up_sum = shard(grad_up, 0).astype(F32)
+    out_sum = shard(grad_out, 1).astype(F32)
+    project_sum = shard(grad_project, 0)
+    cut = [heads * HD, (heads + kvs) * HD]
+    query_sum, key_sum, value_sum = (a.astype(F32) for a in jnp.split(project_sum, cut, 1))
+
+    grad_a, row_dot, gain_a_part = input_gradient(
+        line.size,
+        grads,
+        inv_a,
+        gains,
+        w_query,
+        w_key,
+        w_value,
+        x_low,
+        GROUP_ROWS,
+        (grad_project, ffn_out),
     )
-    grad_key = rotate(dkv_t[:kvs] * SCALE, cos_tab, -sin_tab).astype(BF).reshape(-1, rows)
-    grad_value = dkv_t[kvs:].astype(BF).reshape(-1, rows)
-
-    query_sum = shard(ein("sd,xs->dx", normed_a, grad_query), 0)
-    key_sum = shard(ein("sd,xs->dx", normed_a, grad_key), 0)
-    value_sum = shard(ein("sd,xs->dx", normed_a, grad_value), 0)
-
-    partial_a = (
-        ein("xs,dx->sd", grad_query, w_query)
-        + ein("xs,dx->sd", grad_key, w_key)
-        + ein("xs,dx->sd", grad_value, w_value)
-    )
-    hat_a = x_low.astype(F32) * inv_a
-    row_dot = lax.psum(jnp.sum(partial_a * (hat_a * gain_a), 1), "tensor")[:, None]
-    gain_a_part = jnp.sum(partial_a * hat_a, 0)
-    grad_a = line.scatter(partial_a.astype(BF), width)
-    hat_own = layer_input_hidden[0].astype(F32) * inv_a
-    through = inv_a * (grad_a * gain_attn[None, :] - hat_own * (row_dot / features))
+    hat_own = x_own.astype(F32) * inv_a
+    row_mean = row_dot[0][:, None] / features
+    through = inv_a * (grad_a * gain_attn[None, :] - hat_own * row_mean)
     input_grad = (grad_middle_own + through).astype(BF)
 
-    gain_m_part = lax.dynamic_update_slice(
-        jnp.zeros((1, features), F32), own(gain_m_rows), (0, own_columns)
-    )[0]
     numbers = jnp.stack(
         [
-            jnp.sum(keep * square_a) / line.size,
-            jnp.sum(attn_square) / line.size,
+            jnp.sum(keep * x_own.astype(F32) ** 2),
+            jnp.sum(own(attn_square)),
             jnp.sum(ffn_out * ffn_out),
             jnp.sum(keep) / line.size,
         ]
     )
-    total = lax.psum(
-        jnp.concatenate([gain_a_part, gain_m_part, numbers]), ("dp", "context", "tensor")
+    numbers = lax.psum(numbers, ("dp", "context", "tensor"))
+    gain_a_sum, gain_m_sum = lax.psum(
+        (gain_a_part[0], own(gain_m_rows)[0]), ("dp", "context")
     )
-    gain_a_sum = lax.dynamic_slice_in_dim(total, own_columns, width, 0)
-    gain_m_sum = lax.dynamic_slice_in_dim(total, features + own_columns, width, 0)
-    numbers = total[2 * features :]
     rms = jnp.sqrt(numbers[:3] / (numbers[3] * features))
     return (
         layer_out[None],

time: 1110 us -> 1020 us (0.919)
  Pallas kernels: 366 us -> 533 us
  waiting for transfers between devices: 218 us -> 127 us
  starting transfers between devices: 137 us -> 85.7 us
  matrix products: 108 us -> 57.3 us
  other arithmetic: 104 us -> 62.6 us
    pallas_call x2 -> x4, Pallas kernels: 167 us -> 333 us  [the longest x1 140 us: norm_back(): pl.pallas_call(kernel, in_specs=[vmem] * 3 + [anywhere] * (3 + len(after)...]
    reduce_scatter x5 -> x3, waiting for transfers between devices: 66.4 us -> 4.5 us  [shard(): lax.psum_scatter(grad, ('dp', 'context'), scatter_dimension=dim, tiled=True)]
    dot_general x13 -> x5, matrix products: 108 us -> 57.3 us  [ein(): return jnp.einsum(spec, a, b, preferred_element_type=F32)]
    ppermute x6 -> x3, waiting for transfers between devices: 51.6 us -> 27.4 us  [gather(): b = lax.ppermute(b, 'tensor', self.down)]
    ppermute x6 -> x3, waiting for transfers between devices: 22.5 us -> 0.01 us  [gather(): a = lax.ppermute(a, 'tensor', self.up)]
    ppermute x6 -> x3, starting transfers between devices: 31.9 us -> 11.9 us  [scatter(): a = lax.ppermute(up, 'tensor', self.up)]
    ppermute x6 -> x3, starting transfers between devices: 31.7 us -> 17.3 us  [gather(): a = lax.ppermute(a, 'tensor', self.up)]
    unnamed x98 -> x62, local copies, waits for them, and re-layouts: 30.6 us -> 40.7 us
  transfers between devices with their start and end apart: 36 -> 18, of which waited for: 13 -> 9; matrix products, arithmetic and copies ran while one was open for 21% -> 10% of each run, Pallas kernels for 3% -> 12%
where the time goes in v2:
time: 1020 us; the launch traced here: 1010 us
  Pallas kernels  533 us (52%)
  waiting for transfers between devices  127 us (12%)
  starting transfers between devices  85.7 us (8%)
  blocking collectives  65.2 us (6%)
  local copies, waits for them, and re-layouts  64.4 us (6%)
  other arithmetic  62.6 us (6%)
  matrix products  57.3 us (6%)
  between operations  19.1 us (2%)
    pallas_call x1, Pallas kernels, feed_forward(): pl.pallas_call(functools.partial(ffn_kernel, size, hop, chunk), in_specs=...  168 us
    pallas_call x1, Pallas kernels, norm_back(): pl.pallas_call(kernel, in_specs=[vmem] * 3 + [anywhere] * (3 + len(after)...  140 us
    pallas_call x1, Pallas kernels, project(): pl.pallas_call(functools.partial(project_kernel, size, contexts, chunk),...  103 us
    pallas_call x1, Pallas kernels, input_gradient(): pl.pallas_call(kernel, in_specs=[vmem] * 3 + [anywhere] * (4 + len(after)...  62 us
    dot_general x5, matrix products, ein(): return jnp.einsum(spec, a, b, preferred_element_type=F32)  57.3 us
    ppermute x3, waiting for transfers between devices, scatter(): a = lax.ppermute(up, 'tensor', self.up)  53.2 us
    psum x1, blocking collectives, local(): numbers = lax.psum(numbers, ('dp', 'context', 'tensor'))  49.5 us
    ppermute x1, starting transfers between devices, local(): lax.ppermute(lax.dynamic_index_in_dim(dkv, 1 - place, 1, False), 'context...  48.3 us
  transfers between devices with their start and end apart: 18, of which 9 were waited for; matrix products, arithmetic and copies ran while one was open for 10% of the time, Pallas kernels for 12%

profile of v2, /device:TPU:0, one launch (start us, length us, event | category | flops | bytes accessed | tf_op | source)
XLA Modules:
  0.0 1014.8 jit_solution(6601377072516349241)
XLA Ops:
  14.6 103.0 %project.1 = (bf16[1024,2560]{1,0:T(8,128)(2,1)}, bf16[1024,2560]{1,0:T(8,128)(2,1)}, f32[1024,1]{1,0:T(8,128)}, f32[8,2560]{1,0:T(8,128)}, bf16[8,80,1024]{2,1,0:T(8,128)(2,1)}, /*index=5*/bf16[4,80,2048]{2,1,0:T(8,128)(2,1)}) custom-call(bf16[1024,640]{1,0:T(8,128)(2,1)} %bitcast.65, f32[8,640]{1,0:T(8,128)} %maximum_maximum_fusion.gain_own, ...), custom_call_target="tpu_custom_call" | custom-call | flops 5033164800 | bytes 20971520 | tf_op jit(solution)/shard_map/project/pallas_call | solution.py:986
  141.0 11.7 %collective-permute-done.1 = bf16[1024,640]{1,0:T(8,128)(2,1)} collective-permute-done((bf16[1024,640]{1,0:T(8,128)(2,1)S(1)}, bf16[1024,640]{1,0:T(8,128)(2,1)}, u32[]{:S(2)}, u32[]{:S(2)}) %collective-permute-start.1) | collective-permute-done | bytes 1310752 | tf_op jit(solution)/shard_map/ppermute | solution.py:1294
  165.9 15.7 %collective-permute-done.2 = bf16[1024,640]{1,0:T(8,128)(2,1)} collective-permute-done((bf16[1024,640]{1,0:T(8,128)(2,1)}, bf16[1024,640]{1,0:T(8,128)(2,1)}, u32[]{:S(2)}, u32[]{:S(2)}) %collective-permute-start.2) | collective-permute-done | bytes 1310752 | tf_op jit(solution)/shard_map/ppermute | solution.py:1294
  182.9 6.0 collective-permute-start.5
  190.2 32.4 %attend_fwd.1 = (bf16[8,80,1024]{2,1,0:T(8,128)(2,1)S(1)}, f32[8,1,1024]{2,1,0:T(1,128)S(1)}) custom-call(s32[4,2]{1,0:T(4,128)S(1)} %pad_add_fusion.lim_ref, s32[1,1024]{1,0:T(1,128)S(1)} %fusion.19.kend_ref.refs_1_, bf16[8,80,1024]{2,1,0:T(8,128)(2,1)S(1)} %copy-done.8, bf16[2,2048,80]{2,1,0:T(8,128)(2,1)S(1)} %copy.99.k_ref.refs_6_, ...), custom_call_target="tpu_custom_call" | custom-call | flops 13421772800 | bytes 8388608 | tf_op jit(solution)/shard_map/attend_fwd/pallas_call | solution.py:88
  235.2 167.6 %feed_forward.1 = (bf16[1024,2560]{1,0:T(8,128)(2,1)}, bf16[1024,1792]{1,0:T(8,128)(2,1)}, bf16[1024,1792]{1,0:T(8,128)(2,1)}, bf16[1024,1792]{1,0:T(8,128)(2,1)...) custom-call(bf16[640,1024]{1,0:T(8,128)(2,1)} %bitcast.57, ...), custom_call_target="tpu_custom_call" | custom-call | flops 59726888960 | bytes 83886080 | tf_op jit(solution)/shard_map/feed_forward/pallas_call | solution.py:573
  402.8 15.4 %convolution_convert_fusion.2.refs_6_ = bf16[1792,2560]{1,0:T(8,128)(2,1)} fusion(bf16[1024,1792]{1,0:T(8,128)(2,1)} %get-tuple-element.49, bf16[1024,2560]{1,0:T(8,128)(2,1)} %select_dynamic-update-slice_fusion.cot.refs_5_), kind=kOutput, calls=%fused_computation.2 | convolution fusion | flops 9399828480 | bytes 18087936 | tf_op jit(solution)/shard_map/sf,sd->fd/dot_general | solution.py:37
  418.2 11.9 %convolution_convert_fusion.1.refs_7_ = bf16[2560,1792]{1,0:T(8,128)(2,1)} fusion(bf16[1024,2560]{1,0:T(8,128)(2,1)S(1)} %copy-done.22, bf16[1024,1792]{1,0:T(8,128)(2,1)S(1)} %copy-done.23), kind=kOutput, calls=%fused_computation.1 | convolution fusion | flops 9399828480 | bytes 18087936 | tf_op jit(solution)/shard_map/sd,sf->df/dot_general | solution.py:37
  430.1 15.1 %convolution_convert_fusion.refs_8_ = bf16[2560,1792]{1,0:T(8,128)(2,1)} fusion(bf16[1024,2560]{1,0:T(8,128)(2,1)} %get-tuple-element.50, bf16[1024,1792]{1,0:T(8,128)(2,1)} %get-tuple-element.52), kind=kOutput, calls=%fused_computation | convolution fusion | flops 9399828480 | bytes 18087936 | tf_op jit(solution)/shard_map/sd,sf->df/dot_general | solution.py:37
  445.2 139.7 %norm_back.1 = (f32[1024,2560]{1,0:T(8,128)}, bf16[1024,2560]{1,0:T(8,128)(2,1)}, bf16[640,1024]{1,0:T(8,128)(2,1)}, f32[1,2560]{1,0:T(1,128)}) custom-call(bf16[1024,2560]{1,0:T(8,128)(2,1)} %get-tuple-element.48.refs_0_, f32[1024,1]{1,0:T(8,128)} %fusion.14.keep.refs_1_, f32[1,2560]{1,0:T(1,128)} %slice.68.gain.refs_2_, bf16[640,2560]{1,0:T(8,128)(2,1)} %refs_3_.2, ...), custom_call_target="tpu_custom_call" | custom-call | flops 3355443200 | bytes 41943040 | tf_op jit(solution)/shard_map/norm_back/pallas_call | solution.py:738
  585.0 7.4 convolution_convert_fusion.4.refs_9_
  604.5 28.6 %attend_bwd.1 = (f32[8,80,1024]{2,1,0:T(8,128)S(1)}, f32[2,2048,80]{2,1,0:T(8,128)S(1)}, f32[2,2048,80]{2,1,0:T(8,128)S(1)}) custom-call(s32[4,2]{1,0:T(4,128)S(1)} %pad_add_fusion.1.refs_0_, s32[1,1024]{1,0:T(1,128)S(1)} %fusion.19.kend_ref.refs_1_, bf16[8,80,1024]{2,1,0:T(8,128)(2,1)S(1)} %copy-done.9, bf16[8,80,1024]{2,1,0:T(8,128)(2,1)S(1)} %bitcast.56, ...), custom_call_target="tpu_custom_call" | custom-call | flops 21474836480 | bytes 16777216 | tf_op jit(solution)/shard_map/attend_bwd/pallas_call | solution.py:176
  642.9 48.3 %collective-permute-start.12 = (bf16[4,1024,80]{1,2,0:T(8,128)(2,1)S(1)}, bf16[4,1024,80]{1,2,0:T(8,128)(2,1)S(1)}, u32[]{:S(2)}, u32[]{:S(2)}) collective-permute-start(bf16[4,1024,80]{1,2,0:T(8,128)(2,1)S(1)} %fusion.11), channel_id=1, source_target_pairs={{0,4},{4,0},{1,5},{5,1},{2,6},{6,2},{3,7},{7,3},{8,12},{12,8},{9,1... | collective-permute-start | bytes 1966088 | tf_op jit(solution)/shard_map/ppermute | solution.py:1416
  692.7 7.1 collective-permute-done.12
  700.5 7.5 convolution_convert_fusion.3.refs_7_
  708.1 13.1 %copy.114 = bf16[1792,2560]{0,1:T(8,128)(2,1)} copy(bf16[1792,2560]{1,0:T(8,128)(2,1)} %convolution_convert_fusion.2.refs_6_) | data formatting | bytes 18350080
  728.4 23.8 %collective-permute-done.6 = bf16[1024,640]{1,0:T(8,128)(2,1)S(1)} collective-permute-done((bf16[1024,640]{1,0:T(8,128)(2,1)S(1)}, bf16[1024,640]{1,0:T(8,128)(2,1)S(1)}, u32[]{:S(2)}, u32[]{:S(2)}) %collective-permute-start.6) | collective-permute-done | bytes 1310752 | tf_op jit(solution)/shard_map/ppermute | solution.py:1317
  758.3 28.9 %collective-permute-done.7 = bf16[1024,640]{1,0:T(8,128)(2,1)S(1)} collective-permute-done((bf16[1024,640]{1,0:T(8,128)(2,1)S(1)}, bf16[1024,640]{1,0:T(8,128)(2,1)S(1)}, u32[]{:S(2)}, u32[]{:S(2)}) %collective-permute-start.7) | collective-permute-done | bytes 1310752 | tf_op jit(solution)/shard_map/ppermute | solution.py:1317
  793.1 6.0 collective-permute-start.8
  799.1 12.7 %collective-permute-done.10 = bf16[1024,640]{1,0:T(8,128)(2,1)S(1)} collective-permute-done((bf16[1024,640]{1,0:T(8,128)(2,1)}, bf16[1024,640]{1,0:T(8,128)(2,1)S(1)}, u32[]{:S(2)}, u32[]{:S(2)}) %collective-permute-start.10) | collective-permute-done | bytes 1310752 | tf_op jit(solution)/shard_map/ppermute | solution.py:1318
  821.7 21.0 %collective-permute-done.11 = bf16[1024,640]{1,0:T(8,128)(2,1)} collective-permute-done((bf16[1024,640]{1,0:T(8,128)(2,1)S(1)}, bf16[1024,640]{1,0:T(8,128)(2,1)}, u32[]{:S(2)}, u32[]{:S(2)}) %collective-permute-start.11) | collective-permute-done | bytes 1310752 | tf_op jit(solution)/shard_map/ppermute | solution.py:1318
  847.6 62.0 %input_gradient.1 = (f32[1024,640]{1,0:T(8,128)}, f32[8,1024]{1,0:T(8,128)}, f32[8,640]{1,0:T(8,128)}) custom-call(bf16[960,1024]{1,0:T(8,128)(2,1)} %bitcast.62, f32[1024,1]{1,0:T(8,128)} %get-tuple-element.45.refs_1_, f32[8,2560]{1,0:T(8,128)} %get-tuple-element.43.refs_2_, bf16[2560,640]{1,0:T(8,128)(2,1)} %refs_3_.3, ...), custom_call_target="tpu_custom_call" | custom-call | flops 5033164800 | bytes 20971520 | tf_op jit(solution)/shard_map/input_gradient/pallas_call | solution.py:1241
  918.8 49.5 %psum.23 = f32[4]{0:T(128)S(1)} all-reduce(f32[4]{0:T(128)S(1)} %pad_maximum_fusion.1), channel_id=1, replica_groups=mesh['dp'=4,'context'=2,'tensor'=4] {'dp','context','tensor'}, use_global_device_ids=true, to_apply=%region_14.15 | all-reduce | flops 4 | bytes 32 | tf_op jit(solution)/shard_map/psum | solution.py:1468
  970.2 15.7 %all-reduce = (f32[640]{0:T(1024)}, f32[640]{0:T(1024)}) all-reduce(f32[640]{0:T(1024)S(1)} %slice_reduce_fusion, f32[640]{0:T(1024)S(1)} %fusion.29), channel_id=1, replica_groups=mesh['dp'=4,'context'=2,'tensor'=4] {'dp','context'}, use_global_device_ids=true, to_apply=%region_3.4 | all-reduce | flops 1280 | bytes 10240 | tf_op jit(solution)/shard_map/psum | solution.py:1469
  (158 shorter events, 145.5 us)
Async XLA Ops:
  7.2 812.8 %reduce-scatter.16.cloned.1.call-start = ((), (), s32[]{:S(2)}) async-start(), calls=%async_computation.8 | async-start | bytes 3686400
  122.1 16.5 %copy-start.13 = (bf16[4,80,2048]{2,1,0:T(8,128)(2,1)S(1)}, bf16[4,80,2048]{2,1,0:T(8,128)(2,1)}, u32[]{:S(2)}) copy-start(bf16[4,80,2048]{2,1,0:T(8,128)(2,1)} %get-tuple-element.41) | copy-start | bytes 3932164
  123.6 29.1 %collective-permute-start.1 = (bf16[1024,640]{1,0:T(8,128)(2,1)S(1)}, bf16[1024,640]{1,0:T(8,128)(2,1)}, u32[]{:S(2)}, u32[]{:S(2)}) collective-permute-start(bf16[1024,640]{1,0:T(8,128)(2,1)S(1)} %get-tuple-element.127), channel_id=1, source_target_pairs={{1,0},{2,1},{3,2},{5,4},{6,5},{7,6},{9,8},{10,9},{11,10},{13,12},{... | collective-permute-start | bytes 3932168 | tf_op jit(solution)/shard_map/ppermute | solution.py:1294
  124.9 29.1 %collective-permute-start = (bf16[1024,640]{1,0:T(8,128)(2,1)S(1)}, bf16[1024,640]{1,0:T(8,128)(2,1)}, u32[]{:S(2)}, u32[]{:S(2)}) collective-permute-start(bf16[1024,640]{1,0:T(8,128)(2,1)S(1)} %get-tuple-element.127), channel_id=1, source_target_pairs={{0,1},{1,2},{2,3},{4,5},{5,6},{6,7},{8,9},{9,10},{10,11},{12,13},{... | collective-permute-start | bytes 3932168 | tf_op jit(solution)/shard_map/ppermute | solution.py:1293
  152.7 28.9 %collective-permute-start.2 = (bf16[1024,640]{1,0:T(8,128)(2,1)}, bf16[1024,640]{1,0:T(8,128)(2,1)}, u32[]{:S(2)}, u32[]{:S(2)}) collective-permute-start(bf16[1024,640]{1,0:T(8,128)(2,1)} %collective-permute-done.1), channel_id=1, source_target_pairs={{1,0},{2,1},{3,2},{5,4},{6,5},{7,6},{9,8},{10,9},{11,10},{13,12},{... | collective-permute-start | bytes 3932168 | tf_op jit(solution)/shard_map/ppermute | solution.py:1294
  154.0 28.9 %collective-permute-start.4 = (bf16[1024,640]{1,0:T(8,128)(2,1)}, bf16[1024,640]{1,0:T(8,128)(2,1)}, u32[]{:S(2)}, u32[]{:S(2)}) collective-permute-start(bf16[1024,640]{1,0:T(8,128)(2,1)} %collective-permute-done), channel_id=1, source_target_pairs={{0,1},{1,2},{2,3},{4,5},{5,6},{6,7},{8,9},{9,10},{10,11},{12,13},{... | collective-permute-start | bytes 3932168 | tf_op jit(solution)/shard_map/ppermute | solution.py:1293
  160.5 62.2 %copy-start.2 = (bf16[2,2048,80]{2,1,0:T(8,128)(2,1)}, bf16[2,2048,80]{2,1,0:T(8,128)(2,1)S(1)}, u32[]{:S(2)}) copy-start(bf16[2,2048,80]{2,1,0:T(8,128)(2,1)S(1)} %copy.99.k_ref.refs_6_) | copy-start | bytes 1966084
  181.6 45.2 %collective-permute-start.3 = (bf16[1024,640]{1,0:T(8,128)(2,1)}, bf16[1024,640]{1,0:T(8,128)(2,1)}, u32[]{:S(2)}, u32[]{:S(2)}) collective-permute-start(bf16[1024,640]{1,0:T(8,128)(2,1)} %collective-permute-done.2), channel_id=1, source_target_pairs={{1,0},{2,1},{3,2},{5,4},{6,5},{7,6},{9,8},{10,9},{11,10},{13,12},{... | collective-permute-start | bytes 3932168 | tf_op jit(solution)/shard_map/ppermute | solution.py:1294
  182.9 49.5 %collective-permute-start.5 = (bf16[1024,640]{1,0:T(8,128)(2,1)}, bf16[1024,640]{1,0:T(8,128)(2,1)}, u32[]{:S(2)}, u32[]{:S(2)}) collective-permute-start(bf16[1024,640]{1,0:T(8,128)(2,1)} %collective-permute-done.4), channel_id=1, source_target_pairs={{0,1},{1,2},{2,3},{4,5},{5,6},{6,7},{8,9},{9,10},{10,11},{12,13},{... | collective-permute-start | bytes 3932168 | tf_op jit(solution)/shard_map/ppermute | solution.py:1293
  445.2 139.7 %copy-start.6 = (bf16[8,80,1024]{2,1,0:T(8,128)(2,1)S(1)}, bf16[8,80,1024]{2,1,0:T(8,128)(2,1)}, u32[]{:S(2)}) copy-start(bf16[8,80,1024]{2,1,0:T(8,128)(2,1)} %copy-done.5) | copy-start | bytes 3932164
  598.1 391.5 %reduce-scatter.10.cloned.1.call-start = ((), (), s32[]{:S(2)}) async-start(), calls=%async_computation.5 | async-start | bytes 5898240 | tf_op jit(solution)/shard_map/reduce_scatter | solution.py:1432
  642.9 56.9 %collective-permute-start.12 = (bf16[4,1024,80]{1,2,0:T(8,128)(2,1)S(1)}, bf16[4,1024,80]{1,2,0:T(8,128)(2,1)S(1)}, u32[]{:S(2)}, u32[]{:S(2)}) collective-permute-start(bf16[4,1024,80]{1,2,0:T(8,128)(2,1)S(1)} %fusion.11), channel_id=1, source_target_pairs={{0,4},{4,0},{1,5},{5,1},{2,6},{6,2},{3,7},{7,3},{8,12},{12,8},{9,1... | collective-permute-start | bytes 1966088 | tf_op jit(solution)/shard_map/ppermute | solution.py:1416
  708.0 286.2 %reduce-scatter.18.cloned.1.call-start = ((), (), s32[]{:S(2)}) async-start(), calls=%async_computation.9 | async-start | bytes 10321920
  721.2 276.7 %reduce-scatter.12.cloned.1.call-start = ((), (), s32[]{:S(2)}) async-start(), calls=%async_computation.6 | async-start | bytes 10321920 | tf_op jit(solution)/shard_map/reduce_scatter | solution.py:1432
  721.8 283.4 %reduce-scatter.14.cloned.1.call-start = ((), (), s32[]{:S(2)}) async-start(), calls=%async_computation.7 | async-start | bytes 10321920 | tf_op jit(solution)/shard_map/reduce_scatter | solution.py:1432
  725.7 26.4 %collective-permute-start.6 = (bf16[1024,640]{1,0:T(8,128)(2,1)S(1)}, bf16[1024,640]{1,0:T(8,128)(2,1)S(1)}, u32[]{:S(2)}, u32[]{:S(2)}) collective-permute-start(bf16[1024,640]{1,0:T(8,128)(2,1)S(1)} %get-tuple-element.130), channel_id=1, source_target_pairs={{0,1},{1,2},{2,3},{4,5},{5,6},{6,7},{8,9},{9,10},{10,11},{12,13},{... | collective-permute-start | bytes 3932168 | tf_op jit(solution)/shard_map/ppermute | solution.py:1317
  727.1 31.2 %collective-permute-start.9 = (bf16[1024,640]{1,0:T(8,128)(2,1)}, bf16[1024,640]{1,0:T(8,128)(2,1)}, u32[]{:S(2)}, u32[]{:S(2)}) collective-permute-start(bf16[1024,640]{1,0:T(8,128)(2,1)} %get-tuple-element.131), channel_id=1, source_target_pairs={{1,0},{2,1},{3,2},{5,4},{6,5},{7,6},{9,8},{10,9},{11,10},{13,12},{... | collective-permute-start | bytes 3932168 | tf_op jit(solution)/shard_map/ppermute | solution.py:1318
  753.8 33.4 %collective-permute-start.7 = (bf16[1024,640]{1,0:T(8,128)(2,1)S(1)}, bf16[1024,640]{1,0:T(8,128)(2,1)S(1)}, u32[]{:S(2)}, u32[]{:S(2)}) collective-permute-start(bf16[1024,640]{1,0:T(8,128)(2,1)S(1)} %add_convert_fusion.4), channel_id=1, source_target_pairs={{0,1},{1,2},{2,3},{4,5},{5,6},{6,7},{8,9},{9,10},{10,11},{12,13},{... | collective-permute-start | bytes 3932168 | tf_op jit(solution)/shard_map/ppermute | solution.py:1317
  791.6 23.6 %copy-start.14 = (f32[1024,1]{1,0:T(8,128)S(1)}, f32[1024,1]{1,0:T(8,128)}, u32[]{:S(2)}) copy-start(f32[1024,1]{1,0:T(8,128)} %get-tuple-element.45.refs_1_) | copy-start | bytes 12292
  791.6 20.2 %collective-permute-start.10 = (bf16[1024,640]{1,0:T(8,128)(2,1)}, bf16[1024,640]{1,0:T(8,128)(2,1)S(1)}, u32[]{:S(2)}, u32[]{:S(2)}) collective-permute-start(bf16[1024,640]{1,0:T(8,128)(2,1)} %get-tuple-element.129), channel_id=1, source_target_pairs={{1,0},{2,1},{3,2},{5,4},{6,5},{7,6},{9,8},{10,9},{11,10},{13,12},{... | collective-permute-start | bytes 3932168 | tf_op jit(solution)/shard_map/ppermute | solution.py:1318
  793.1 28.7 %collective-permute-start.8 = (bf16[1024,640]{1,0:T(8,128)(2,1)}, bf16[1024,640]{1,0:T(8,128)(2,1)}, u32[]{:S(2)}, u32[]{:S(2)}) collective-permute-start(bf16[1024,640]{1,0:T(8,128)(2,1)} %get-tuple-element.128), channel_id=1, source_target_pairs={{0,1},{1,2},{2,3},{4,5},{5,6},{6,7},{8,9},{9,10},{10,11},{12,13},{... | collective-permute-start | bytes 3932168 | tf_op jit(solution)/shard_map/ppermute | solution.py:1317
  813.7 29.1 %collective-permute-start.11 = (bf16[1024,640]{1,0:T(8,128)(2,1)S(1)}, bf16[1024,640]{1,0:T(8,128)(2,1)}, u32[]{:S(2)}, u32[]{:S(2)}) collective-permute-start(bf16[1024,640]{1,0:T(8,128)(2,1)S(1)} %add_convert_fusion.1), channel_id=1, source_target_pairs={{1,0},{2,1},{3,2},{5,4},{6,5},{7,6},{9,8},{10,9},{11,10},{13,12},{... | collective-permute-start | bytes 3932168 | tf_op jit(solution)/shard_map/ppermute | solution.py:1318
  847.6 62.8 %copy-start.19 = (f32[640]{0:T(1024)S(1)}, f32[640]{0:T(1024)}, u32[]{:S(2)}) copy-start(f32[640]{0:T(1024)} %param.17) | copy-start | bytes 7684
  910.3 76.2 %copy-start.10 = (f32[1024,640]{1,0:T(8,128)S(1)}, f32[1024,640]{1,0:T(8,128)}, u32[]{:S(2)}) copy-start(f32[1024,640]{1,0:T(8,128)} %get-tuple-element.125.refs_8_) | copy-start | bytes 7864324
  (20 other events, 101.0 us)
Sparse Core Ops, SparseCore 0:
  598.2 65.7 reduce-scatter.15
  708.2 58.6 reduce-scatter.9
  770.9 75.0 reduce-scatter.17
  849.5 75.0 reduce-scatter.11
  928.5 76.6 reduce-scatter.13

commit v3 on v2

--- a/solution.py
+++ b/solution.py
@@ -10,6 +10,7 @@
 
 HD = 80
 PIC = 256
+LEAST_VALID = 1536
 F32 = jnp.float32
 BF = jnp.bfloat16
 SCALE = HD**-0.5
@@ -37,179 +38,6 @@
     return jnp.einsum(spec, a, b, preferred_element_type=F32)
 
 
-def forward_kernel(
-    group, key_rows, lim_ref, kend_ref, q_ref, k_ref, vt_ref, o_ref, lse_ref, acc, mx, sm
-):
-    rows = q_ref.shape[-1]
-    acc[...] = jnp.zeros_like(acc)
-    sm[...] = jnp.zeros_like(sm)
-    mx[...] = jnp.full_like(mx, LOWEST)
-    kend = kend_ref[...]
-
-    def step(masked, i, _):
-        at = pl.multiple_of(i * key_rows, key_rows)
-        k_blk = k_ref[0, pl.ds(at, key_rows), :]
-        v_blk = vt_ref[0, :, pl.ds(at, key_rows)]
-        if masked:
-            keep = (lax.broadcasted_iota(jnp.int32, (key_rows, rows), 0) + at) < kend
-        for h in range(group):
-            s = dot(k_blk, q_ref[h])
-            if masked:
-                s = jnp.where(keep, s, LOWEST)
-            old = mx[h]
-            new = jnp.maximum(old, jnp.max(s, 0, keepdims=True))
-            p = jnp.exp2(s * SCALE2 - new * SCALE2)
-            alpha = jnp.exp2((old - new) * SCALE2)
-            mx[h] = new
-            sm[h] = sm[h] * alpha + jnp.sum(p, 0, keepdims=True)
-            acc[h] = acc[h] * alpha + dot(v_blk, p.astype(BF))
-        return 0
-
-    lax.fori_loop(0, lim_ref[pl.program_id(1), 0], functools.partial(step, False), 0)
-    lax.fori_loop(lim_ref[pl.program_id(1), 0], lim_ref[pl.program_id(1), 1], functools.partial(step, True), 0)
-    for h in range(group):
-        o_ref[h] = (acc[h] / sm[h]).astype(BF)
-        lse_ref[h] = mx[h] * SCALE2 + jnp.log2(sm[h])
-
-
-def key_limits(kend, key_rows):
-    by_group = kend.reshape(-1, GROUP_ROWS)
-    return jnp.stack(
-        [jnp.min(by_group, 1) // key_rows, -(-jnp.max(by_group, 1) // key_rows)], 1
-    ).astype(jnp.int32)
-
-
-def attend_forward(q, k, vt, kend):
-    heads, _, total = q.shape
-    rows = GROUP_ROWS
-    kvs, keys, _ = k.shape
-    group = heads // kvs
-    key_rows = min(KEY_ROWS_FWD, keys)
-    return pl.pallas_call(
-        functools.partial(forward_kernel, group, key_rows),
-        grid=(kvs, total // rows),
-        in_specs=[
-            pl.BlockSpec(memory_space=pltpu.SMEM),
-            pl.BlockSpec((1, rows), lambda g, i: (0, i)),
-            pl.BlockSpec((group, HD, rows), lambda g, i: (g, 0, i)),
-            pl.BlockSpec((1, keys, HD), lambda g, i: (g, 0, 0)),
-            pl.BlockSpec((1, HD, keys), lambda g, i: (g, 0, 0)),
-        ],
-        out_specs=[
-            pl.BlockSpec((group, HD, rows), lambda g, i: (g, 0, i)),
-            pl.BlockSpec((group, 1, rows), lambda g, i: (g, 0, i)),
-        ],
-        out_shape=[
-            jax.ShapeDtypeStruct((heads, HD, total), BF),
-            jax.ShapeDtypeStruct((heads, 1, total), F32),
-        ],
-        scratch_shapes=[
-            pltpu.VMEM((group, HD, rows), F32),
-            pltpu.VMEM((group, 1, rows), F32),
-            pltpu.VMEM((group, 1, rows), F32),
-        ],
-        compiler_params=pltpu.CompilerParams(vmem_limit_bytes=32 << 20),
-        cost_estimate=pl.CostEstimate(
-            flops=10 * heads * total * keys * HD,
-            bytes_accessed=8 << 20,
-            transcendentals=heads * total * keys,
-        ),
-        name="attend_fwd",
-    )(key_limits(kend, key_rows), kend, q, k, vt)
-
-
-def backward_kernel(
-    group, key_rows, lim_ref, kend_ref, q_ref, do_ref, o_ref, lse_ref, k_ref, kt_ref, v_ref,
-    dq_ref, dk_ref, dv_ref, ds_all, p_all, q_all, do_all,
-):
-    @pl.when(pl.program_id(1) == 0)
-    def _():
-        dk_ref[...] = jnp.zeros_like(dk_ref)
-        dv_ref[...] = jnp.zeros_like(dv_ref)
-
-    rows = q_ref.shape[-1]
-    dq_ref[...] = jnp.zeros_like(dq_ref)
-    kend = kend_ref[...]
-    delta = []
-    for h in range(group):
-        q_all[:, h * rows : (h + 1) * rows] = q_ref[h]
-        do_all[:, h * rows : (h + 1) * rows] = do_ref[h]
-        delta.append(jnp.sum(do_ref[h].astype(F32) * o_ref[h].astype(F32), 0, keepdims=True))
-
-    def step(masked, i, _):
-        at = pl.multiple_of(i * key_rows, key_rows)
-        k_blk = k_ref[0, pl.ds(at, key_rows), :]
-        v_blk = v_ref[0, pl.ds(at, key_rows), :]
-        kt_blk = kt_ref[0, :, pl.ds(at, key_rows)]
-        if masked:
-            keep = (lax.broadcasted_iota(jnp.int32, (key_rows, rows), 0) + at) < kend
-        for h in range(group):
-            s = dot(k_blk, q_ref[h])
-            p = jnp.exp2(s * SCALE2 - lse_ref[h])
-            if masked:
-                p = jnp.where(keep, p, 0.0)
-            dp = dot(v_blk, do_ref[h])
-            ds = (p * (dp - delta[h])).astype(BF)
-            p_all[:, h * rows : (h + 1) * rows] = p.astype(BF)
-            ds_all[:, h * rows : (h + 1) * rows] = ds
-            dq_ref[h] += dot(kt_blk, ds)
-        dk_ref[0, pl.ds(at, key_rows), :] += dot_nt(ds_all[...], q_all[...])
-        dv_ref[0, pl.ds(at, key_rows), :] += dot_nt(p_all[...], do_all[...])
-        return 0
-
-    lax.fori_loop(0, lim_ref[pl.program_id(1), 0], functools.partial(step, False), 0)
-    lax.fori_loop(lim_ref[pl.program_id(1), 0], lim_ref[pl.program_id(1), 1], functools.partial(step, True), 0)
-
-
-def attend_backward(q, do, o, lse, k, kt, v, kend, after):
-    heads, _, total = q.shape
-    rows = GROUP_ROWS
-    kvs, keys, _ = k.shape
-    group = heads // kvs
-    key_rows = min(KEY_ROWS_BWD, keys)
-    by_head = pl.BlockSpec((group, HD, rows), lambda g, i: (g, 0, i))
-    by_key = pl.BlockSpec((1, keys, HD), lambda g, i: (g, 0, 0))
-
-    def kernel(*refs):
-        backward_kernel(group, key_rows, *refs[:9], *refs[9 + len(after) :])
-
-    return pl.pallas_call(
-        kernel,
-        grid=(kvs, total // rows),
-        in_specs=[
-            pl.BlockSpec(memory_space=pltpu.SMEM),
-            pl.BlockSpec((1, rows), lambda g, i: (0, i)),
-            by_head,
-            by_head,
-            by_head,
-            pl.BlockSpec((group, 1, rows), lambda g, i: (g, 0, i)),
-            by_key,
-            pl.BlockSpec((1, HD, keys), lambda g, i: (g, 0, 0)),
-            by_key,
-        ]
-        + [pl.BlockSpec(memory_space=pl.ANY)] * len(after),
-        out_specs=[by_head, by_key, by_key],
-        out_shape=[
-            jax.ShapeDtypeStruct((heads, HD, total), F32),
-            jax.ShapeDtypeStruct(k.shape, F32),
-            jax.ShapeDtypeStruct(k.shape, F32),
-        ],
-        scratch_shapes=[
-            pltpu.VMEM((key_rows, group * rows), BF),
-            pltpu.VMEM((key_rows, group * rows), BF),
-            pltpu.VMEM((HD, group * rows), BF),
-            pltpu.VMEM((HD, group * rows), BF),
-        ],
-        compiler_params=pltpu.CompilerParams(vmem_limit_bytes=40 << 20),
-        cost_estimate=pl.CostEstimate(
-            flops=16 * heads * total * keys * HD,
-            bytes_accessed=16 << 20,
-            transcendentals=heads * total * keys,
-        ),
-        name="attend_bwd",
-    )(key_limits(kend, key_rows), kend, q, do, o, lse, k, kt, v, *after)
-
-
 MESH_ID = pl.DeviceIdType.MESH
 RING = 8
 SENT = 4
@@ -361,7 +189,7 @@
     mixed, keep, gain, w_out, w_gate, w_up, w_down, x, cot,
     normed_o, act_o, gg_o, gu_o, ffn_o, back_o, middle_o, square_o,
     low, high, sent, low_send, low_recv, high_send, high_recv,
-    wo, wg, wu, wd, parts, normed, xs, cots, mids, act, gg, gu, ffn, back,
+    wo, wg, wu, wd, parts, normed, xs, cots, mids, act, gg, gu, ffn, back, split,
     w_sem, x_sem, cot_sem, normed_sem, mid_sem, act_sem, ffn_sem,
 ):
     rows, features = x.shape
@@ -408,9 +236,10 @@
         ]
 
     def save_ffn(g):
+        part = pl.ds(g * chunk, chunk)
         return [
-            pltpu.make_async_copy(a, b.at[pl.ds(g * chunk, chunk)], ffn_sem.at[i])
-            for i, (a, b) in enumerate(((ffn, ffn_o), (back, back_o)))
+            pltpu.make_async_copy(split, ffn_o.at[:, part], ffn_sem.at[0]),
+            pltpu.make_async_copy(back, back_o.at[part], ffn_sem.at[1]),
         ]
 
     def project(g):
@@ -549,6 +378,8 @@
         @pl.when(going & (stage == 3))
         def _():
             outer(g, half_d, tiles_d)
+            for j in range(size):
+                split[j] = ffn[:, j * (features // size) : (j + 1) * (features // size)]
             for copy in save_ffn(g):
                 copy.start()
 
@@ -579,7 +410,7 @@
             shape((rows, hidden), BF),
             shape((rows, hidden), BF),
             shape((rows, hidden), BF),
-            shape((rows, features), BF),
+            shape((size, rows, features // size), BF),
             shape((rows, features), BF),
             shape((rows, features), F32),
             shape((1, features), F32),
@@ -600,6 +431,7 @@
             pltpu.VMEM((chunk, hidden), BF),
             pltpu.VMEM((chunk, features), BF),
             pltpu.VMEM((chunk, features), BF),
+            pltpu.VMEM((size, chunk, features // size), BF),
             pltpu.SemaphoreType.DMA((4,)),
             pltpu.SemaphoreType.DMA((2,)),
             pltpu.SemaphoreType.DMA,
@@ -779,93 +611,250 @@
 
 def others(axis, size):
     here = lax.axis_index(axis)
-    return [lax.rem(here + i, size) for i in range(1, size)]
+    return [{axis: lax.rem(here + i, size)} for i in range(1, size)]
+
+
+class Gather:
+    def __init__(self, size, groups, chunk, own, blocks, sems):
+        self.size, self.groups, self.chunk = size, groups, chunk
+        self.own, self.blocks = own, blocks
+        self.up_send, self.up_recv, self.down_send, self.down_recv, self.own_sem = sems
+        self.steps = size - 1
+        self.ticks = groups * self.steps + 1
+        self.here = lax.axis_index("tensor")
+
+    def load(self, g):
+        part = pl.ds(g * self.chunk, self.chunk)
+        return pltpu.make_async_copy(
+            self.own.at[part], self.blocks.at[self.here, part], self.own_sem.at[g]
+        )
+
+    def load_all(self):
+        for g in range(self.groups):
+            self.load(g).start()
+
+    def move(self, g, s, owner, peer, send, recv):
+        block = self.blocks.at[jnp.clip(owner, 0, self.size - 1), pl.ds(g * self.chunk, self.chunk)]
+        return pltpu.make_async_remote_copy(
+            src_ref=block,
+            dst_ref=block,
+            send_sem=send.at[g, s],
+            recv_sem=recv.at[g, s],
+            device_id={"tensor": peer},
+            device_id_type=MESH_ID,
+        )
+
+    def up(self, g, s):
+        return self.move(g, s, self.here - s, self.here + 1, self.up_send, self.up_recv)
+
+    def down(self, g, s):
+        return self.move(g, s, self.here + s, self.here - 1, self.down_send, self.down_recv)
+
+    def each(self, g, s, act):
+        @pl.when((self.here >= s) & (self.here < self.size - 1))
+        def _():
+            act(self.up(g, s))
+
+        @pl.when((self.here + s < self.size) & (self.here > 0))
+        def _():
+            act(self.down(g, s))
+
+    def send(self, g, s):
+        self.each(g, s, lambda copy: copy.start())
+
+    def receive(self, g, s):
+        @pl.when(self.here - 1 - s >= 0)
+        def _():
+            self.up(g, s).wait_recv()
+
+        @pl.when(self.here + 1 + s < self.size)
+        def _():
+            self.down(g, s).wait_recv()
+
+    def begin(self):
+        self.load(0).wait()
+        self.send(0, 0)
+
+    def tick(self, k, then):
+        g, s = lax.div(k, self.steps), lax.rem(k, self.steps)
+
+        @pl.when((s > 0) & (g < self.groups))
+        def _():
+            self.receive(g, s - 1)
+            self.send(g, s)
+
+        @pl.when((s == self.steps - 1) & (g + 1 < self.groups))
+        def _():
+            self.load(g + 1).wait()
+            self.send(g + 1, 0)
+
+        @pl.when((s == 0) & (g > 0) & (g <= self.groups))
+        def _():
+            self.receive(g - 1, self.steps - 1)
+            then(g - 1)
+
+    def drain(self):
+        for g in range(self.groups):
+            for s in range(self.steps):
+                self.each(g, s, lambda copy: copy.wait_send())
+
+
+def gather_scratch(size, rows, width, chunk):
+    dma, groups = pltpu.SemaphoreType.DMA, rows // chunk
+    return [pltpu.VMEM((size, rows, width), BF)] + [dma((groups, size - 1))] * 4 + [dma((groups,))]
+
+
+class Scatter:
+    def __init__(self, size, groups, chunk, parts, ups, downs, sems):
+        self.size, self.groups, self.chunk = size, groups, chunk
+        self.parts, self.ups, self.downs = parts, ups, downs
+        self.up_send, self.up_recv, self.down_send, self.down_recv = sems
+        self.count = (size - 1) * groups
+        self.here = lax.axis_index("tensor")
+
+    def rows(self, m):
+        return pl.ds(pl.multiple_of(lax.rem(m, self.groups) * self.chunk, self.chunk), self.chunk)
+
+    def up(self, m, first):
+        owner = self.size - 1 - lax.div(m, self.groups)
+        return pltpu.make_async_remote_copy(
+            src_ref=self.parts.at[owner, self.rows(m)] if first else self.ups.at[m],
+            dst_ref=self.ups.at[m],
+            send_sem=self.up_send.at[m],
+            recv_sem=self.up_recv.at[m],
+            device_id={"tensor": self.here + 1},
+            device_id_type=MESH_ID,
+        )
+
+    def down(self, m, first):
+        owner = lax.div(m, self.groups)
+        return pltpu.make_async_remote_copy(
+            src_ref=self.parts.at[owner, self.rows(m)] if first else self.downs.at[m],
+            dst_ref=self.downs.at[m],
+            send_sem=self.down_send.at[m],
+            recv_sem=self.down_recv.at[m],
+            device_id={"tensor": self.here - 1},
+            device_id_type=MESH_ID,
+        )
+
+    def tick(self, k):
+        bottom, top = self.here == 0, self.here == self.size - 1
+        m = k - self.here
+        owner = self.size - 1 - lax.div(m, self.groups)
+
+        @pl.when((m >= 0) & (owner > self.here))
+        def _():
+            @pl.when(bottom)
+            def _():
+                self.up(m, True).start()
+
+            @pl.when(jnp.logical_not(bottom))
+            def _():
+                self.up(m, False).wait_recv()
+                self.ups[m] = add_low(self.ups[m], self.parts[owner, self.rows(m), :])
+                self.up(m, False).start()
+
+        n = k - (self.size - 1 - self.here)
+        below = lax.div(n, self.groups)
+
+        @pl.when((n >= 0) & (below < self.here))
+        def _():
+            @pl.when(top)
+            def _():
+                self.down(n, True).start()
+
+            @pl.when(jnp.logical_not(top))
+            def _():
+                self.down(n, False).wait_recv()
+                self.downs[n] = add_low(self.downs[n], self.parts[below, self.rows(n), :])
+                self.down(n, False).start()
+
+    def finish(self, out):
+        here = self.here
+
+        def last(c, _):
+            part = self.rows(c)
+            m, n = (self.size - 1 - here) * self.groups + c, here * self.groups + c
+            out[part, :] = self.parts[here, part, :].astype(F32)
+
+            @pl.when(here > 0)
+            def _():
+                self.up(m, False).wait_recv()
+                out[part, :] += self.ups[m].astype(F32)
+
+            @pl.when(here < self.size - 1)
+            def _():
+                self.down(n, False).wait_recv()
+                out[part, :] += self.downs[n].astype(F32)
+
+            return 0
+
+        lax.fori_loop(0, self.groups, last, 0)
+
+        def drain(m, _):
+            @pl.when(self.size - 1 - lax.div(m, self.groups) > here)
+            def _():
+                self.up(m, False).wait_send()
+
+            @pl.when(lax.div(m, self.groups) < here)
+            def _():
+                self.down(m, False).wait_send()
+
+            return 0
+
+        lax.fori_loop(0, self.count, drain, 0)
+
+
+def scatter_scratch(size, rows, width, chunk):
+    count = (size - 1) * (rows // chunk)
+    return [
+        pltpu.VMEM((size, rows, width), BF),
+        pltpu.VMEM((count, chunk, width), BF),
+        pltpu.VMEM((count, chunk, width), BF),
+    ] + [pltpu.SemaphoreType.DMA((count,))] * 4
+
+
+def turn(u, cos_t, sin_t):
+    lower, upper = u[: HD // 2], u[HD // 2 :]
+    return jnp.concatenate([lower * cos_t - upper * sin_t, upper * cos_t + lower * sin_t], 0)
+
+
+def flip(a):
+    return a.astype(F32).T
+
+
+def key_blocks(g, chunk, rows, keys, key_rows):
+    start = lax.axis_index("context") * rows + g * chunk
+    free = jnp.minimum(start + 1, min(LEAST_VALID, keys))
+    last = jnp.minimum(start + chunk + PIC - 1, keys)
+    return lax.div(free, key_rows), lax.div(last + key_rows - 1, key_rows)
 
 
 def project_kernel(
     size, contexts, chunk,
     own, gain_own, cos_tab, sin_tab, w_query, w_key, w_value,
     x_o, normed_o, inv_o, gain_o, query_o, kv_o,
-    xs, gains, full, normed, kv, wq, wk, wv,
-    up_send, up_recv, down_send, down_recv, gain_send, gain_recv, kv_send, kv_recv,
-    own_sem, w_sem, out_sem, kv_sem,
+    xs, up_send, up_recv, down_send, down_recv, own_sem,
+    gains, full, normed, kv, wq, wk, wv,
+    gain_send, gain_recv, kv_send, kv_recv, w_sem, out_sem, kv_sem,
 ):
     here, place = lax.axis_index("tensor"), lax.axis_index("context")
     rows, width = own.shape
     features = size * width
-    groups, steps = rows // chunk, size - 1
+    groups = rows // chunk
     heads, kvs = w_query.shape[1] // HD, w_key.shape[1] // HD
-    bottom, top = here == 0, here == size - 1
-
+    line = Gather(
+        size, groups, chunk, own, xs, (up_send, up_recv, down_send, down_recv, own_sem)
+    )
     loads = [
         pltpu.make_async_copy(a, b, w_sem.at[i])
         for i, (a, b) in enumerate(((w_query, wq), (w_key, wk), (w_value, wv)))
     ]
-
-    def load_own(g):
-        part = pl.ds(g * chunk, chunk)
-        return pltpu.make_async_copy(own.at[part], xs.at[here, part], own_sem.at[g])
-
-    for g in range(groups):
-        load_own(g).start()
+    line.load_all()
     for load in loads:
         load.start()
     gains[here] = gain_own[...]
-
-    def block(owner, g):
-        return xs.at[owner, pl.ds(g * chunk, chunk)]
-
-    def up(g, s):
-        owner = jnp.clip(here - s, 0, size - 1)
-        return pltpu.make_async_remote_copy(
-            src_ref=block(owner, g),
-            dst_ref=block(owner, g),
-            send_sem=up_send.at[g, s],
-            recv_sem=up_recv.at[g, s],
-            device_id={"tensor": here + 1},
-            device_id_type=MESH_ID,
-        )
-
-    def down(g, s):
-        owner = jnp.clip(here + s, 0, size - 1)
-        return pltpu.make_async_remote_copy(
-            src_ref=block(owner, g),
-            dst_ref=block(owner, g),
-            send_sem=down_send.at[g, s],
-            recv_sem=down_recv.at[g, s],
-            device_id={"tensor": here - 1},
-            device_id_type=MESH_ID,
-        )
-
-    def send(g, s):
-        @pl.when((here >= s) & jnp.logical_not(top))
-        def _():
-            up(g, s).start()
-
-        @pl.when((here + s < size) & jnp.logical_not(bottom))
-        def _():
-            down(g, s).start()
-
-    def sent(g, s):
-        @pl.when((here >= s) & jnp.logical_not(top))
-        def _():
-            up(g, s).wait_send()
-
-        @pl.when((here + s < size) & jnp.logical_not(bottom))
-        def _():
-            down(g, s).wait_send()
-
-    def receive(g, s):
-        @pl.when(here - 1 - s >= 0)
-        def _():
-            up(g, s).wait_recv()
-
-        @pl.when(here + 1 + s < size)
-        def _():
-            down(g, s).wait_recv()
-
-    tensor_peers = [{"tensor": i} for i in others("tensor", size)]
-    context_peers = [{"context": i} for i in others("context", contexts)]
+    tensor_peers, context_peers = others("tensor", size), others("context", contexts)
     greet(tensor_peers + context_peers)
 
     def gain_copy(i):
@@ -889,8 +878,7 @@
             device_id_type=MESH_ID,
         )
 
-    load_own(0).wait()
-    send(0, 0)
+    line.begin()
     for i in range(size - 1):
         gain_copy(i).start()
 
@@ -900,10 +888,6 @@
             pltpu.make_async_copy(full, x_o.at[part], out_sem.at[0]),
             pltpu.make_async_copy(normed, normed_o.at[part], out_sem.at[1]),
         ]
-
-    def turn(u, cos_t, sin_t):
-        lower, upper = u[: HD // 2], u[HD // 2 :]
-        return jnp.concatenate([lower * cos_t - upper * sin_t, upper * cos_t + lower * sin_t], 0)
 
     def compute(g):
         part = pl.ds(pl.multiple_of(g * chunk, chunk), chunk)
@@ -942,33 +926,16 @@
             query_o[h, :, part] = turn(query[h * HD : (h + 1) * HD], cos_t, sin_t).astype(BF)
 
     def tick(k, _):
-        g, s = lax.div(k, steps), lax.rem(k, steps)
-
-        @pl.when(s > 0)
-        def _():
-            receive(g, s - 1)
-            send(g, s)
-
-        @pl.when((s == steps - 1) & (g + 1 < groups))
-        def _():
-            load_own(g + 1).wait()
-            send(g + 1, 0)
-
-        @pl.when((s == 0) & (g > 0))
-        def _():
-            receive(g - 1, steps - 1)
-            compute(g - 1)
-
+        line.tick(k, compute)
         return 0
 
-    lax.fori_loop(0, groups * steps + 1, tick, 0)
+    lax.fori_loop(0, line.ticks, tick, 0)
     for copy in save(groups - 1):
         copy.wait()
     for i in range(size - 1):
         gain_copy(i).wait_send()
+    line.drain()
     for g in range(groups):
-        for s in range(steps):
-            sent(g, s)
         for i in range(contexts - 1):
             kv_copy(g, i).wait()
     out = pltpu.make_async_copy(kv, kv_o, kv_sem)
@@ -976,16 +943,20 @@
     out.wait()
 
 
-def project(axes, own, gain_own, cos_tab, sin_tab, w_query, w_key, w_value, chunk):
+def project(axes, own, gain_own, cos_tab, sin_tab, w_query, w_key, w_value, chunk, after):
     size, contexts = axes["tensor"], axes["context"]
     rows, width = own.shape
     features, groups = size * width, rows // chunk
     heads, kvs = w_query.shape[1] // HD, w_key.shape[1] // HD
     anywhere, vmem = pl.BlockSpec(memory_space=pl.ANY), pl.BlockSpec(memory_space=pltpu.VMEM)
     shape, dma = jax.ShapeDtypeStruct, pltpu.SemaphoreType.DMA
+
+    def kernel(*refs):
+        project_kernel(size, contexts, chunk, *refs[:7], *refs[7 + len(after) :])
+
     return pl.pallas_call(
-        functools.partial(project_kernel, size, contexts, chunk),
-        in_specs=[anywhere] + [vmem] * 3 + [anywhere] * 3,
+        kernel,
+        in_specs=[anywhere] + [vmem] * 3 + [anywhere] * (3 + len(after)),
         out_specs=[anywhere] * 2 + [vmem] * 3 + [anywhere],
         out_shape=[
             shape((rows, features), BF),
@@ -995,8 +966,8 @@
             shape((heads, HD, rows), BF),
             shape((2 * kvs, HD, contexts * rows), BF),
         ],
-        scratch_shapes=[
-            pltpu.VMEM((size, rows, width), BF),
+        scratch_shapes=gather_scratch(size, rows, width, chunk)
+        + [
             pltpu.VMEM((size, 8, width), F32),
             pltpu.VMEM((chunk, features), BF),
             pltpu.VMEM((chunk, features), BF),
@@ -1004,15 +975,10 @@
             pltpu.VMEM(w_query.shape, BF),
             pltpu.VMEM(w_key.shape, BF),
             pltpu.VMEM(w_value.shape, BF),
-            dma((groups, size - 1)),
-            dma((groups, size - 1)),
-            dma((groups, size - 1)),
-            dma((groups, size - 1)),
             dma((size - 1,)),
             dma((size - 1,)),
             dma((groups, max(contexts - 1, 1))),
             dma((groups, max(contexts - 1, 1))),
-            dma((groups,)),
             dma((3,)),
             dma((2,)),
             dma,
@@ -1026,23 +992,310 @@
             transcendentals=rows,
         ),
         name="project",
-    )(own, gain_own, cos_tab, sin_tab, w_query, w_key, w_value)
+    )(own, gain_own, cos_tab, sin_tab, w_query, w_key, w_value, *after)
+
+
+def attend_kernel(
+    size, chunk, key_rows,
+    own, q, kv, kend,
+    cot_o, mixed_o, lse_o,
+    blocks, up_send, up_recv, down_send, down_recv, own_sem,
+    full, keys_in_rows, acc, mx, sm, out_sem,
+):
+    rows, _ = own.shape
+    heads, kvs, keys = q.shape[0], kv.shape[0] // 2, kv.shape[2]
+    groups, group = rows // chunk, heads // kvs
+    units = kvs * groups
+    line = Gather(
+        size, groups, chunk, own, blocks, (up_send, up_recv, down_send, down_recv, own_sem)
+    )
+    line.load_all()
+    greet(others("tensor", size))
+    line.begin()
+    for h in range(kvs):
+        keys_in_rows[h] = flip(kv[h]).astype(BF)
+
+    def save(g):
+        return pltpu.make_async_copy(full, cot_o.at[pl.ds(g * chunk, chunk)], out_sem)
+
+    def join(g):
+        @pl.when(g > 0)
+        def _():
+            save(g - 1).wait()
+
+        part = pl.ds(pl.multiple_of(g * chunk, chunk), chunk)
+        full[...] = jnp.concatenate([blocks[j, part, :] for j in range(size)], 1)
+        save(g).start()
+
+    def unit(u):
+        pair, g = lax.div(u, groups), lax.rem(u, groups)
+        part = pl.ds(pl.multiple_of(g * chunk, chunk), chunk)
+        free, last = key_blocks(g, chunk, rows, keys, key_rows)
+        acc[...] = jnp.zeros_like(acc)
+        sm[...] = jnp.zeros_like(sm)
+        mx[...] = jnp.full_like(mx, LOWEST)
+        limit = kend[:, part]
+
+        def step(masked, i, _):
+            at = pl.multiple_of(i * key_rows, key_rows)
+            k_blk = keys_in_rows[pair, pl.ds(at, key_rows), :]
+            v_blk = kv[kvs + pair, :, pl.ds(at, key_rows)]
+            if masked:
+                keep = (lax.broadcasted_iota(jnp.int32, (key_rows, chunk), 0) + at) < limit
+            for h in range(group):
+                s = dot(k_blk, q[pair * group + h, :, part])
+                if masked:
+                    s = jnp.where(keep, s, LOWEST)
+                old = mx[h]
+                new = jnp.maximum(old, jnp.max(s, 0, keepdims=True))
+                p = jnp.exp2(s * SCALE2 - new * SCALE2)
+                alpha = jnp.exp2((old - new) * SCALE2)
+                mx[h] = new
+                sm[h] = sm[h] * alpha + jnp.sum(p, 0, keepdims=True)
+                acc[h] = acc[h] * alpha + dot(v_blk, p.astype(BF))
+            return 0
+
+        lax.fori_loop(0, free, functools.partial(step, False), 0)
+        lax.fori_loop(free, last, functools.partial(step, True), 0)
+        for h in range(group):
+            mixed_o[pair * group + h, :, part] = (acc[h] / sm[h]).astype(BF)
+            lse_o[pair * group + h, :, part] = mx[h] * SCALE2 + jnp.log2(sm[h])
+
+    def tick(k, _):
+        line.tick(k, join)
+
+        @pl.when(k < units)
+        def _():
+            unit(k)
+
+        return 0
+
+    lax.fori_loop(0, max(line.ticks, units), tick, 0)
+    save(groups - 1).wait()
+    line.drain()
+
+
+def attend_forward(size, own, q, kv, kend, chunk):
+    heads, _, rows = q.shape
+    kvs, keys = kv.shape[0] // 2, kv.shape[2]
+    group, width = heads // kvs, own.shape[1]
+    key_rows = min(KEY_ROWS_FWD, keys)
+    anywhere, vmem = pl.BlockSpec(memory_space=pl.ANY), pl.BlockSpec(memory_space=pltpu.VMEM)
+    shape = jax.ShapeDtypeStruct
+    return pl.pallas_call(
+        functools.partial(attend_kernel, size, chunk, key_rows),
+        in_specs=[anywhere] + [vmem] * 3,
+        out_specs=[anywhere] + [vmem] * 2,
+        out_shape=[
+            shape((rows, size * width), BF),
+            shape((heads, HD, rows), BF),
+            shape((heads, 1, rows), F32),
+        ],
+        scratch_shapes=gather_scratch(size, rows, width, chunk)
+        + [
+            pltpu.VMEM((chunk, size * width), BF),
+            pltpu.VMEM((kvs, keys, HD), BF),
+            pltpu.VMEM((group, HD, chunk), F32),
+            pltpu.VMEM((group, 1, chunk), F32),
+            pltpu.VMEM((group, 1, chunk), F32),
+            pltpu.SemaphoreType.DMA,
+        ],
+        compiler_params=pltpu.CompilerParams(
+            collective_id=5, has_side_effects=True, vmem_limit_bytes=VMEM_LIMIT
+        ),
+        cost_estimate=pl.CostEstimate(
+            flops=10 * heads * rows * keys * HD,
+            bytes_accessed=16 << 20,
+            transcendentals=heads * rows * keys,
+        ),
+        name="attend_forward",
+    )(own, q, kv, kend)
+
+
+def attend_back_kernel(
+    size, contexts, chunk, key_rows,
+    ffn, q, kv, kend, do, o, lse, cos_tab, sin_tab,
+    grads_o, ffn_o,
+    parts, ups, downs, up_send, up_recv, down_send, down_recv,
+    keys_in_rows, values_in_rows, dq, dk, dv, ds_all, p_all, q_all, do_all, mine, out_kv, in_kv,
+    kv_send, kv_recv, part_sem,
+):
+    heads, _, rows = q.shape
+    kvs, keys = kv.shape[0] // 2, kv.shape[2]
+    groups, group = rows // chunk, heads // kvs
+    units = kvs * groups
+    place = lax.axis_index("context")
+    line = Scatter(
+        size, groups, chunk, parts, ups, downs, (up_send, up_recv, down_send, down_recv)
+    )
+    load = pltpu.make_async_copy(ffn, parts, part_sem)
+    load.start()
+    peers = others("context", contexts)
+    greet(others("tensor", size) + peers)
+    for h in range(kvs):
+        keys_in_rows[h] = flip(kv[h]).astype(BF)
+        values_in_rows[h] = flip(kv[kvs + h]).astype(BF)
+    load.wait()
+
+    def half(of):
+        at = pl.ds(pl.multiple_of(of * rows, rows), rows)
+        return dk[at, :].T, dv[at, :].T
+
+    def kv_copy(pair, i):
+        return pltpu.make_async_remote_copy(
+            src_ref=out_kv.at[pair, i],
+            dst_ref=in_kv.at[pair, i],
+            send_sem=kv_send.at[pair, i],
+            recv_sem=kv_recv.at[pair, i],
+            device_id=peers[i],
+            device_id_type=MESH_ID,
+        )
+
+    def unit(u):
+        pair, g = lax.div(u, groups), lax.rem(u, groups)
+        part = pl.ds(pl.multiple_of(g * chunk, chunk), chunk)
+        free, last = key_blocks(g, chunk, rows, keys, key_rows)
+        limit = kend[:, part]
+
+        @pl.when(g == 0)
+        def _():
+            dk[...] = jnp.zeros_like(dk)
+            dv[...] = jnp.zeros_like(dv)
+
+        dq[...] = jnp.zeros_like(dq)
+        delta = []
+        for h in range(group):
+            head = pair * group + h
+            cols = slice(h * chunk, (h + 1) * chunk)
+            q_all[:, cols] = q[head, :, part]
+            do_all[:, cols] = do[head, :, part]
+            delta.append(
+                jnp.sum(do_all[:, cols].astype(F32) * o[head, :, part].astype(F32), 0, keepdims=True)
+            )
+
+        def step(masked, i, _):
+            at = pl.multiple_of(i * key_rows, key_rows)
+            k_blk = keys_in_rows[pair, pl.ds(at, key_rows), :]
+            v_blk = values_in_rows[pair, pl.ds(at, key_rows), :]
+            kt_blk = kv[pair, :, pl.ds(at, key_rows)]
+            if masked:
+                keep = (lax.broadcasted_iota(jnp.int32, (key_rows, chunk), 0) + at) < limit
+            for h in range(group):
+                cols = slice(h * chunk, (h + 1) * chunk)
+                s = dot(k_blk, q_all[:, cols])
+                p = jnp.exp2(s * SCALE2 - lse[pair * group + h, :, part])
+                if masked:
+                    p = jnp.where(keep, p, 0.0)
+                dp = dot(v_blk, do_all[:, cols])
+                ds = (p * (dp - delta[h])).astype(BF)
+                p_all[:, cols] = p.astype(BF)
+                ds_all[:, cols] = ds
+                dq[h] += dot(kt_blk, ds)
+            dk[pl.ds(at, key_rows), :] += dot_nt(ds_all[...], q_all[...])
+            dv[pl.ds(at, key_rows), :] += dot_nt(p_all[...], do_all[...])
+            return 0
+
+        lax.fori_loop(0, free, functools.partial(step, False), 0)
+        lax.fori_loop(free, last, functools.partial(step, True), 0)
+        for h in range(group):
+            grads_o[pair * group + h, :, part] = turn(
+                dq[h] * SCALE, cos_tab[:, part], -sin_tab[:, part]
+            ).astype(BF)
+
+        @pl.when(g == groups - 1)
+        def _():
+            for i in range(contexts - 1):
+                key, value = half(peers[i]["context"])
+                out_kv[pair, i, 0] = key.astype(BF)
+                out_kv[pair, i, 1] = value.astype(BF)
+                kv_copy(pair, i).start()
+            mine[pair, 0], mine[pair, 1] = half(place)
+
+    def tick(k, _):
+        line.tick(k)
+
+        @pl.when(k < units)
+        def _():
+            unit(k)
+
+        return 0
+
+    lax.fori_loop(0, max(line.count, units), tick, 0)
+    for pair in range(kvs):
+        key, value = mine[pair, 0], mine[pair, 1]
+        for i in range(contexts - 1):
+            kv_copy(pair, i).wait()
+            key = key + in_kv[pair, i, 0].astype(F32)
+            value = value + in_kv[pair, i, 1].astype(F32)
+        grads_o[heads + pair] = turn(key * SCALE, cos_tab[...], -sin_tab[...]).astype(BF)
+        grads_o[heads + kvs + pair] = value.astype(BF)
+    line.finish(ffn_o)
+
+
+def attend_backward(axes, ffn, q, kv, kend, do, o, lse, cos_tab, sin_tab, chunk, after):
+    size, contexts = axes["tensor"], axes["context"]
+    heads, _, rows = q.shape
+    kvs, keys = kv.shape[0] // 2, kv.shape[2]
+    group, width = heads // kvs, ffn.shape[2]
+    key_rows = min(KEY_ROWS_BWD, keys)
+    anywhere, vmem = pl.BlockSpec(memory_space=pl.ANY), pl.BlockSpec(memory_space=pltpu.VMEM)
+    shape, dma = jax.ShapeDtypeStruct, pltpu.SemaphoreType.DMA
+    slots = max(contexts - 1, 1)
+
+    def kernel(*refs):
+        attend_back_kernel(size, contexts, chunk, key_rows, *refs[:9], *refs[9 + len(after) :])
+
+    return pl.pallas_call(
+        kernel,
+        in_specs=[anywhere] + [vmem] * 8 + [anywhere] * len(after),
+        out_specs=[vmem] * 2,
+        out_shape=[shape((heads + 2 * kvs, HD, rows), BF), shape((rows, width), F32)],
+        scratch_shapes=scatter_scratch(size, rows, width, chunk)
+        + [
+            pltpu.VMEM((kvs, keys, HD), BF),
+            pltpu.VMEM((kvs, keys, HD), BF),
+            pltpu.VMEM((group, HD, chunk), F32),
+            pltpu.VMEM((keys, HD), F32),
+            pltpu.VMEM((keys, HD), F32),
+            pltpu.VMEM((key_rows, group * chunk), BF),
+            pltpu.VMEM((key_rows, group * chunk), BF),
+            pltpu.VMEM((HD, group * chunk), BF),
+            pltpu.VMEM((HD, group * chunk), BF),
+            pltpu.VMEM((kvs, 2, HD, rows), F32),
+            pltpu.VMEM((kvs, slots, 2, HD, rows), BF),
+            pltpu.VMEM((kvs, slots, 2, HD, rows), BF),
+            dma((kvs, slots)),
+            dma((kvs, slots)),
+            dma,
+        ],
+        compiler_params=pltpu.CompilerParams(
+            collective_id=6, has_side_effects=True, vmem_limit_bytes=VMEM_LIMIT
+        ),
+        cost_estimate=pl.CostEstimate(
+            flops=16 * heads * rows * keys * HD,
+            bytes_accessed=16 << 20,
+            transcendentals=heads * rows * keys,
+        ),
+        name="attend_backward",
+    )(ffn, q, kv, kend, do, o, lse, cos_tab, sin_tab, *after)
 
 
 def input_kernel(
-    size, chunk,
-    grads, inv, gain, w_query, w_key, w_value, x,
-    out_o, dot_o, gain_o,
-    parts, ups, downs, xs, wq, wk, wv, dots, cols,
-    up_send, up_recv, down_send, down_recv, dot_send, dot_recv, col_send, col_recv, w_sem, x_sem,
+    axes, chunk,
+    grads, inv, gain, extra, w_query, w_key, w_value, x,
+    out_o, dot_o, sum_o,
+    parts, ups, downs, up_send, up_recv, down_send, down_recv,
+    xs, wq, wk, wv, dots, cols, cols_in, world,
+    dot_send, dot_recv, col_send, col_recv, world_send, world_recv, w_sem, x_sem,
 ):
+    size = axes["tensor"]
     here = lax.axis_index("tensor")
     rows, features = x.shape
     width, groups = features // size, rows // chunk
-    count = (size - 1) * groups
-    bottom, top = here == 0, here == size - 1
     nq, nk = w_query.shape[1], w_key.shape[1]
-
+    line = Scatter(
+        size, groups, chunk, parts, ups, downs, (up_send, up_recv, down_send, down_recv)
+    )
     loads = [
         pltpu.make_async_copy(a, b, w_sem.at[i])
         for i, (a, b) in enumerate(((w_query, wq), (w_key, wk), (w_value, wv)))
@@ -1055,10 +1308,15 @@
     for load in loads:
         load.start()
     load_x(0).start()
-    peers = [{"tensor": i} for i in others("tensor", size)]
-    greet(peers)
+    contexts, replicas = axes["context"], axes["dp"] * axes["context"]
+    spot = lax.axis_index("dp") * contexts + lax.axis_index("context")
+    peers = others("tensor", size)
+    far = [lax.rem(spot + i, replicas) for i in range(1, replicas)]
+    far = [{"dp": lax.div(i, contexts), "context": lax.rem(i, contexts)} for i in far]
+    greet(peers + far)
     for load in loads:
         load.wait()
+    top_row = lax.broadcasted_iota(jnp.int32, (8, width), 0) == 0
 
     def compute(c):
         slot = lax.rem(c, 2)
@@ -1069,7 +1327,7 @@
         def _():
             load_x(c + 1).start()
 
-        g = grads[:, part].astype(F32).T.astype(BF)
+        g = flip(grads[:, part]).astype(BF)
         whole = (
             dot_nt(g[:, :nq], wq[...])
             + dot_nt(g[:, nq : nq + nk], wk[...])
@@ -1083,184 +1341,109 @@
         low = whole.astype(BF)
         for j in range(size):
             parts[j, part, :] = low[:, j * width : (j + 1) * width]
-            piece = jnp.broadcast_to(colsum[:, j * width : (j + 1) * width], (8, width))
+            piece = jnp.where(top_row, colsum[:, j * width : (j + 1) * width], 0.0)
 
             @pl.when(c == 0)
             def _():
-                cols[j] = piece
+                cols[j] = piece + extra[0]
 
             @pl.when(c > 0)
             def _():
                 cols[j] += piece
 
-    def rows_of(m):
-        return pl.ds(pl.multiple_of(lax.rem(m, groups) * chunk, chunk), chunk)
-
-    def up(m, first):
-        owner = size - 1 - lax.div(m, groups)
+    def copy_to(src, dst, send, recv, peer):
         return pltpu.make_async_remote_copy(
-            src_ref=parts.at[owner, rows_of(m)] if first else ups.at[m],
-            dst_ref=ups.at[m],
-            send_sem=up_send.at[m],
-            recv_sem=up_recv.at[m],
-            device_id={"tensor": here + 1},
+            src_ref=src,
+            dst_ref=dst,
+            send_sem=send,
+            recv_sem=recv,
+            device_id=peer,
             device_id_type=MESH_ID,
         )
 
-    def down(m, first):
-        owner = lax.div(m, groups)
-        return pltpu.make_async_remote_copy(
-            src_ref=parts.at[owner, rows_of(m)] if first else downs.at[m],
-            dst_ref=downs.at[m],
-            send_sem=down_send.at[m],
-            recv_sem=down_recv.at[m],
-            device_id={"tensor": here - 1},
-            device_id_type=MESH_ID,
-        )
-
     def dot_copy(i):
-        return pltpu.make_async_remote_copy(
-            src_ref=dots.at[here],
-            dst_ref=dots.at[here],
-            send_sem=dot_send.at[i],
-            recv_sem=dot_recv.at[i],
-            device_id=peers[i],
-            device_id_type=MESH_ID,
-        )
+        mine = dots.at[here]
+        return copy_to(mine, mine, dot_send.at[i], dot_recv.at[i], peers[i])
 
     def col_copy(i):
-        return pltpu.make_async_remote_copy(
-            src_ref=cols.at[peers[i]["tensor"]],
-            dst_ref=cols.at[size + i],
-            send_sem=col_send.at[i],
-            recv_sem=col_recv.at[i],
-            device_id=peers[i],
-            device_id_type=MESH_ID,
-        )
+        src = cols.at[peers[i]["tensor"]]
+        return copy_to(src, cols_in.at[here], col_send.at[i], col_recv.at[i], peers[i])
+
+    def world_copy(i):
+        mine = world.at[spot]
+        return copy_to(mine, mine, world_send.at[i], world_recv.at[i], far[i])
 
     def tick(k, _):
         @pl.when(k < groups)
         def _():
             compute(k)
 
-        m = k - here
-        owner = size - 1 - lax.div(m, groups)
-
-        @pl.when((m >= 0) & (owner > here))
-        def _():
-            @pl.when(bottom)
-            def _():
-                up(m, True).start()
-
-            @pl.when(jnp.logical_not(bottom))
-            def _():
-                up(m, False).wait_recv()
-                ups[m] = add_low(ups[m], parts[owner, rows_of(m), :])
-                up(m, False).start()
-
-        n = k - (size - 1 - here)
-        below = lax.div(n, groups)
-
-        @pl.when((n >= 0) & (below < here))
-        def _():
-            @pl.when(top)
-            def _():
-                down(n, True).start()
-
-            @pl.when(jnp.logical_not(top))
-            def _():
-                down(n, False).wait_recv()
-                downs[n] = add_low(downs[n], parts[below, rows_of(n), :])
-                down(n, False).start()
+        line.tick(k)
 
         @pl.when(k == groups)
         def _():
+            cols_in[here] = cols[here]
             for i in range(size - 1):
                 dot_copy(i).start()
                 col_copy(i).start()
 
+        @pl.when(k == groups + 3)
+        def _():
+            for i in range(size - 1):
+                dot_copy(i).wait()
+                col_copy(i).wait()
+            total, column = dots[0], cols_in[0]
+            for j in range(1, size):
+                total = total + dots[j]
+                column = column + cols_in[j]
+            dot_o[...] = total
+            world[spot] = column + extra[1]
+            for i in range(replicas - 1):
+                world_copy(i).start()
+
         return 0
 
-    lax.fori_loop(0, max(count, groups + 1), tick, 0)
-
-    for i in range(size - 1):
-        dot_copy(i).wait()
-        col_copy(i).wait()
-    total = dots[0]
-    for j in range(1, size):
-        total = total + dots[j]
-    dot_o[...] = total
-    column = cols[here]
-    for j in range(size - 1):
-        column = column + cols[size + j]
-    gain_o[...] = column
-
-    def last(c, _):
-        part = pl.ds(pl.multiple_of(c * chunk, chunk), chunk)
-        m, n = (size - 1 - here) * groups + c, here * groups + c
-        out_o[part, :] = parts[here, part, :].astype(F32)
-
-        @pl.when(jnp.logical_not(bottom))
-        def _():
-            up(m, False).wait_recv()
-            out_o[part, :] += ups[m].astype(F32)
-
-        @pl.when(jnp.logical_not(top))
-        def _():
-            down(n, False).wait_recv()
-            out_o[part, :] += downs[n].astype(F32)
-
-        return 0
-
-    lax.fori_loop(0, groups, last, 0)
-
-    def drain(m, _):
-        @pl.when(size - 1 - lax.div(m, groups) > here)
-        def _():
-            up(m, False).wait_send()
-
-        @pl.when(lax.div(m, groups) < here)
-        def _():
-            down(m, False).wait_send()
-
-        return 0
-
-    lax.fori_loop(0, count, drain, 0)
-
-
-def input_gradient(size, grads, inv, gain, w_query, w_key, w_value, x, chunk, after):
+    lax.fori_loop(0, max(line.count, groups + 4), tick, 0)
+    line.finish(out_o)
+    for i in range(replicas - 1):
+        world_copy(i).wait()
+    total = world[0]
+    for j in range(1, replicas):
+        total = total + world[j]
+    sum_o[...] = total
+
+
+def input_gradient(axes, grads, inv, gain, extra, w_query, w_key, w_value, x, chunk, after):
+    size, replicas = axes["tensor"], axes["dp"] * axes["context"]
     rows, features = x.shape
-    width, groups = features // size, rows // chunk
-    count = (size - 1) * groups
+    width = features // size
     anywhere, vmem = pl.BlockSpec(memory_space=pl.ANY), pl.BlockSpec(memory_space=pltpu.VMEM)
     shape, dma = jax.ShapeDtypeStruct, pltpu.SemaphoreType.DMA
 
     def kernel(*refs):
-        input_kernel(size, chunk, *refs[:7], *refs[7 + len(after) :])
+        input_kernel(axes, chunk, *refs[:8], *refs[8 + len(after) :])
 
     return pl.pallas_call(
         kernel,
-        in_specs=[vmem] * 3 + [anywhere] * (4 + len(after)),
+        in_specs=[vmem] * 4 + [anywhere] * (4 + len(after)),
         out_specs=[vmem] * 3,
         out_shape=[shape((rows, width), F32), shape((8, rows), F32), shape((8, width), F32)],
-        scratch_shapes=[
-            pltpu.VMEM((size, rows, width), BF),
-            pltpu.VMEM((count, chunk, width), BF),
-            pltpu.VMEM((count, chunk, width), BF),
+        scratch_shapes=scatter_scratch(size, rows, width, chunk)
+        + [
             pltpu.VMEM((2, chunk, features), BF),
             pltpu.VMEM(w_query.shape, BF),
             pltpu.VMEM(w_key.shape, BF),
             pltpu.VMEM(w_value.shape, BF),
             pltpu.VMEM((size, 8, rows), F32),
-            pltpu.VMEM((2 * size - 1, 8, width), F32),
-            dma((count,)),
-            dma((count,)),
-            dma((count,)),
-            dma((count,)),
+            pltpu.VMEM((size, 8, width), F32),
+            pltpu.VMEM((size, 8, width), F32),
+            pltpu.VMEM((replicas, 8, width), F32),
             dma((size - 1,)),
             dma((size - 1,)),
             dma((size - 1,)),
             dma((size - 1,)),
+            dma((replicas - 1,)),
+            dma((replicas - 1,)),
             dma((3,)),
             dma((2,)),
         ],
@@ -1273,56 +1456,7 @@
             transcendentals=rows,
         ),
         name="input_gradient",
-    )(grads, inv, gain, w_query, w_key, w_value, x, *after)
-
-
-class Line:
-    def __init__(self, size):
-        self.size = size
-        self.here = lax.axis_index("tensor")
-        self.up = [(i, i + 1) for i in range(size - 1)]
-        self.down = [(i + 1, i) for i in range(size - 1)]
-
-    def gather(self, own):
-        size, here, width = self.size, self.here, own.shape[1]
-        full = jnp.zeros((own.shape[0], size * width), own.dtype)
-        full = lax.dynamic_update_slice(full, own, (0, here * width))
-        rising, falling = [], []
-        a = b = own
-        for _ in range(size - 1):
-            a = lax.ppermute(a, "tensor", self.up)
-            b = lax.ppermute(b, "tensor", self.down)
-            rising.append(a)
-            falling.append(b)
-        for s in range(size - 1):
-            slot = lax.rem(here - 1 - s + size, size)
-            block = jnp.where(here > s, rising[s], falling[size - 2 - s])
-            full = lax.dynamic_update_slice(full, block, (0, slot * width))
-        return full
-
-    def scatter(self, partial_value, width):
-        size, here = self.size, self.here
-
-        def block(index):
-            start = jnp.clip(index, 0, size - 1) * width
-            return lax.dynamic_slice_in_dim(partial_value, start, width, 1)
-
-        a = b = None
-        for s in range(size - 1):
-            up = block(here + (size - 1 - s))
-            down = block(here - (size - 1 - s))
-            if s:
-                up = (up.astype(F32) + a.astype(F32)).astype(BF)
-                down = (down.astype(F32) + b.astype(F32)).astype(BF)
-            a = lax.ppermute(up, "tensor", self.up)
-            b = lax.ppermute(down, "tensor", self.down)
-        return block(here).astype(F32) + a.astype(F32) + b.astype(F32)
-
-
-def rotate(vectors, cos_tab, sin_tab):
-    lower = vectors[:, : HD // 2]
-    upper = vectors[:, HD // 2 :]
-    return jnp.concatenate([lower * cos_tab - upper * sin_tab, upper * cos_tab + lower * sin_tab], 1)
+    )(grads, inv, gain, extra, w_query, w_key, w_value, x, *after)
 
 
 def local(
@@ -1341,10 +1475,10 @@
     w_up,
     w_down,
 ):
-    line = Line(axes["tensor"])
-    here = line.here
+    here = lax.axis_index("tensor")
     _, rows, width = layer_input_hidden.shape
-    features = width * line.size
+    size = axes["tensor"]
+    features = width * size
     kvs = w_key.shape[1] // HD
     heads = w_query.shape[1] // HD
     place = lax.axis_index("context")
@@ -1370,23 +1504,25 @@
     x_own = layer_input_hidden[0]
     gain_own = jnp.concatenate([gain_attn[None], gain_mlp[None], jnp.zeros((6, width), F32)])
     x_low, normed_a, inv_a, gains, query_t, both = project(
-        axes, x_own, gain_own, cos_tab, sin_tab, w_query, w_key, w_value, GROUP_ROWS
+        axes, x_own, gain_own, cos_tab, sin_tab, w_query, w_key, w_value, GROUP_ROWS, (kend, keep)
     )
     gain_m = gains[1:2]
-    kt_all, vt_all = both[:kvs], both[kvs:]
-    k_all, v_all = jnp.swapaxes(kt_all, 1, 2), jnp.swapaxes(vt_all, 1, 2)
-    cot = line.gather(jnp.where(inv_a[0, 0] >= 0.0, cotangent[0], 0.0))
-
-    mixed, lse = attend_forward(query_t, k_all, vt_all, kend)
+
+    cot, mixed, lse = attend_forward(size, cotangent[0], query_t, both, kend, GROUP_ROWS)
     mixed_t = mixed.reshape(heads * HD, rows)
     normed_m, act, gg, gu, down_part, back_part, middle, attn_square = feed_forward(
-        line.size, mixed_t, keep, gain_m, w_out, w_gate, w_up, w_down, x_low, cot, GROUP_ROWS, HOP_ROWS
+        size, mixed_t, keep, gain_m, w_out, w_gate, w_up, w_down, x_low, cot, GROUP_ROWS, HOP_ROWS
     )
+
+    def shard(grad, dim):
+        return lax.psum_scatter(grad, ("dp", "context"), scatter_dimension=dim, tiled=True)
+
     grad_down = ein("sf,sd->fd", act, cot).astype(BF)
     grad_gate = ein("sd,sf->df", normed_m, gg).astype(BF)
     grad_up = ein("sd,sf->df", normed_m, gu).astype(BF)
+    down_sum, gate_sum, up_sum = shard(grad_down, 1), shard(grad_gate, 0), shard(grad_up, 0)
     grad_middle, grad_attn, grad_mixed, gain_m_rows = norm_back(
-        line.size,
+        size,
         back_part,
         keep,
         gain_m,
@@ -1398,77 +1534,59 @@
         (grad_down, grad_gate, grad_up),
     )
     grad_out = ein("xs,sd->xd", mixed_t, grad_attn).astype(BF)
-    grad_mixed = grad_mixed.reshape(heads, HD, rows)
-    grad_q, grad_k, grad_v = attend_backward(
-        query_t, grad_mixed, mixed, lse, k_all, kt_all, v_all, kend, (grad_out,)
+    out_sum = shard(grad_out, 1)
+    grads, ffn_out = attend_backward(
+        axes,
+        down_part,
+        query_t,
+        both,
+        kend,
+        grad_mixed.reshape(heads, HD, rows),
+        mixed,
+        lse,
+        cos_tab,
+        sin_tab,
+        GROUP_ROWS,
+        (grad_out, down_sum, gate_sum),
     )
-    middle_own, grad_middle_own = own(middle), own(grad_middle)
-
-    ffn_out = line.scatter(down_part, width)
-    layer_out = (middle_own + ffn_out).astype(BF)
-
-    def halves(a):
-        return a.astype(BF).reshape(kvs, axes["context"], rows, HD)
-
-    dkv = jnp.concatenate([halves(grad_k), halves(grad_v)])
-    dkv_own = lax.dynamic_index_in_dim(dkv, place, 1, False).astype(F32)
-    if axes["context"] == 2:
-        sent = lax.ppermute(
-            lax.dynamic_index_in_dim(dkv, 1 - place, 1, False), "context", [(0, 1), (1, 0)]
-        )
-        dkv_own = dkv_own + sent.astype(F32)
-    else:
-        dkv_own = lax.psum_scatter(dkv, "context", scatter_dimension=1, tiled=False).astype(F32)
-    dkv_t = jnp.swapaxes(dkv_own, 1, 2)
-    grads = jnp.concatenate(
+    grads = grads.reshape(-1, rows)
+    grad_project = ein("sd,xs->dx", normed_a, grads).astype(BF)
+    project_sum = shard(grad_project, 0)
+    layer_out = (own(middle) + ffn_out).astype(BF)
+
+    numbers = jnp.stack(
         [
-            rotate(grad_q * SCALE, cos_tab, -sin_tab).astype(BF),
-            rotate(dkv_t[:kvs] * SCALE, cos_tab, -sin_tab).astype(BF),
-            dkv_t[kvs:].astype(BF),
+            jnp.sum(keep * x_own.astype(F32) ** 2),
+            jnp.sum(own(attn_square)),
+            jnp.sum(ffn_out * ffn_out),
+            jnp.sum(keep) / size,
         ]
-    ).reshape(-1, rows)
-
-    def shard(grad, dim):
-        return lax.psum_scatter(grad, ("dp", "context"), scatter_dimension=dim, tiled=True)
-
-    grad_project = ein("sd,xs->dx", normed_a, grads).astype(BF)
-    down_sum = shard(grad_down, 1).astype(F32)
-    gate_sum = shard(grad_gate, 0).astype(F32)
-    up_sum = shard(grad_up, 0).astype(F32)
-    out_sum = shard(grad_out, 1).astype(F32)
-    project_sum = shard(grad_project, 0)
-    cut = [heads * HD, (heads + kvs) * HD]
-    query_sum, key_sum, value_sum = (a.astype(F32) for a in jnp.split(project_sum, cut, 1))
-
-    grad_a, row_dot, gain_a_part = input_gradient(
-        line.size,
+    )
+    numbers = jnp.pad(numbers[None], ((1, 6), (0, width - 4)))
+    extra = jnp.stack([numbers, jnp.pad(own(gain_m_rows), ((2, 5), (0, 0)))])
+    grad_a, row_dot, sums = input_gradient(
+        axes,
         grads,
         inv_a,
         gains,
+        extra,
         w_query,
         w_key,
         w_value,
         x_low,
         GROUP_ROWS,
-        (grad_project, ffn_out),
+        (grad_project, up_sum, out_sum),
     )
     hat_own = x_own.astype(F32) * inv_a
     row_mean = row_dot[0][:, None] / features
     through = inv_a * (grad_a * gain_attn[None, :] - hat_own * row_mean)
-    input_grad = (grad_middle_own + through).astype(BF)
-
-    numbers = jnp.stack(
-        [
-            jnp.sum(keep * x_own.astype(F32) ** 2),
-            jnp.sum(own(attn_square)),
-            jnp.sum(ffn_out * ffn_out),
-            jnp.sum(keep) / line.size,
-        ]
+    input_grad = (own(grad_middle) + through).astype(BF)
+    gain_a_sum, gain_m_sum, numbers = sums[0], sums[2], sums[1, :4]
+    down_sum, gate_sum, up_sum, out_sum, project_sum = (
+        a.astype(F32) for a in (down_sum, gate_sum, up_sum, out_sum, project_sum)
     )
-    numbers = lax.psum(numbers, ("dp", "context", "tensor"))
-    gain_a_sum, gain_m_sum = lax.psum(
-        (gain_a_part[0], own(gain_m_rows)[0]), ("dp", "context")
-    )
+    cut = [heads * HD, (heads + kvs) * HD]
+    query_sum, key_sum, value_sum = jnp.split(project_sum, cut, 1)
     rms = jnp.sqrt(numbers[:3] / (numbers[3] * features))
     return (
         layer_out[None],

time: 1020 us -> 857 us (0.84)
  Pallas kernels: 533 us -> 673 us
  waiting for transfers between devices: 127 us -> 27.7 us
  starting transfers between devices: 85.7 us -> 0.78 us
  blocking collectives: 65.2 us -> 0 us
  other arithmetic: 62.6 us -> 29.6 us
  local copies, waits for them, and re-layouts: 64.4 us -> 39.5 us
    pallas_call x4, Pallas kernels: 226 us -> 366 us  [the longest x1 103 us: project(): pl.pallas_call(kernel, in_specs=[anywhere] + [vmem] * 3 + [anywhere] * (3...]
    ppermute x13 -> x0, waiting for transfers between devices: 121 us -> none  [the longest x3 53.2 us: scatter(): a = lax.ppermute(up, 'tensor', self.up)]
    ppermute x13 -> x0, starting transfers between devices: 85.5 us -> none  [the longest x1 48.3 us: local(): lax.ppermute(lax.dynamic_index_in_dim(dkv, 1 - place, 1, False), 'context...]
    psum x2 -> x0, blocking collectives: 65.2 us -> none  [the longest x1 49.5 us: local(): numbers = lax.psum(numbers, ('dp', 'context', 'tensor'))]
    reduce_scatter x3, waiting for transfers between devices: 4.5 us -> 27.1 us  [shard(): lax.psum_scatter(grad, ('dp', 'context'), scatter_dimension=dim, tiled=True)]
    convert_element_type x7 -> x0, other arithmetic: 17.3 us -> none  [the longest x2 6.08 us: scatter(): up = (up.astype(F32) + a.astype(F32)).astype(BF)]
    unnamed x62 -> x30, local copies, waits for them, and re-layouts: 40.7 us -> 29.4 us
  transfers between devices with their start and end apart: 18 -> 5, of which waited for: 9 -> 1; matrix products, arithmetic and copies ran while one was open for 10% -> 10% of each run, Pallas kernels for 12% -> 37%
where the time goes in v3:
time: 857 us; the launch traced here: 850 us
  Pallas kernels  673 us (79%)
  matrix products  61.5 us (7%)
  local copies, waits for them, and re-layouts  39.5 us (5%)
  other arithmetic  29.6 us (3%)
  waiting for transfers between devices  27.7 us (3%)
  between operations  18.1 us (2%)
    pallas_call x1, Pallas kernels, feed_forward(): pl.pallas_call(functools.partial(ffn_kernel, size, hop, chunk), in_specs=...  168 us
    pallas_call x1, Pallas kernels, norm_back(): pl.pallas_call(kernel, in_specs=[vmem] * 3 + [anywhere] * (3 + len(after)...  138 us
    pallas_call x1, Pallas kernels, project(): pl.pallas_call(kernel, in_specs=[anywhere] + [vmem] * 3 + [anywhere] * (3...  103 us
    pallas_call x1, Pallas kernels, input_gradient(): pl.pallas_call(kernel, in_specs=[vmem] * 4 + [anywhere] * (4 + len(after)...  97.6 us
    pallas_call x1, Pallas kernels, attend_forward(): pl.pallas_call(functools.partial(attend_kernel, size, chunk, key_rows), i...  90.6 us
    pallas_call x1, Pallas kernels, attend_backward(): pl.pallas_call(kernel, in_specs=[anywhere] + [vmem] * 8 + [anywhere] * le...  75 us
    dot_general x5, matrix products, ein(): return jnp.einsum(spec, a, b, preferred_element_type=F32)  61.5 us
    unnamed x30, local copies, waits for them, and re-layouts  29.4 us
  transfers between devices with their start and end apart: 5, of which 1 were waited for; matrix products, arithmetic and copies ran while one was open for 10% of the time, Pallas kernels for 37%

profile of v3, /device:TPU:0, one launch (start us, length us, event | category | flops | bytes accessed | tf_op | source)
XLA Modules:
  0.0 850.0 jit_solution(818651708166440471)
XLA Ops:
  14.0 2.3 copy.45.refs_5_
  16.4 2.3 copy.46.refs_6_
  20.9 2.6 fusion.13.refs_7_.kend.refs_3_
  23.4 103.0 %project.1 = (bf16[1024,2560]{1,0:T(8,128)(2,1)}, bf16[1024,2560]{1,0:T(8,128)(2,1)}, f32[1024,1]{1,0:T(8,128)}, f32[8,2560]{1,0:T(8,128)}, bf16[8,80,1024]{2,1,0:T(8,128)(2,1)}, /*index=5*/bf16[4,80,2048]{2,1,0:T(8,128)(2,1)}) custom-call(bf16[1024,640]{1,0:T(8,128)(2,1)} %bitcast.44, f32[8,640]{1,0:T(8,128)} %maximum_maximum_fusion.refs_1_, ...), custom_call_target="tpu_custom_call" | custom-call | flops 5033164800 | bytes 20971520 | tf_op jit(solution)/shard_map/project/pallas_call | solution.py:957
  127.9 90.6 %attend_forward.1 = (bf16[1024,2560]{1,0:T(8,128)(2,1)}, bf16[8,80,1024]{2,1,0:T(8,128)(2,1)}, f32[8,1,1024]{2,1,0:T(1,128)}) custom-call(bf16[1024,640]{1,0:T(8,128)(2,1)} %bitcast.50, bf16[8,80,1024]{2,1,0:T(8,128)(2,1)} %get-tuple-element.40.q.refs_1_, bf16[4,80,2048]{2,1,0:T(8,128)(2,1)} %get-tuple-element.41.kv.refs_2_, ...), custom_call_target="tpu_custom_call" | custom-call | flops 13421772800 | bytes 16777216 | tf_op jit(solution)/shard_map/attend_forward/pallas_call | solution.py:1085
  218.6 168.1 %feed_forward.1 = (bf16[1024,2560]{1,0:T(8,128)(2,1)}, bf16[1024,1792]{1,0:T(8,128)(2,1)}, bf16[1024,1792]{1,0:T(8,128)(2,1)}, bf16[1024,1792]{1,0:T(8,128)(2,1)...) custom-call(bf16[640,1024]{1,0:T(8,128)(2,1)} %bitcast.52, ...), custom_call_target="tpu_custom_call" | custom-call | flops 59726888960 | bytes 83886080 | tf_op jit(solution)/shard_map/feed_forward/pallas_call | solution.py:404
  386.6 15.1 %convolution_convert_fusion.2.refs_6_ = bf16[1792,2560]{1,0:T(8,128)(2,1)} fusion(bf16[1024,1792]{1,0:T(8,128)(2,1)} %get-tuple-element.49, bf16[1024,2560]{1,0:T(8,128)(2,1)} %get-tuple-element.45.cot.refs_5_), kind=kOutput, calls=%fused_computation.2 | convolution fusion | flops 9399828480 | bytes 18087936 | tf_op jit(solution)/shard_map/sf,sd->fd/dot_general | solution.py:38
  401.7 12.7 %copy.55 = bf16[1792,2560]{0,1:T(8,128)(2,1)} copy(bf16[1792,2560]{1,0:T(8,128)(2,1)} %convolution_convert_fusion.2.refs_6_) | data formatting | bytes 18350080
  415.0 15.3 %convolution_convert_fusion.1.refs_7_ = bf16[2560,1792]{1,0:T(8,128)(2,1)} fusion(bf16[1024,2560]{1,0:T(8,128)(2,1)} %get-tuple-element.50, bf16[1024,1792]{1,0:T(8,128)(2,1)} %get-tuple-element.51), kind=kOutput, calls=%fused_computation.1 | convolution fusion | flops 9399828480 | bytes 18087936 | tf_op jit(solution)/shard_map/sd,sf->df/dot_general | solution.py:38
  430.3 15.0 %convolution_convert_fusion.refs_8_ = bf16[2560,1792]{1,0:T(8,128)(2,1)} fusion(bf16[1024,2560]{1,0:T(8,128)(2,1)} %get-tuple-element.50, bf16[1024,1792]{1,0:T(8,128)(2,1)} %get-tuple-element.52), kind=kOutput, calls=%fused_computation | convolution fusion | flops 9399828480 | bytes 18087936 | tf_op jit(solution)/shard_map/sd,sf->df/dot_general | solution.py:38
  445.3 138.4 %norm_back.1 = (f32[1024,2560]{1,0:T(8,128)}, bf16[1024,2560]{1,0:T(8,128)(2,1)}, bf16[640,1024]{1,0:T(8,128)(2,1)}, f32[1,2560]{1,0:T(1,128)}) custom-call(bf16[1024,2560]{1,0:T(8,128)(2,1)} %get-tuple-element.48.refs_0_, f32[1024,1]{1,0:T(8,128)} %fusion.9.refs_8_.keep.refs_1_, f32[1,2560]{1,0:T(1,128)} %slice.49.gain.refs_2_, bf16[640,2560]{1,0:T(8,128)(2,1)} %refs_3_.1, ...), custom_call_target="tpu_custom_call" | custom-call | flops 3355443200 | bytes 41943040 | tf_op jit(solution)/shard_map/norm_back/pallas_call | solution.py:570
  583.7 6.4 convolution_convert_fusion.4.refs_9_
  590.2 3.7 copy.57
  594.7 2.5 copy.56.refs_10_
  597.2 75.0 %attend_backward.1 = (bf16[12,80,1024]{2,1,0:T(8,128)(2,1)}, f32[1024,640]{1,0:T(8,128)}) custom-call(bf16[4,1024,640]{2,1,0:T(8,128)(2,1)} %get-tuple-element.47.refs_0_, bf16[8,80,1024]{2,1,0:T(8,128)(2,1)} %get-tuple-element.40.q.refs_1_, bf16[4,80,2048]{2,1,0:T(8,128)(2,1)} %get-tuple-element.41.kv.refs_2_, s32[1,1024]{1,0:T(1,128)} %fusion.13.refs_7_.kend.refs_3_, ...), custom_call_target="tpu_custom_call" | custom-call | flops 21474836480 | bytes 16777216 | tf_op jit(solution)/shard_map/attend_backward/pallas_call | solution.py:1248
  672.1 9.7 %convolution_convert_fusion.3.refs_8_ = bf16[2560,960]{1,0:T(8,128)(2,1)} fusion(bf16[1024,2560]{1,0:T(8,128)(2,1)} %get-tuple-element.62, bf16[960,1024]{1,0:T(8,128)(2,1)} %bitcast.45), kind=kOutput, calls=%fused_computation.3 | convolution fusion | flops 5035622400 | bytes 12124160 | tf_op jit(solution)/shard_map/sd,xs->dx/dot_general | solution.py:38
  690.7 1.8 copy.53
  692.5 5.1 multiply_reduce_fusion
  697.6 2.0 maximum_bitcast_fusion
  700.2 27.1 %reduce-scatter.12.cloned.1.call-done.refs_9_ = bf16[320,1792]{1,0:T(8,128)(2,1)} async-done(((bf16[2560,1792]{1,0:T(8,128)(2,1)}), bf16[320,1792]{1,0:T(8,128)(2,1)}) %reduce-scatter.12.cloned.1.call-update) | async-done | bytes 1146896 | tf_op jit(solution)/shard_map/reduce_scatter | solution.py:1518
  727.3 97.6 %input_gradient.1 = (f32[1024,640]{1,0:T(8,128)}, f32[8,1024]{1,0:T(8,128)}, f32[8,640]{1,0:T(8,128)}) custom-call(bf16[960,1024]{1,0:T(8,128)(2,1)} %bitcast.46, f32[1024,1]{1,0:T(8,128)} %get-tuple-element.58.refs_1_, f32[8,2560]{1,0:T(8,128)} %get-tuple-element.43.refs_2_, f32[2,8,640]{2,1,0:T(8,128)} %pad_maximum_fusion.refs_3_, ...), custom_call_target="tpu_custom_call" | custom-call | flops 5033164800 | bytes 20971520 | tf_op jit(solution)/shard_map/input_gradient/pallas_call | solution.py:1426
  828.6 2.8 convert_element_type.78
  834.9 3.6 fusion.8
  841.3 1.9 split.12
  (66 shorter events, 27.2 us)
Async XLA Ops:
  7.2 11.5 %copy-start.7 = (f32[640]{0:T(1024)S(1)}, f32[640]{0:T(1024)}, u32[]{:S(2)}) copy-start(f32[640]{0:T(1024)} %param.17) | copy-start | bytes 7684
  7.2 11.5 %copy-start.9 = (f32[640]{0:T(1024)S(1)}, f32[640]{0:T(1024)}, u32[]{:S(2)}) copy-start(f32[640]{0:T(1024)} %param.22) | copy-start | bytes 7684
  7.2 587.5 %reduce-scatter.16.cloned.1.call-start = ((), (), s32[]{:S(2)}) async-start(), calls=%async_computation.8 | async-start | bytes 10321920
  414.5 182.7 %reduce-scatter.10.cloned.1.call-start = ((), (), s32[]{:S(2)}) async-start(), calls=%async_computation.5 | async-start | bytes 10321920 | tf_op jit(solution)/shard_map/reduce_scatter | solution.py:1518
  430.3 258.0 %reduce-scatter.18.cloned.1.call-start = ((), (), s32[]{:S(2)}) async-start(), calls=%async_computation.9 | async-start | bytes 3686400
  590.1 3.7 copy-start.4
  593.9 133.5 %reduce-scatter.12.cloned.1.call-start = ((), (), s32[]{:S(2)}) async-start(), calls=%async_computation.6 | async-start | bytes 10321920 | tf_op jit(solution)/shard_map/reduce_scatter | solution.py:1518
  594.5 244.0 %reduce-scatter.14.cloned.1.call-start = ((), (), s32[]{:S(2)}) async-start(), calls=%async_computation.7 | async-start | bytes 5898240 | tf_op jit(solution)/shard_map/reduce_scatter | solution.py:1518
  681.8 2.1 copy-start.6
  681.8 4.9 copy-start.1
  681.8 8.8 %copy-start = (bf16[1792,320]{1,0:T(8,128)(2,1)S(1)}, bf16[1792,320]{1,0:T(8,128)(2,1)}, u32[]{:S(2)}) copy-start(bf16[1792,320]{1,0:T(8,128)(2,1)} %copy.56.refs_10_) | copy-start | bytes 3440644
  689.6 8.0 copy-start.3
  727.3 99.7 %copy-start.2 = (bf16[320,1792]{1,0:T(8,128)(2,1)S(1)}, bf16[320,1792]{1,0:T(8,128)(2,1)}, u32[]{:S(2)}) copy-start(bf16[320,1792]{1,0:T(8,128)(2,1)} %reduce-scatter.12.cloned.1.call-done.refs_9_) | copy-start | bytes 3440644
  825.0 9.9 %copy-start.5 = (f32[1024,640]{1,0:T(8,128)S(1)}, f32[1024,640]{1,0:T(8,128)}, u32[]{:S(2)}) copy-start(f32[1024,640]{1,0:T(8,128)} %get-tuple-element.63) | copy-start | bytes 7864324
  825.0 9.9 %copy-start.8 = (f32[640]{0:T(1024)S(1)}, f32[640]{0:T(1024)}, u32[]{:S(2)}) copy-start(f32[640]{0:T(1024)} %param.17) | copy-start | bytes 7684
Sparse Core Ops, SparseCore 0:
  414.6 72.4 reduce-scatter.15
  491.2 75.0 reduce-scatter.9
  594.0 54.9 reduce-scatter.17
  652.5 74.8 reduce-scatter.11
  730.9 57.4 reduce-scatter.13

commit v4 on v3

--- a/solution.py
+++ b/solution.py
@@ -177,6 +177,15 @@
     ]
 
 
+def own_columns(size, a, then):
+    width = a.shape[1] // size
+    for j in range(size):
+
+        @pl.when(lax.axis_index("tensor") == j)
+        def _():
+            then(a[:, j * width : (j + 1) * width])
+
+
 def tile_of(n, most):
     for tile in range(most, 0, -128):
         if n % tile == 0:
@@ -187,10 +196,10 @@
 def ffn_kernel(
     size, hop, chunk,
     mixed, keep, gain, w_out, w_gate, w_up, w_down, x, cot,
-    normed_o, act_o, gg_o, gu_o, ffn_o, back_o, middle_o, square_o,
+    normed_o, act_o, ggu_o, ffn_o, back_o, middle_o, own_o, square_o,
     low, high, sent, low_send, low_recv, high_send, high_recv,
-    wo, wg, wu, wd, parts, normed, xs, cots, mids, act, gg, gu, ffn, back, split,
-    w_sem, x_sem, cot_sem, normed_sem, mid_sem, act_sem, ffn_sem,
+    wo, wg, wu, wd, parts, normed, xs, cots, mids, owns, act, ggu, ffn, back, split,
+    w_sem, x_sem, cot_sem, normed_sem, mid_sem, own_sem, act_sem, ffn_sem,
 ):
     rows, features = x.shape
     hidden = w_gate.shape[1]
@@ -229,10 +238,14 @@
         slot = lax.rem(c, 2)
         return pltpu.make_async_copy(mids.at[slot], middle_o.at[pl.ds(c * hop, hop)], mid_sem.at[slot])
 
+    def save_own(c):
+        slot = lax.rem(c, 2)
+        return pltpu.make_async_copy(owns.at[slot], own_o.at[pl.ds(c * hop, hop)], own_sem.at[slot])
+
     def save_act(g):
         return [
             pltpu.make_async_copy(a, b.at[pl.ds(g * chunk, chunk)], act_sem.at[i])
-            for i, (a, b) in enumerate(((act, act_o), (gg, gg_o), (gu, gu_o)))
+            for i, (a, b) in enumerate(((act, act_o), (ggu, ggu_o)))
         ]
 
     def save_ffn(g):
@@ -273,6 +286,7 @@
         @pl.when(c >= 2)
         def _():
             save_mid(c - 2).wait()
+            save_own(c - 2).wait()
 
         @pl.when(c >= 2 * per)
         def _():
@@ -287,10 +301,12 @@
 
         sums.total(c, then)
         mid = mids[slot]
+        own_columns(size, mid, lambda piece: owns.__setitem__(slot, piece))
+        save_own(c).start()
         inv = lax.rsqrt(jnp.sum(mid * mid, 1, keepdims=True) / features + epsilon)
         at = lax.rem(lax.div(c, per), 2)
         normed[at, pl.ds(pl.multiple_of(lax.rem(c, per) * hop, hop), hop), :] = (
-            mid * inv * gain[...]
+            mid * inv * gain[1:2, :]
         ).astype(BF)
         save_mid(c).start()
         save_normed(c).start()
@@ -307,8 +323,9 @@
             sig = jax.nn.sigmoid(gate)
             silu = gate * sig
             act[:, cols] = (silu * up * kept).astype(BF)
-            gg[:, cols] = (grad * up * (sig + silu * (1.0 - sig))).astype(BF)
-            gu[:, cols] = (grad * silu).astype(BF)
+            ggu[:, cols] = (grad * up * (sig + silu * (1.0 - sig))).astype(BF)
+            cols = pl.ds(pl.multiple_of(hidden + j * tile_f, tile_f), tile_f)
+            ggu[:, cols] = (grad * silu).astype(BF)
             return 0
 
         lax.fori_loop(lo, hi, one, 0)
@@ -317,7 +334,9 @@
         def one(j, _):
             cols = pl.ds(pl.multiple_of(j * tile_d, tile_d), tile_d)
             ffn[:, cols] = dot(act[...], wd[:, cols]).astype(BF)
-            back[:, cols] = (dot_nt(gg[...], wg[cols, :]) + dot_nt(gu[...], wu[cols, :])).astype(BF)
+            back[:, cols] = (
+                dot_nt(ggu[:, :hidden], wg[cols, :]) + dot_nt(ggu[:, hidden:], wu[cols, :])
+            ).astype(BF)
             return 0
 
         lax.fori_loop(lo, hi, one, 0)
@@ -390,6 +409,7 @@
         copy.wait()
     for c in range(count - 2, count):
         save_mid(c).wait()
+        save_own(c).wait()
     for c in range(count - 2 * per, count):
         save_normed(c).wait()
 
@@ -408,11 +428,11 @@
         out_shape=[
             shape((rows, features), BF),
             shape((rows, hidden), BF),
-            shape((rows, hidden), BF),
-            shape((rows, hidden), BF),
+            shape((rows, 2 * hidden), BF),
             shape((size, rows, features // size), BF),
             shape((rows, features), BF),
             shape((rows, features), F32),
+            shape((rows, features // size), F32),
             shape((1, features), F32),
         ],
         scratch_shapes=sum_scratch(hop, features)
@@ -426,9 +446,9 @@
             pltpu.VMEM((2, hop, features), BF),
             pltpu.VMEM((chunk, features), BF),
             pltpu.VMEM((2, hop, features), F32),
+            pltpu.VMEM((2, hop, features // size), F32),
             pltpu.VMEM((chunk, hidden), BF),
-            pltpu.VMEM((chunk, hidden), BF),
-            pltpu.VMEM((chunk, hidden), BF),
+            pltpu.VMEM((chunk, 2 * hidden), BF),
             pltpu.VMEM((chunk, features), BF),
             pltpu.VMEM((chunk, features), BF),
             pltpu.VMEM((size, chunk, features // size), BF),
@@ -437,7 +457,8 @@
             pltpu.SemaphoreType.DMA,
             pltpu.SemaphoreType.DMA((2, per)),
             pltpu.SemaphoreType.DMA((2,)),
-            pltpu.SemaphoreType.DMA((3,)),
+            pltpu.SemaphoreType.DMA((2,)),
+            pltpu.SemaphoreType.DMA((2,)),
             pltpu.SemaphoreType.DMA((2,)),
         ],
         compiler_params=pltpu.CompilerParams(
@@ -454,33 +475,36 @@
 
 def back_kernel(
     size, hop, chunk,
-    parts, keep, gain, w_out, middle, cot,
-    grad_o, grad_low_o, mixed_o, gain_o,
+    parts, keep, gain, w_out, middle, cot, act,
+    own_o, grad_low_o, mixed_o, gain_o, down_o,
     low, high, sent, low_send, low_recv, high_send, high_recv,
-    wo, mids, cots, grads, grads_low,
-    w_sem, mid_sem, cot_sem, grad_sem, grad_low_sem,
+    wo, mids, cots, acts, owns, grads_low, tiles,
+    load_sem, mid_sem, own_sem, grad_low_sem, tile_sem,
 ):
     rows, features = middle.shape
     count, per, groups = rows // hop, chunk // hop, rows // chunk
-    ticks = max(count + size, per * (groups - 1) + size - 1 + per)
+    tile = tile_of(features, 256)
+    tile_count = features // tile
+    ticks = max(count + size, per * (groups - 1) + size - 1 + per, tile_count + 1)
 
     def part(c):
         return parts[pl.ds(pl.multiple_of(c * hop, hop), hop), :]
 
     sums = Sums(size, count, part, low, high, sent, (low_send, low_recv, high_send, high_recv))
-    load_w = pltpu.make_async_copy(w_out, wo, w_sem)
-    load_w.start()
-
-    def load_row(c):
+    loads = [
+        pltpu.make_async_copy(a, b, load_sem.at[i])
+        for i, (a, b) in enumerate(((cot, cots), (w_out, wo), (act, acts)))
+    ]
+
+    def load_mid(c):
         slot = lax.rem(c, 2)
-        return [
-            pltpu.make_async_copy(middle.at[pl.ds(c * hop, hop)], mids.at[slot], mid_sem.at[slot]),
-            pltpu.make_async_copy(cot.at[pl.ds(c * hop, hop)], cots.at[slot], cot_sem.at[slot]),
-        ]
-
-    def save_grad(c):
+        return pltpu.make_async_copy(
+            middle.at[pl.ds(c * hop, hop)], mids.at[slot], mid_sem.at[slot]
+        )
+
+    def save_own(c):
         slot = lax.rem(c, 2)
-        return pltpu.make_async_copy(grads.at[slot], grad_o.at[pl.ds(c * hop, hop)], grad_sem.at[slot])
+        return pltpu.make_async_copy(owns.at[slot], own_o.at[pl.ds(c * hop, hop)], own_sem.at[slot])
 
     def save_low(c):
         q = lax.rem(c, per)
@@ -488,51 +512,75 @@
             grads_low.at[pl.ds(q * hop, hop)], grad_low_o.at[pl.ds(c * hop, hop)], grad_low_sem.at[q]
         )
 
-    for copy in load_row(0):
-        copy.start()
+    def save_tile(j):
+        slot = lax.rem(j, 2)
+        return pltpu.make_async_copy(
+            tiles.at[slot], down_o.at[pl.ds(j * tile, tile)], tile_sem.at[slot]
+        )
+
+    load_mid(0).start()
+    for load in loads:
+        load.start()
     gain_o[...] = jnp.zeros_like(gain_o)
     sums.barrier()
 
     def finish(c):
         slot = lax.rem(c, 2)
-        for copy in load_row(c):
-            copy.wait()
+        load_mid(c).wait()
 
         @pl.when(c + 1 < count)
         def _():
-            for copy in load_row(c + 1):
-                copy.start()
+            load_mid(c + 1).start()
 
         @pl.when(c >= 2)
         def _():
-            save_grad(c - 2).wait()
+            save_own(c - 2).wait()
 
         @pl.when(c >= per)
         def _():
             save_low(c - per).wait()
 
-        kept = keep[pl.ds(pl.multiple_of(c * hop, hop), hop), :]
+        chunk_rows = pl.ds(pl.multiple_of(c * hop, hop), hop)
+        kept = keep[chunk_rows, :]
         mid = mids[slot]
         inv = lax.rsqrt(jnp.sum(mid * mid, 1, keepdims=True) / features + epsilon)
         hat = mid * inv
 
         def then(total):
             gain_o[...] += jnp.sum(total * hat, 0, keepdims=True)
-            weighted = total * gain[...]
+            weighted = total * gain[1:2, :]
             mean = jnp.sum(weighted * hat, 1, keepdims=True) / features
-            grads[slot] = cots[slot].astype(F32) + inv * (weighted - hat * mean)
+            mids[slot] = cots[chunk_rows, :].astype(F32) + inv * (weighted - hat * mean)
 
         sums.total(c, then)
-        grads_low[pl.ds(pl.multiple_of(lax.rem(c, per) * hop, hop), hop), :] = (
-            kept * grads[slot]
-        ).astype(BF)
-        save_grad(c).start()
+        grad = mids[slot]
+        own_columns(size, grad, lambda piece: owns.__setitem__(slot, piece))
+        grads_low[pl.ds(pl.multiple_of(lax.rem(c, per) * hop, hop), hop), :] = (kept * grad).astype(
+            BF
+        )
+        save_own(c).start()
         save_low(c).start()
+
+    def weight_tile(j):
+        slot = lax.rem(j, 2)
+
+        @pl.when(j >= 2)
+        def _():
+            save_tile(j - 2).wait()
+
+        cols = pl.ds(pl.multiple_of(j * tile, tile), tile)
+        tiles[slot] = dot(flip(cots[:, cols]).astype(BF), acts[...]).astype(BF)
+        save_tile(j).start()
 
     def tick(k, _):
         sums.tick(k)
         c = k - (size - 1)
 
+        @pl.when(k == 1)
+        def _():
+            for load in loads:
+                load.wait()
+
         @pl.when((c >= 0) & (c < count))
         def _():
             finish(c)
@@ -540,66 +588,70 @@
             @pl.when(lax.rem(c, per) == per - 1)
             def _():
                 g = lax.div(c, per)
-
-                @pl.when(g == 0)
-                def _():
-                    load_w.wait()
-
                 mixed_o[:, pl.ds(pl.multiple_of(g * chunk, chunk), chunk)] = dot_nt(
                     wo[...], grads_low[...]
                 ).astype(BF)
 
+        @pl.when((k >= 1) & (k <= tile_count))
+        def _():
+            weight_tile(k - 1)
+
         return 0
 
     lax.fori_loop(0, ticks, tick, 0)
     for c in range(count - 2, count):
-        save_grad(c).wait()
+        save_own(c).wait()
     for c in range(count - per, count):
         save_low(c).wait()
-
-
-def norm_back(size, parts, keep, gain, w_out, middle, cot, chunk, hop, after):
+    for j in range(max(tile_count - 2, 0), tile_count):
+        save_tile(j).wait()
+
+
+def norm_back(size, parts, keep, gain, w_out, middle, cot, act, chunk, hop, after):
     rows, features = middle.shape
     per = chunk // hop
     anywhere, vmem = pl.BlockSpec(memory_space=pl.ANY), pl.BlockSpec(memory_space=pltpu.VMEM)
-    shape = jax.ShapeDtypeStruct
+    shape, dma = jax.ShapeDtypeStruct, pltpu.SemaphoreType.DMA
 
     def kernel(*refs):
-        back_kernel(size, hop, chunk, *refs[:6], *refs[6 + len(after) :])
+        back_kernel(size, hop, chunk, *refs[:7], *refs[7 + len(after) :])
 
     return pl.pallas_call(
         kernel,
-        in_specs=[vmem] * 3 + [anywhere] * (3 + len(after)),
-        out_specs=[anywhere] * 2 + [vmem] * 2,
+        in_specs=[vmem] * 3 + [anywhere] * (4 + len(after)),
+        out_specs=[anywhere] * 2 + [vmem] * 2 + [anywhere],
         out_shape=[
-            shape((rows, features), F32),
+            shape((rows, features // size), F32),
             shape((rows, features), BF),
             shape((w_out.shape[0], rows), BF),
             shape((1, features), F32),
+            shape((features, act.shape[1]), BF),
         ],
         scratch_shapes=sum_scratch(hop, features)
         + [
             pltpu.VMEM(w_out.shape, BF),
             pltpu.VMEM((2, hop, features), F32),
-            pltpu.VMEM((2, hop, features), BF),
-            pltpu.VMEM((2, hop, features), F32),
+            pltpu.VMEM(cot.shape, BF),
+            pltpu.VMEM(act.shape, BF),
+            pltpu.VMEM((2, hop, features // size), F32),
             pltpu.VMEM((chunk, features), BF),
-            pltpu.SemaphoreType.DMA,
-            pltpu.SemaphoreType.DMA((2,)),
-            pltpu.SemaphoreType.DMA((2,)),
-            pltpu.SemaphoreType.DMA((2,)),
-            pltpu.SemaphoreType.DMA((per,)),
+            pltpu.VMEM((2, tile_of(features, 256), act.shape[1]), BF),
+            dma((3,)),
+            dma((2,)),
+            dma((2,)),
+            dma((per,)),
+            dma((2,)),
         ],
         compiler_params=pltpu.CompilerParams(
             collective_id=2, has_side_effects=True, vmem_limit_bytes=VMEM_LIMIT
         ),
         cost_estimate=pl.CostEstimate(
-            flops=2 * rows * features * w_out.shape[0],
+            flops=2 * rows * features * (w_out.shape[0] + act.shape[1]),
             bytes_accessed=40 << 20,
             transcendentals=rows,
         ),
         name="norm_back",
-    )(parts, keep, gain, w_out, middle, cot, *after)
+    )(parts, keep, gain, w_out, middle, cot, act, *after)
 
 
 def greet(peers):
@@ -769,24 +821,25 @@
                 self.downs[n] = add_low(self.downs[n], self.parts[below, self.rows(n), :])
                 self.down(n, False).start()
 
-    def finish(self, out):
+    def finish(self, total, then):
         here = self.here
 
         def last(c, _):
             part = self.rows(c)
             m, n = (self.size - 1 - here) * self.groups + c, here * self.groups + c
-            out[part, :] = self.parts[here, part, :].astype(F32)
+            total[...] = self.parts[here, part, :].astype(F32)
 
             @pl.when(here > 0)
             def _():
                 self.up(m, False).wait_recv()
-                out[part, :] += self.ups[m].astype(F32)
+                total[...] += self.ups[m].astype(F32)
 
             @pl.when(here < self.size - 1)
             def _():
                 self.down(n, False).wait_recv()
-                out[part, :] += self.downs[n].astype(F32)
-
+                total[...] += self.downs[n].astype(F32)
+
+            then(part, total[...])
             return 0
 
         lax.fori_loop(0, self.groups, last, 0)
@@ -811,6 +864,7 @@
         pltpu.VMEM((size, rows, width), BF),
         pltpu.VMEM((count, chunk, width), BF),
         pltpu.VMEM((count, chunk, width), BF),
+        pltpu.VMEM((chunk, width), F32),
     ] + [pltpu.SemaphoreType.DMA((count,))] * 4
 
 
@@ -832,8 +886,8 @@
 
 def project_kernel(
     size, contexts, chunk,
-    own, gain_own, cos_tab, sin_tab, w_query, w_key, w_value,
-    x_o, normed_o, inv_o, gain_o, query_o, kv_o,
+    own, gain_attn, gain_mlp, cos_tab, sin_tab, mask, starts, w_query, w_key_t, w_value_t,
+    x_o, normed_o, inv_o, gain_o, query_o, kv_o, kend_o, keep_o,
     xs, up_send, up_recv, down_send, down_recv, own_sem,
     gains, full, normed, kv, wq, wk, wv,
     gain_send, gain_recv, kv_send, kv_recv, w_sem, out_sem, kv_sem,
@@ -842,18 +896,20 @@
     rows, width = own.shape
     features = size * width
     groups = rows // chunk
-    heads, kvs = w_query.shape[1] // HD, w_key.shape[1] // HD
+    heads, kvs = w_query.shape[1] // HD, w_key_t.shape[0] // HD
     line = Gather(
         size, groups, chunk, own, xs, (up_send, up_recv, down_send, down_recv, own_sem)
     )
     loads = [
         pltpu.make_async_copy(a, b, w_sem.at[i])
-        for i, (a, b) in enumerate(((w_query, wq), (w_key, wk), (w_value, wv)))
+        for i, (a, b) in enumerate(((w_query, wq), (w_key_t, wk), (w_value_t, wv)))
     ]
     line.load_all()
     for load in loads:
         load.start()
-    gains[here] = gain_own[...]
+    gains[here] = jnp.zeros_like(gains[here])
+    gains[here, 0:1] = gain_attn[...]
+    gains[here, 1:2] = gain_mlp[...]
     tensor_peers, context_peers = others("tensor", size), others("context", contexts)
     greet(tensor_peers + context_peers)
 
@@ -882,6 +938,17 @@
     for i in range(size - 1):
         gain_copy(i).start()
 
+    length = jnp.sum(mask[...].astype(F32), 1, keepdims=True).astype(jnp.int32)
+    position = lax.broadcasted_iota(jnp.int32, (1, rows), 1) + place * rows
+    last = position
+    for k in range(starts.shape[1]):
+        start = starts[:, k : k + 1]
+        inside = (position >= start) & (position < start + PIC)
+        last = jnp.maximum(last, jnp.where(inside, start + PIC - 1, 0))
+    kend_o[...] = jnp.minimum(last + 1, length)
+    down_rows = lax.broadcasted_iota(jnp.int32, (rows, 1), 0) + place * rows
+    keep_o[...] = jnp.where(down_rows < length, 1.0, 0.0)
+
     def save(g):
         part = pl.ds(g * chunk, chunk)
         return [
@@ -914,8 +981,8 @@
             copy.start()
         cos_t, sin_t = cos_tab[:, part], sin_tab[:, part]
         mine = pl.ds(pl.multiple_of(place * rows + g * chunk, chunk), chunk)
-        key = dot(normed[...], wk[...]).T
-        value = dot(normed[...], wv[...]).T
+        key = dot_nt(wk[...], normed[...])
+        value = dot_nt(wv[...], normed[...])
         for h in range(kvs):
             kv[h, :, mine] = turn(key[h * HD : (h + 1) * HD], cos_t, sin_t).astype(BF)
             kv[kvs + h, :, mine] = value[h * HD : (h + 1) * HD].astype(BF)
@@ -943,21 +1010,19 @@
     out.wait()
 
 
-def project(axes, own, gain_own, cos_tab, sin_tab, w_query, w_key, w_value, chunk, after):
+def project(
+    axes, own, gain_attn, gain_mlp, cos_tab, sin_tab, mask, starts, w_query, w_key_t, w_value_t, chunk
+):
     size, contexts = axes["tensor"], axes["context"]
     rows, width = own.shape
     features, groups = size * width, rows // chunk
-    heads, kvs = w_query.shape[1] // HD, w_key.shape[1] // HD
+    heads, kvs = w_query.shape[1] // HD, w_key_t.shape[0] // HD
     anywhere, vmem = pl.BlockSpec(memory_space=pl.ANY), pl.BlockSpec(memory_space=pltpu.VMEM)
     shape, dma = jax.ShapeDtypeStruct, pltpu.SemaphoreType.DMA
-
-    def kernel(*refs):
-        project_kernel(size, contexts, chunk, *refs[:7], *refs[7 + len(after) :])
-
     return pl.pallas_call(
-        kernel,
-        in_specs=[anywhere] + [vmem] * 3 + [anywhere] * (3 + len(after)),
-        out_specs=[anywhere] * 2 + [vmem] * 3 + [anywhere],
+        functools.partial(project_kernel, size, contexts, chunk),
+        in_specs=[anywhere] + [vmem] * 6 + [anywhere] * 3,
+        out_specs=[anywhere] * 2 + [vmem] * 3 + [anywhere] + [vmem] * 2,
         out_shape=[
             shape((rows, features), BF),
             shape((rows, features), BF),
@@ -965,6 +1030,8 @@
             shape((8, features), F32),
             shape((heads, HD, rows), BF),
             shape((2 * kvs, HD, contexts * rows), BF),
+            shape((1, rows), jnp.int32),
+            shape((rows, 1), F32),
         ],
         scratch_shapes=gather_scratch(size, rows, width, chunk)
         + [
@@ -973,8 +1040,8 @@
             pltpu.VMEM((chunk, features), BF),
             pltpu.VMEM((2 * kvs, HD, contexts * rows), BF),
             pltpu.VMEM(w_query.shape, BF),
-            pltpu.VMEM(w_key.shape, BF),
-            pltpu.VMEM(w_value.shape, BF),
+            pltpu.VMEM(w_key_t.shape, BF),
+            pltpu.VMEM(w_value_t.shape, BF),
             dma((size - 1,)),
             dma((size - 1,)),
             dma((groups, max(contexts - 1, 1))),
@@ -992,7 +1059,7 @@
             transcendentals=rows,
         ),
         name="project",
-    )(own, gain_own, cos_tab, sin_tab, w_query, w_key, w_value, *after)
+    )(own, gain_attn, gain_mlp, cos_tab, sin_tab, mask, starts, w_query, w_key_t, w_value_t)
 
 
 def attend_kernel(
@@ -1114,11 +1181,12 @@
 
 def attend_back_kernel(
     size, contexts, chunk, key_rows,
-    ffn, q, kv, kend, do, o, lse, cos_tab, sin_tab,
-    grads_o, ffn_o,
-    parts, ups, downs, up_send, up_recv, down_send, down_recv,
+    ffn, q, kv, kend, do, o, lse, cos_tab, sin_tab, middle, grad_attn, normed,
+    grads_o, layer_o, square_o, weights_o,
+    parts, ups, downs, total, up_send, up_recv, down_send, down_recv,
     keys_in_rows, values_in_rows, dq, dk, dv, ds_all, p_all, q_all, do_all, mine, out_kv, in_kv,
-    kv_send, kv_recv, part_sem,
+    grads_in, normed_in, tiles,
+    kv_send, kv_recv, part_sem, tile_sem,
 ):
     heads, _, rows = q.shape
     kvs, keys = kv.shape[0] // 2, kv.shape[2]
@@ -1128,14 +1196,19 @@
     line = Scatter(
         size, groups, chunk, parts, ups, downs, (up_send, up_recv, down_send, down_recv)
     )
-    load = pltpu.make_async_copy(ffn, parts, part_sem)
-    load.start()
+    loads = [
+        pltpu.make_async_copy(a, b, part_sem.at[i])
+        for i, (a, b) in enumerate(((ffn, parts), (grad_attn, grads_in), (normed, normed_in)))
+    ]
+    for load in loads:
+        load.start()
+    square_o[...] = jnp.zeros_like(square_o)
     peers = others("context", contexts)
     greet(others("tensor", size) + peers)
     for h in range(kvs):
         keys_in_rows[h] = flip(kv[h]).astype(BF)
         values_in_rows[h] = flip(kv[kvs + h]).astype(BF)
-    load.wait()
+    loads[0].wait()
 
     def half(of):
         at = pl.ds(pl.multiple_of(of * rows, rows), rows)
@@ -1211,6 +1284,41 @@
                 kv_copy(pair, i).start()
             mine[pair, 0], mine[pair, 1] = half(place)
 
+    def join():
+        for pair in range(kvs):
+            key, value = mine[pair, 0], mine[pair, 1]
+            for i in range(contexts - 1):
+                kv_copy(pair, i).wait()
+                key = key + in_kv[pair, i, 0].astype(F32)
+                value = value + in_kv[pair, i, 1].astype(F32)
+            grads_o[heads + pair] = turn(key * SCALE, cos_tab[...], -sin_tab[...]).astype(BF)
+            grads_o[heads + kvs + pair] = value.astype(BF)
+
+    features = normed.shape[1]
+    tile = tile_of(features, 256)
+    tile_count, each = features // tile, 4
+
+    def save_tile(j):
+        slot = lax.rem(j, 2)
+        return pltpu.make_async_copy(
+            tiles.at[slot], weights_o.at[pl.ds(j * tile, tile)], tile_sem.at[slot]
+        )
+
+    def weight_tile(j):
+        slot = lax.rem(j, 2)
+
+        @pl.when(j >= 2)
+        def _():
+            save_tile(j - 2).wait()
+
+        cols = pl.ds(pl.multiple_of(j * tile, tile), tile)
+        out = dot_nt(flip(grads_in[:, cols]).astype(BF), o[...].reshape(heads * HD, rows))
+        into = dot_nt(
+            flip(normed_in[:, cols]).astype(BF), grads_o[...].reshape((heads + 2 * kvs) * HD, rows)
+        )
+        tiles[slot] = jnp.concatenate([out, into], 1).astype(BF)
+        save_tile(j).start()
+
     def tick(k, _):
         line.tick(k)
 
@@ -1218,21 +1326,35 @@
         def _():
             unit(k)
 
+        @pl.when(k == units)
+        def _():
+            join()
+            for load in loads[1:]:
+                load.wait()
+
+        first = (k - units - 1) * each
+        for j in range(each):
+
+            @pl.when((first >= 0) & (first + j < tile_count))
+            def _():
+                weight_tile(first + j)
+
         return 0
 
-    lax.fori_loop(0, max(line.count, units), tick, 0)
-    for pair in range(kvs):
-        key, value = mine[pair, 0], mine[pair, 1]
-        for i in range(contexts - 1):
-            kv_copy(pair, i).wait()
-            key = key + in_kv[pair, i, 0].astype(F32)
-            value = value + in_kv[pair, i, 1].astype(F32)
-        grads_o[heads + pair] = turn(key * SCALE, cos_tab[...], -sin_tab[...]).astype(BF)
-        grads_o[heads + kvs + pair] = value.astype(BF)
-    line.finish(ffn_o)
-
-
-def attend_backward(axes, ffn, q, kv, kend, do, o, lse, cos_tab, sin_tab, chunk, after):
+    lax.fori_loop(0, max(line.count, units + 1 + -(-tile_count // each)), tick, 0)
+
+    def then(part, ffn_out):
+        square_o[...] += jnp.sum(ffn_out * ffn_out, 0, keepdims=True)
+        layer_o[part, :] = (middle[part, :] + ffn_out).astype(BF)
+
+    line.finish(total, then)
+    for j in range(max(tile_count - 2, 0), tile_count):
+        save_tile(j).wait()
+
+
+def attend_backward(
+    axes, ffn, q, kv, kend, do, o, lse, cos_tab, sin_tab, middle, grad_attn, normed, chunk, after
+):
     size, contexts = axes["tensor"], axes["context"]
     heads, _, rows = q.shape
     kvs, keys = kv.shape[0] // 2, kv.shape[2]
@@ -1243,13 +1365,18 @@
     slots = max(contexts - 1, 1)
 
     def kernel(*refs):
-        attend_back_kernel(size, contexts, chunk, key_rows, *refs[:9], *refs[9 + len(after) :])
+        attend_back_kernel(size, contexts, chunk, key_rows, *refs[:12], *refs[12 + len(after) :])
 
     return pl.pallas_call(
         kernel,
-        in_specs=[anywhere] + [vmem] * 8 + [anywhere] * len(after),
-        out_specs=[vmem] * 2,
-        out_shape=[shape((heads + 2 * kvs, HD, rows), BF), shape((rows, width), F32)],
+        in_specs=[anywhere] + [vmem] * 9 + [anywhere] * (2 + len(after)),
+        out_specs=[vmem] * 3 + [anywhere],
+        out_shape=[
+            shape((heads + 2 * kvs, HD, rows), BF),
+            shape((rows, width), BF),
+            shape((1, width), F32),
+            shape((size * width, (2 * heads + 2 * kvs) * HD), BF),
+        ],
         scratch_shapes=scatter_scratch(size, rows, width, chunk)
         + [
             pltpu.VMEM((kvs, keys, HD), BF),
@@ -1264,9 +1391,13 @@
             pltpu.VMEM((kvs, 2, HD, rows), F32),
             pltpu.VMEM((kvs, slots, 2, HD, rows), BF),
             pltpu.VMEM((kvs, slots, 2, HD, rows), BF),
+            pltpu.VMEM(grad_attn.shape, BF),
+            pltpu.VMEM(normed.shape, BF),
+            pltpu.VMEM((2, tile_of(size * width, 256), (2 * heads + 2 * kvs) * HD), BF),
             dma((kvs, slots)),
             dma((kvs, slots)),
-            dma,
+            dma((3,)),
+            dma((2,)),
         ],
         compiler_params=pltpu.CompilerParams(
             collective_id=6, has_side_effects=True, vmem_limit_bytes=VMEM_LIMIT
@@ -1277,28 +1408,32 @@
             transcendentals=heads * rows * keys,
         ),
         name="attend_backward",
-    )(ffn, q, kv, kend, do, o, lse, cos_tab, sin_tab, *after)
+    )(ffn, q, kv, kend, do, o, lse, cos_tab, sin_tab, middle, grad_attn, normed, *after)
 
 
 def input_kernel(
     axes, chunk,
-    grads, inv, gain, extra, w_query, w_key, w_value, x,
-    out_o, dot_o, sum_o,
-    parts, ups, downs, up_send, up_recv, down_send, down_recv,
-    xs, wq, wk, wv, dots, cols, cols_in, world,
-    dot_send, dot_recv, col_send, col_recv, world_send, world_recv, w_sem, x_sem,
+    grads, inv, gain, keep, attn_square, gain_rows, ffn_square, gain_own, x_own, grad_own,
+    w_query, w_key_t, w_value_t, x, ggu_sum, down_sum,
+    out_o, sum_o, gate_o, up_o, down_o,
+    parts, ups, downs, total, up_send, up_recv, down_send, down_recv,
+    xs, wq, wk, wv, dots, dot_sum, cols, cols_in, world, square, ggu, downw, gate_f, up_f, down_f,
+    dot_send, dot_recv, col_send, col_recv, world_send, world_recv, w_sem, x_sem, out_sem,
 ):
     size = axes["tensor"]
     here = lax.axis_index("tensor")
     rows, features = x.shape
     width, groups = features // size, rows // chunk
-    nq, nk = w_query.shape[1], w_key.shape[1]
+    nq, nk = w_query.shape[1], w_key_t.shape[0]
+    hidden = down_sum.shape[1]
     line = Scatter(
         size, groups, chunk, parts, ups, downs, (up_send, up_recv, down_send, down_recv)
     )
     loads = [
         pltpu.make_async_copy(a, b, w_sem.at[i])
-        for i, (a, b) in enumerate(((w_query, wq), (w_key, wk), (w_value, wv)))
+        for i, (a, b) in enumerate(
+            ((w_query, wq), (w_key_t, wk), (w_value_t, wv), (ggu_sum, ggu), (down_sum, downw))
+        )
     ]
 
     def load_x(c):
@@ -1314,9 +1449,11 @@
     far = [lax.rem(spot + i, replicas) for i in range(1, replicas)]
     far = [{"dp": lax.div(i, contexts), "context": lax.rem(i, contexts)} for i in far]
     greet(peers + far)
-    for load in loads:
+    for load in loads[:3]:
         load.wait()
-    top_row = lax.broadcasted_iota(jnp.int32, (8, width), 0) == 0
+    square[...] = jnp.zeros_like(square)
+    row = lax.broadcasted_iota(jnp.int32, (8, width), 0)
+    lane = lax.broadcasted_iota(jnp.int32, (8, width), 1)
 
     def compute(c):
         slot = lax.rem(c, 2)
@@ -1330,22 +1467,23 @@
         g = flip(grads[:, part]).astype(BF)
         whole = (
             dot_nt(g[:, :nq], wq[...])
-            + dot_nt(g[:, nq : nq + nk], wk[...])
-            + dot_nt(g[:, nq + nk :], wv[...])
-        )
-        hat = xs[slot].astype(F32) * inv[part, :]
-        moved = whole * hat
+            + dot(g[:, nq : nq + nk], wk[...])
+            + dot(g[:, nq + nk :], wv[...])
+        )
+        stream = xs[slot].astype(F32)
+        square[...] += jnp.sum(stream * stream * keep[part, :], 0, keepdims=True)
+        moved = whole * (stream * inv[part, :])
         rowsum = jnp.sum(moved * gain[0:1, :], 1, keepdims=True)
         dots[here, :, part] = jnp.broadcast_to(rowsum, (chunk, 128)).T[:8]
         colsum = jnp.sum(moved, 0, keepdims=True)
         low = whole.astype(BF)
         for j in range(size):
             parts[j, part, :] = low[:, j * width : (j + 1) * width]
-            piece = jnp.where(top_row, colsum[:, j * width : (j + 1) * width], 0.0)
+            piece = jnp.where(row == 0, colsum[:, j * width : (j + 1) * width], 0.0)
 
             @pl.when(c == 0)
             def _():
-                cols[j] = piece + extra[0]
+                cols[j] = piece
 
             @pl.when(c > 0)
             def _():
@@ -1373,6 +1511,42 @@
         mine = world.at[spot]
         return copy_to(mine, mine, world_send.at[i], world_recv.at[i], far[i])
 
+    saves = [
+        pltpu.make_async_copy(a, b, out_sem.at[i])
+        for i, (a, b) in enumerate(((gate_f, gate_o), (up_f, up_o), (down_f, down_o)))
+    ]
+
+    def exchange():
+        numbers = jnp.zeros((8, width), F32)
+        for i, a in enumerate((square[...], attn_square[...], ffn_square[...], keep[...])):
+            a = jnp.sum(jnp.sum(a, 0, keepdims=True), 1, keepdims=True)
+            share = 1.0 if i == 2 else 1.0 / size
+            numbers += jnp.where((row == 1) & (lane == i), a * share, 0.0)
+        for j in range(size):
+            cols[j] += numbers
+        cols_in[here] = cols[here]
+        for i in range(size - 1):
+            dot_copy(i).start()
+            col_copy(i).start()
+
+    def spread():
+        for i in range(size - 1):
+            dot_copy(i).wait()
+            col_copy(i).wait()
+        dot_total, column = dots[0], cols_in[0]
+        for j in range(1, size):
+            dot_total = dot_total + dots[j]
+            column = column + cols_in[j]
+        dot_sum[...] = dot_total
+        world[spot] = column
+
+        def put(piece):
+            world[spot, 2:3] = piece
+
+        own_columns(size, gain_rows[...], put)
+        for i in range(replicas - 1):
+            world_copy(i).start()
+
     def tick(k, _):
         @pl.when(k < groups)
         def _():
@@ -1382,70 +1556,101 @@
 
         @pl.when(k == groups)
         def _():
-            cols_in[here] = cols[here]
-            for i in range(size - 1):
-                dot_copy(i).start()
-                col_copy(i).start()
+            exchange()
+
+        @pl.when(k == groups + 1)
+        def _():
+            for load in loads[3:]:
+                load.wait()
+            gate_f[...] = ggu[:, :hidden].astype(F32)
+            saves[0].start()
+
+        @pl.when(k == groups + 2)
+        def _():
+            up_f[...] = ggu[:, hidden:].astype(F32)
+            saves[1].start()
 
         @pl.when(k == groups + 3)
         def _():
-            for i in range(size - 1):
-                dot_copy(i).wait()
-                col_copy(i).wait()
-            total, column = dots[0], cols_in[0]
-            for j in range(1, size):
-                total = total + dots[j]
-                column = column + cols_in[j]
-            dot_o[...] = total
-            world[spot] = column + extra[1]
-            for i in range(replicas - 1):
-                world_copy(i).start()
+            spread()
+
+        @pl.when(k == groups + 4)
+        def _():
+            down_f[...] = flip(downw[...])
+            saves[2].start()
 
         return 0
 
-    lax.fori_loop(0, max(line.count, groups + 4), tick, 0)
-    line.finish(out_o)
+    lax.fori_loop(0, max(line.count, groups + 5), tick, 0)
+
+    def then(part, grad):
+        through = grad * gain_own[...] - x_own[part, :].astype(F32) * inv[part, :] * (
+            dot_sum[:, part].T[:, :1] / features
+        )
+        out_o[part, :] = (grad_own[part, :] + inv[part, :] * through).astype(BF)
+
+    line.finish(total, then)
     for i in range(replicas - 1):
         world_copy(i).wait()
-    total = world[0]
+    everything = world[0]
     for j in range(1, replicas):
-        total = total + world[j]
-    sum_o[...] = total
-
-
-def input_gradient(axes, grads, inv, gain, extra, w_query, w_key, w_value, x, chunk, after):
+        everything = everything + world[j]
+    sum_o[...] = everything
+    for save in saves:
+        save.wait()
+
+
+def input_gradient(
+    axes, grads, inv, gain, keep, attn_square, gain_rows, ffn_square, gain_own, x_own, grad_own,
+    w_query, w_key_t, w_value_t, x, ggu_sum, down_sum, chunk, after,
+):
     size, replicas = axes["tensor"], axes["dp"] * axes["context"]
     rows, features = x.shape
     width = features // size
+    share, hidden = down_sum.shape
     anywhere, vmem = pl.BlockSpec(memory_space=pl.ANY), pl.BlockSpec(memory_space=pltpu.VMEM)
     shape, dma = jax.ShapeDtypeStruct, pltpu.SemaphoreType.DMA
 
     def kernel(*refs):
-        input_kernel(axes, chunk, *refs[:8], *refs[8 + len(after) :])
+        input_kernel(axes, chunk, *refs[:16], *refs[16 + len(after) :])
 
     return pl.pallas_call(
         kernel,
-        in_specs=[vmem] * 4 + [anywhere] * (4 + len(after)),
-        out_specs=[vmem] * 3,
-        out_shape=[shape((rows, width), F32), shape((8, rows), F32), shape((8, width), F32)],
+        in_specs=[vmem] * 10 + [anywhere] * (6 + len(after)),
+        out_specs=[vmem] * 2 + [anywhere] * 3,
+        out_shape=[
+            shape((rows, width), BF),
+            shape((8, width), F32),
+            shape((share, hidden), F32),
+            shape((share, hidden), F32),
+            shape((hidden, share), F32),
+        ],
         scratch_shapes=scatter_scratch(size, rows, width, chunk)
         + [
             pltpu.VMEM((2, chunk, features), BF),
             pltpu.VMEM(w_query.shape, BF),
-            pltpu.VMEM(w_key.shape, BF),
-            pltpu.VMEM(w_value.shape, BF),
+            pltpu.VMEM(w_key_t.shape, BF),
+            pltpu.VMEM(w_value_t.shape, BF),
             pltpu.VMEM((size, 8, rows), F32),
+            pltpu.VMEM((8, rows), F32),
             pltpu.VMEM((size, 8, width), F32),
             pltpu.VMEM((size, 8, width), F32),
             pltpu.VMEM((replicas, 8, width), F32),
+            pltpu.VMEM((1, features), F32),
+            pltpu.VMEM(ggu_sum.shape, BF),
+            pltpu.VMEM(down_sum.shape, BF),
+            pltpu.VMEM((share, hidden), F32),
+            pltpu.VMEM((share, hidden), F32),
+            pltpu.VMEM((hidden, share), F32),
             dma((size - 1,)),
             dma((size - 1,)),
             dma((size - 1,)),
             dma((size - 1,)),
             dma((replicas - 1,)),
             dma((replicas - 1,)),
+            dma((5,)),
+            dma((2,)),
             dma((3,)),
-            dma((2,)),
         ],
         compiler_params=pltpu.CompilerParams(
             collective_id=4, has_side_effects=True, vmem_limit_bytes=VMEM_LIMIT
@@ -1456,7 +1661,10 @@
             transcendentals=rows,
         ),
         name="input_gradient",
-    )(grads, inv, gain, extra, w_query, w_key, w_value, x, *after)
+    )(
+        grads, inv, gain, keep, attn_square, gain_rows, ffn_square, gain_own, x_own, grad_own,
+        w_query, w_key_t, w_value_t, x, ggu_sum, down_sum, *after,
+    )
 
 
 def local(
@@ -1475,67 +1683,58 @@
     w_up,
     w_down,
 ):
-    here = lax.axis_index("tensor")
     _, rows, width = layer_input_hidden.shape
     size = axes["tensor"]
     features = width * size
     kvs = w_key.shape[1] // HD
     heads = w_query.shape[1] // HD
-    place = lax.axis_index("context")
-    offset = place * rows
-    own_columns = here * width
-
-    def own(a):
-        return lax.dynamic_slice_in_dim(a, own_columns, width, 1)
-
-    position = offset + jnp.arange(rows, dtype=jnp.int32)
-    length = jnp.sum(valid_mask[0])
-    starts = span_starts[0]
-    last = position
-    for k in range(starts.shape[0]):
-        inside = (position >= starts[k]) & (position < starts[k] + PIC)
-        last = jnp.maximum(last, jnp.where(inside, starts[k] + PIC - 1, 0))
-    kend = jnp.minimum(last + 1, length)[None, :]
-    keep = (position < length).astype(F32)[:, None]
+    position = lax.axis_index("context") * rows + jnp.arange(rows, dtype=jnp.int32)
     inverse_freq = rope_base ** (-2.0 * jnp.arange(HD // 2, dtype=F32) / HD)
     angles = inverse_freq[:, None] * position.astype(F32)[None, :]
     cos_tab, sin_tab = jnp.cos(angles), jnp.sin(angles)
-
     x_own = layer_input_hidden[0]
-    gain_own = jnp.concatenate([gain_attn[None], gain_mlp[None], jnp.zeros((6, width), F32)])
-    x_low, normed_a, inv_a, gains, query_t, both = project(
-        axes, x_own, gain_own, cos_tab, sin_tab, w_query, w_key, w_value, GROUP_ROWS, (kend, keep)
+    w_key_t, w_value_t = w_key.T, w_value.T
+
+    def shard(grad):
+        return lax.psum_scatter(grad, ("dp", "context"), scatter_dimension=0, tiled=True)
+
+    x_low, normed_a, inv_a, gains, query_t, both, kend, keep = project(
+        axes,
+        x_own,
+        gain_attn[None],
+        gain_mlp[None],
+        cos_tab,
+        sin_tab,
+        valid_mask,
+        span_starts,
+        w_query,
+        w_key_t,
+        w_value_t,
+        GROUP_ROWS,
     )
-    gain_m = gains[1:2]
-
     cot, mixed, lse = attend_forward(size, cotangent[0], query_t, both, kend, GROUP_ROWS)
-    mixed_t = mixed.reshape(heads * HD, rows)
-    normed_m, act, gg, gu, down_part, back_part, middle, attn_square = feed_forward(
-        size, mixed_t, keep, gain_m, w_out, w_gate, w_up, w_down, x_low, cot, GROUP_ROWS, HOP_ROWS
-    )
-
-    def shard(grad, dim):
-        return lax.psum_scatter(grad, ("dp", "context"), scatter_dimension=dim, tiled=True)
-
-    grad_down = ein("sf,sd->fd", act, cot).astype(BF)
-    grad_gate = ein("sd,sf->df", normed_m, gg).astype(BF)
-    grad_up = ein("sd,sf->df", normed_m, gu).astype(BF)
-    down_sum, gate_sum, up_sum = shard(grad_down, 1), shard(grad_gate, 0), shard(grad_up, 0)
-    grad_middle, grad_attn, grad_mixed, gain_m_rows = norm_back(
+    normed_m, act, ggu, down_part, back_part, middle, middle_own, attn_square = feed_forward(
         size,
-        back_part,
+        mixed.reshape(heads * HD, rows),
         keep,
-        gain_m,
+        gains,
         w_out,
-        middle,
+        w_gate,
+        w_up,
+        w_down,
+        x_low,
         cot,
         GROUP_ROWS,
         HOP_ROWS,
-        (grad_down, grad_gate, grad_up),
     )
-    grad_out = ein("xs,sd->xd", mixed_t, grad_attn).astype(BF)
-    out_sum = shard(grad_out, 1)
-    grads, ffn_out = attend_backward(
+    grad_ggu = ein("sd,sf->df", normed_m, ggu).astype(BF)
+    ggu_sum = shard(grad_ggu)
+
+    grad_own, grad_attn, grad_mixed, gain_m_rows, grad_down = norm_back(
+        size, back_part, keep, gains, w_out, middle, cot, act, GROUP_ROWS, HOP_ROWS, (grad_ggu,)
+    )
+    down_sum = shard(grad_down)
+    grads, layer_out, ffn_square, grad_rest = attend_backward(
         axes,
         down_part,
         query_t,
@@ -1546,57 +1745,48 @@
         lse,
         cos_tab,
         sin_tab,
+        middle_own,
+        grad_attn,
+        normed_a,
         GROUP_ROWS,
-        (grad_out, down_sum, gate_sum),
+        (grad_down,),
     )
-    grads = grads.reshape(-1, rows)
-    grad_project = ein("sd,xs->dx", normed_a, grads).astype(BF)
-    project_sum = shard(grad_project, 0)
-    layer_out = (own(middle) + ffn_out).astype(BF)
-
-    numbers = jnp.stack(
-        [
-            jnp.sum(keep * x_own.astype(F32) ** 2),
-            jnp.sum(own(attn_square)),
-            jnp.sum(ffn_out * ffn_out),
-            jnp.sum(keep) / size,
-        ]
-    )
-    numbers = jnp.pad(numbers[None], ((1, 6), (0, width - 4)))
-    extra = jnp.stack([numbers, jnp.pad(own(gain_m_rows), ((2, 5), (0, 0)))])
-    grad_a, row_dot, sums = input_gradient(
+    rest_sum = shard(grad_rest)
+
+    input_grad, sums, gate_sum, up_sum, down_sum = input_gradient(
         axes,
-        grads,
+        grads.reshape(-1, rows),
         inv_a,
         gains,
-        extra,
+        keep,
+        attn_square,
+        gain_m_rows,
+        ffn_square,
+        gain_attn[None],
+        x_own,
+        grad_own,
         w_query,
-        w_key,
-        w_value,
+        w_key_t,
+        w_value_t,
         x_low,
+        ggu_sum,
+        down_sum,
         GROUP_ROWS,
-        (grad_project, up_sum, out_sum),
+        (grad_rest,),
     )
-    hat_own = x_own.astype(F32) * inv_a
-    row_mean = row_dot[0][:, None] / features
-    through = inv_a * (grad_a * gain_attn[None, :] - hat_own * row_mean)
-    input_grad = (own(grad_middle) + through).astype(BF)
-    gain_a_sum, gain_m_sum, numbers = sums[0], sums[2], sums[1, :4]
-    down_sum, gate_sum, up_sum, out_sum, project_sum = (
-        a.astype(F32) for a in (down_sum, gate_sum, up_sum, out_sum, project_sum)
-    )
-    cut = [heads * HD, (heads + kvs) * HD]
-    query_sum, key_sum, value_sum = jnp.split(project_sum, cut, 1)
-    rms = jnp.sqrt(numbers[:3] / (numbers[3] * features))
+    rest_sum = rest_sum.astype(F32)
+    cut = [heads * HD, 2 * heads * HD, (2 * heads + kvs) * HD]
+    out_sum, query_sum, key_sum, value_sum = jnp.split(rest_sum, cut, 1)
+    rms = jnp.sqrt(sums[1, :3] / (sums[1, 3] * features))
     return (
         layer_out[None],
         input_grad[None],
-        gain_a_sum,
+        sums[0],
         query_sum,
         key_sum,
         value_sum,
-        out_sum,
-        gain_m_sum,
+        out_sum.T,
+        sums[2],
         gate_sum,
         up_sum,
         down_sum,

time: 857 us -> 1040 us (1.21)
  waiting for transfers between devices: 27.7 us -> 278 us
  matrix products: 61.5 us -> 26.7 us
  other arithmetic: 29.6 us -> 2.22 us
  Pallas kernels: 673 us -> 697 us
  local copies, waits for them, and re-layouts: 39.5 us -> 20 us
    reduce_scatter x3, waiting for transfers between devices: 27.1 us -> 277 us  [shard(): lax.psum_scatter(grad, ('dp', 'context'), scatter_dimension=0, tiled=True)]
    dot_general x5 -> x1, matrix products: 61.5 us -> 26.7 us  [ein(): return jnp.einsum(spec, a, b, preferred_element_type=F32)]
    pallas_call x4, Pallas kernels: 414 us -> 437 us  [the longest x1 147 us: norm_back(): pl.pallas_call(kernel, in_specs=[vmem] * 3 + [anywhere] * (4 + len(after)...]
    unnamed x30 -> x17, local copies, waits for them, and re-layouts: 29.4 us -> 10 us
    reduce_sum x5 -> x0, other arithmetic: 10.6 us -> none  [the longest x1 5.09 us: local(): jnp.sum(ffn_out * ffn_out)]
  transfers between devices with their start and end apart: 5 -> 3, of which waited for: 1 -> 3; matrix products, arithmetic and copies ran while one was open for 10% -> 1% of each run, Pallas kernels for 37% -> 0%
where the time goes in v4:
time: 1040 us
  Pallas kernels  697 us (67%)
  waiting for transfers between devices  278 us (27%)
  matrix products  26.7 us (3%)
  local copies, waits for them, and re-layouts  20 us (2%)
  between operations  14.7 us (1%)
    reduce_scatter x3, waiting for transfers between devices, shard(): lax.psum_scatter(grad, ('dp', 'context'), scatter_dimension=0, tiled=True)  277 us
    pallas_call x1, Pallas kernels, feed_forward(): pl.pallas_call(functools.partial(ffn_kernel, size, hop, chunk), in_specs=...  170 us
    pallas_call x1, Pallas kernels, norm_back(): pl.pallas_call(kernel, in_specs=[vmem] * 3 + [anywhere] * (4 + len(after)...  147 us
    pallas_call x1, Pallas kernels, project(): pl.pallas_call(functools.partial(project_kernel, size, contexts, chunk),...  103 us
    pallas_call x1, Pallas kernels, input_gradient(): pl.pallas_call(kernel, in_specs=[vmem] * 10 + [anywhere] * (6 + len(after...  99.3 us
    pallas_call x1, Pallas kernels, attend_forward(): pl.pallas_call(functools.partial(attend_kernel, size, chunk, key_rows), i...  90.7 us
    pallas_call x1, Pallas kernels, attend_backward(): pl.pallas_call(kernel, in_specs=[anywhere] + [vmem] * 9 + [anywhere] * (2...  87.3 us
    dot_general x1, matrix products, ein(): return jnp.einsum(spec, a, b, preferred_element_type=F32)  26.7 us
  transfers between devices with their start and end apart: 3, of which 3 were waited for; matrix products, arithmetic and copies ran while one was open for 1% of the time, Pallas kernels for 0%

profile of v4, /device:TPU:0, one launch (start us, length us, event | category | flops | bytes accessed | tf_op | source)
XLA Modules:
  0.0 1039.0 jit_solution(12404976426263320750)
XLA Ops:
  7.2 1.3 broadcast_in_dim.15.gain_attn.refs_7_
  8.5 1.3 broadcast_in_dim.16.gain_mlp
  9.8 1.4 multiply_sine_fusion
  11.2 103.4 %project.1 = (bf16[1024,2560]{1,0:T(8,128)(2,1)}, bf16[1024,2560]{1,0:T(8,128)(2,1)}, f32[1024,1]{1,0:T(8,128)}, f32[8,2560]{1,0:T(8,128)}, bf16[8,80,1024]{2,1,...) custom-call(bf16[1024,640]{1,0:T(8,128)(2,1)} %bitcast.18, ...), custom_call_target="tpu_custom_call" | custom-call | flops 5033164800 | bytes 20971520 | tf_op jit(solution)/shard_map/project/pallas_call | solution.py:1022
  114.6 90.7 %attend_forward.1 = (bf16[1024,2560]{1,0:T(8,128)(2,1)}, bf16[8,80,1024]{2,1,0:T(8,128)(2,1)}, f32[8,1,1024]{2,1,0:T(1,128)}) custom-call(bf16[1024,640]{1,0:T(8,128)(2,1)} %bitcast.26, bf16[8,80,1024]{2,1,0:T(8,128)(2,1)} %get-tuple-element.47.q.refs_1_, bf16[4,80,2048]{2,1,0:T(8,128)(2,1)} %get-tuple-element.48.kv.refs_2_, ...), custom_call_target="tpu_custom_call" | custom-call | flops 13421772800 | bytes 16777216 | tf_op jit(solution)/shard_map/attend_forward/pallas_call | solution.py:1152
  205.3 169.6 %feed_forward.1 = (bf16[1024,2560]{1,0:T(8,128)(2,1)}, bf16[1024,1792]{1,0:T(8,128)(2,1)}, bf16[1024,3584]{1,0:T(8,128)(2,1)}, bf16[4,1024,640]{2,1,0:T(8,128)(2...) custom-call(bf16[640,1024]{1,0:T(8,128)(2,1)} %bitcast.27, ...), custom_call_target="tpu_custom_call" | custom-call | flops 59726888960 | bytes 83886080 | tf_op jit(solution)/shard_map/feed_forward/pallas_call | solution.py:424
  374.9 26.7 %convolution_convert_fusion.refs_7_ = bf16[2560,3584]{1,0:T(8,128)(2,1)} fusion(bf16[1024,2560]{1,0:T(8,128)(2,1)} %get-tuple-element.59, bf16[1024,3584]{1,0:T(8,128)(2,1)} %get-tuple-element.60), kind=kOutput, calls=%fused_computation | convolution fusion | flops 18799656960 | bytes 30932992 | tf_op jit(solution)/shard_map/sd,sf->df/dot_general | solution.py:38
  401.6 146.9 %norm_back.1 = (f32[1024,640]{1,0:T(8,128)}, bf16[1024,2560]{1,0:T(8,128)(2,1)}, bf16[640,1024]{1,0:T(8,128)(2,1)}, f32[1,2560]{1,0:T(1,128)}, bf16[2560,1792]{1,0:T(8,128)(2,1)}) custom-call(bf16[1024,2560]{1,0:T(8,128)(2,1)} %get-tuple-element.56.refs_0_, f32[1024,1]{1,0:T(8,128)} %get-tuple-element.51.keep.refs_1_.refs_3_, ...), custom_call_target="tpu_custom_call" | custom-call | flops 12750684160 | bytes 41943040 | tf_op jit(solution)/shard_map/norm_back/pallas_call | solution.py:619
  548.5 87.3 %attend_backward.1 = (bf16[12,80,1024]{2,1,0:T(8,128)(2,1)}, bf16[1024,640]{1,0:T(8,128)(2,1)}, f32[1,640]{1,0:T(1,128)}, bf16[2560,1600]{1,0:T(8,128)(2,1)}) custom-call(bf16[4,1024,640]{2,1,0:T(8,128)(2,1)} %get-tuple-element.55.refs_0_, bf16[8,80,1024]{2,1,0:T(8,128)(2,1)} %get-tuple-element.47.q.refs_1_, ...), custom_call_target="tpu_custom_call" | custom-call | flops 21474836480 | bytes 16777216 | tf_op jit(solution)/shard_map/attend_backward/pallas_call | solution.py:1370
  637.3 76.3 %reduce-scatter.8.cloned.1.call-done = bf16[320,1600]{1,0:T(8,128)(2,1)} async-done(((bf16[2560,1600]{1,0:T(8,128)(2,1)}), bf16[320,1600]{1,0:T(8,128)(2,1)}) %reduce-scatter.8.cloned.1.call-update) | async-done | bytes 1024016 | tf_op jit(solution)/shard_map/reduce_scatter | solution.py:1699
  713.6 1.2 fusion
  714.8 0.8 copy.28
  716.5 1.9 split.16
  718.6 0.9 slice_bitcast_fusion
  719.5 72.8 %reduce-scatter.6.cloned.1.call-done.refs_15_ = bf16[320,1792]{1,0:T(8,128)(2,1)} async-done(((bf16[2560,1792]{1,0:T(8,128)(2,1)}), bf16[320,1792]{1,0:T(8,128)(2,1)}) %reduce-scatter.6.cloned.1.call-update) | async-done | bytes 1146896 | tf_op jit(solution)/shard_map/reduce_scatter | solution.py:1699
  792.3 127.6 %reduce-scatter.4.cloned.1.call-done.refs_14_ = bf16[320,3584]{1,0:T(8,128)(2,1)} async-done(((bf16[2560,3584]{1,0:T(8,128)(2,1)}), bf16[320,3584]{1,0:T(8,128)(2,1)}) %reduce-scatter.4.cloned.1.call-update) | async-done | bytes 2293776 | tf_op jit(solution)/shard_map/reduce_scatter | solution.py:1699
  919.8 99.3 %input_gradient.1 = (bf16[1024,640]{1,0:T(8,128)(2,1)}, f32[8,640]{1,0:T(8,128)}, f32[320,1792]{1,0:T(8,128)}, f32[320,1792]{1,0:T(8,128)}, f32[1792,320]{1,0:T(8,128)}) custom-call(bf16[960,1024]{1,0:T(8,128)(2,1)} %bitcast.17, f32[1024,1]{1,0:T(8,128)} %get-tuple-element.69.refs_1_, f32[8,2560]{1,0:T(8,128)} %get-tuple-element.52.gain.refs_2_, ...), custom_call_target="tpu_custom_call" | custom-call | flops 5033164800 | bytes 20971520 | tf_op jit(solution)/shard_map/input_gradient/pallas_call | solution.py:1617
  1019.2 1.4 slice.27
  1020.5 1.4 slice_reduce_fusion
  1023.9 3.3 copy.29
  1027.2 1.1 copy.34
  1028.3 1.1 copy.35
  1029.5 1.4 copy.36
  1030.9 1.4 copy.37
  (22 shorter events, 4.0 us)
Async XLA Ops:
  7.2 706.4 %reduce-scatter.8.cloned.1.call-start = ((), (), s32[]{:S(2)}) async-start(), calls=%async_computation.5 | async-start | bytes 9584640 | tf_op jit(solution)/shard_map/reduce_scatter | solution.py:1699
  635.9 156.4 %reduce-scatter.6.cloned.1.call-start = ((), (), s32[]{:S(2)}) async-start(), calls=%async_computation.4 | async-start | bytes 10321920 | tf_op jit(solution)/shard_map/reduce_scatter | solution.py:1699
  636.6 283.2 %reduce-scatter.4.cloned.1.call-start = ((), (), s32[]{:S(2)}) async-start(), calls=%async_computation.3 | async-start | bytes 20643840 | tf_op jit(solution)/shard_map/reduce_scatter | solution.py:1699
  713.6 4.8 copy-start
  1019.2 8.0 copy-start.3
  1023.9 4.4 copy-start.4
  1027.2 2.3 copy-start.2
  1028.3 2.6 copy-start.1
Sparse Core Ops, SparseCore 0:
  636.0 77.5 reduce-scatter.7
  717.2 75.0 reduce-scatter.5
  796.5 123.3 reduce-scatter.3

commit v5 on v4

--- a/solution.py
+++ b/solution.py
@@ -1414,26 +1414,23 @@
 def input_kernel(
     axes, chunk,
     grads, inv, gain, keep, attn_square, gain_rows, ffn_square, gain_own, x_own, grad_own,
-    w_query, w_key_t, w_value_t, x, ggu_sum, down_sum,
-    out_o, sum_o, gate_o, up_o, down_o,
+    w_query, w_key_t, w_value_t, x,
+    out_o, sum_o,
     parts, ups, downs, total, up_send, up_recv, down_send, down_recv,
-    xs, wq, wk, wv, dots, dot_sum, cols, cols_in, world, square, ggu, downw, gate_f, up_f, down_f,
-    dot_send, dot_recv, col_send, col_recv, world_send, world_recv, w_sem, x_sem, out_sem,
+    xs, wq, wk, wv, dots, dot_sum, cols, cols_in, world, square,
+    dot_send, dot_recv, col_send, col_recv, world_send, world_recv, w_sem, x_sem,
 ):
     size = axes["tensor"]
     here = lax.axis_index("tensor")
     rows, features = x.shape
     width, groups = features // size, rows // chunk
     nq, nk = w_query.shape[1], w_key_t.shape[0]
-    hidden = down_sum.shape[1]
     line = Scatter(
         size, groups, chunk, parts, ups, downs, (up_send, up_recv, down_send, down_recv)
     )
     loads = [
         pltpu.make_async_copy(a, b, w_sem.at[i])
-        for i, (a, b) in enumerate(
-            ((w_query, wq), (w_key_t, wk), (w_value_t, wv), (ggu_sum, ggu), (down_sum, downw))
-        )
+        for i, (a, b) in enumerate(((w_query, wq), (w_key_t, wk), (w_value_t, wv)))
     ]
 
     def load_x(c):
@@ -1449,7 +1446,7 @@
     far = [lax.rem(spot + i, replicas) for i in range(1, replicas)]
     far = [{"dp": lax.div(i, contexts), "context": lax.rem(i, contexts)} for i in far]
     greet(peers + far)
-    for load in loads[:3]:
+    for load in loads:
         load.wait()
     square[...] = jnp.zeros_like(square)
     row = lax.broadcasted_iota(jnp.int32, (8, width), 0)
@@ -1511,11 +1508,6 @@
         mine = world.at[spot]
         return copy_to(mine, mine, world_send.at[i], world_recv.at[i], far[i])
 
-    saves = [
-        pltpu.make_async_copy(a, b, out_sem.at[i])
-        for i, (a, b) in enumerate(((gate_f, gate_o), (up_f, up_o), (down_f, down_o)))
-    ]
-
     def exchange():
         numbers = jnp.zeros((8, width), F32)
         for i, a in enumerate((square[...], attn_square[...], ffn_square[...], keep[...])):
@@ -1558,30 +1550,13 @@
         def _():
             exchange()
 
-        @pl.when(k == groups + 1)
-        def _():
-            for load in loads[3:]:
-                load.wait()
-            gate_f[...] = ggu[:, :hidden].astype(F32)
-            saves[0].start()
-
-        @pl.when(k == groups + 2)
-        def _():
-            up_f[...] = ggu[:, hidden:].astype(F32)
-            saves[1].start()
-
         @pl.when(k == groups + 3)
         def _():
             spread()
 
-        @pl.when(k == groups + 4)
-        def _():
-            down_f[...] = flip(downw[...])
-            saves[2].start()
-
         return 0
 
-    lax.fori_loop(0, max(line.count, groups + 5), tick, 0)
+    lax.fori_loop(0, max(line.count, groups + 4), tick, 0)
 
     def then(part, grad):
         through = grad * gain_own[...] - x_own[part, :].astype(F32) * inv[part, :] * (
@@ -1596,34 +1571,28 @@
     for j in range(1, replicas):
         everything = everything + world[j]
     sum_o[...] = everything
-    for save in saves:
-        save.wait()
 
 
 def input_gradient(
     axes, grads, inv, gain, keep, attn_square, gain_rows, ffn_square, gain_own, x_own, grad_own,
-    w_query, w_key_t, w_value_t, x, ggu_sum, down_sum, chunk, after,
+    w_query, w_key_t, w_value_t, x, chunk, after,
 ):
     size, replicas = axes["tensor"], axes["dp"] * axes["context"]
     rows, features = x.shape
     width = features // size
-    share, hidden = down_sum.shape
     anywhere, vmem = pl.BlockSpec(memory_space=pl.ANY), pl.BlockSpec(memory_space=pltpu.VMEM)
     shape, dma = jax.ShapeDtypeStruct, pltpu.SemaphoreType.DMA
 
     def kernel(*refs):
-        input_kernel(axes, chunk, *refs[:16], *refs[16 + len(after) :])
+        input_kernel(axes, chunk, *refs[:14], *refs[14 + len(after) :])
 
     return pl.pallas_call(
         kernel,
-        in_specs=[vmem] * 10 + [anywhere] * (6 + len(after)),
-        out_specs=[vmem] * 2 + [anywhere] * 3,
+        in_specs=[vmem] * 10 + [anywhere] * (4 + len(after)),
+        out_specs=[vmem] * 2,
         out_shape=[
             shape((rows, width), BF),
             shape((8, width), F32),
-            shape((share, hidden), F32),
-            shape((share, hidden), F32),
-            shape((hidden, share), F32),
         ],
         scratch_shapes=scatter_scratch(size, rows, width, chunk)
         + [
@@ -1637,20 +1606,14 @@
             pltpu.VMEM((size, 8, width), F32),
             pltpu.VMEM((replicas, 8, width), F32),
             pltpu.VMEM((1, features), F32),
-            pltpu.VMEM(ggu_sum.shape, BF),
-            pltpu.VMEM(down_sum.shape, BF),
-            pltpu.VMEM((share, hidden), F32),
-            pltpu.VMEM((share, hidden), F32),
-            pltpu.VMEM((hidden, share), F32),
             dma((size - 1,)),
             dma((size - 1,)),
             dma((size - 1,)),
             dma((size - 1,)),
             dma((replicas - 1,)),
             dma((replicas - 1,)),
-            dma((5,)),
+            dma((3,)),
             dma((2,)),
-            dma((3,)),
         ],
         compiler_params=pltpu.CompilerParams(
             collective_id=4, has_side_effects=True, vmem_limit_bytes=VMEM_LIMIT
@@ -1663,7 +1626,7 @@
         name="input_gradient",
     )(
         grads, inv, gain, keep, attn_square, gain_rows, ffn_square, gain_own, x_own, grad_own,
-        w_query, w_key_t, w_value_t, x, ggu_sum, down_sum, *after,
+        w_query, w_key_t, w_value_t, x, *after,
     )
 
 
@@ -1749,11 +1712,11 @@
         grad_attn,
         normed_a,
         GROUP_ROWS,
-        (grad_down,),
+        (ggu_sum,),
     )
     rest_sum = shard(grad_rest)
 
-    input_grad, sums, gate_sum, up_sum, down_sum = input_gradient(
+    input_grad, sums = input_gradient(
         axes,
         grads.reshape(-1, rows),
         inv_a,
@@ -1769,12 +1732,12 @@
         w_key_t,
         w_value_t,
         x_low,
-        ggu_sum,
-        down_sum,
         GROUP_ROWS,
-        (grad_rest,),
+        (grad_rest, down_sum),
     )
-    rest_sum = rest_sum.astype(F32)
+    rest_sum = jnp.where(sums[1, 3] >= 0.0, rest_sum.astype(F32), 0.0)
+    gate_sum, up_sum = jnp.split(ggu_sum.astype(F32), 2, 1)
+    down_sum = down_sum.astype(F32).T
     cut = [heads * HD, 2 * heads * HD, (2 * heads + kvs) * HD]
     out_sum, query_sum, key_sum, value_sum = jnp.split(rest_sum, cut, 1)
     rms = jnp.sqrt(sums[1, :3] / (sums[1, 3] * features))

time: 1040 us -> 768 us (0.74)
  waiting for transfers between devices: 278 us -> 0.09 us
    reduce_scatter x3, waiting for transfers between devices: 277 us -> 0.04 us  [shard(): lax.psum_scatter(grad, ('dp', 'context'), scatter_dimension=0, tiled=True)]
  transfers between devices with their start and end apart: 3 -> 3, of which waited for: 3 -> 0; matrix products, arithmetic and copies ran while one was open for 1% -> 1% of each run, Pallas kernels for 0% -> 44%
where the time goes in v5:
time: 768 us; the launch traced here: 765 us
  Pallas kernels  703 us (92%)
  matrix products  26.7 us (3%)
  between operations  15.4 us (2%)
  local copies, waits for them, and re-layouts  13.5 us (2%)
    pallas_call x1, Pallas kernels, feed_forward(): pl.pallas_call(functools.partial(ffn_kernel, size, hop, chunk), in_specs=...  169 us
    pallas_call x1, Pallas kernels, norm_back(): pl.pallas_call(kernel, in_specs=[vmem] * 3 + [anywhere] * (4 + len(after)...  149 us
    pallas_call x1, Pallas kernels, project(): pl.pallas_call(functools.partial(project_kernel, size, contexts, chunk),...  103 us
    pallas_call x1, Pallas kernels, input_gradient(): pl.pallas_call(kernel, in_specs=[vmem] * 10 + [anywhere] * (4 + len(after...  97.1 us
    pallas_call x1, Pallas kernels, attend_backward(): pl.pallas_call(kernel, in_specs=[anywhere] + [vmem] * 9 + [anywhere] * (2...  93.9 us
    pallas_call x1, Pallas kernels, attend_forward(): pl.pallas_call(functools.partial(attend_kernel, size, chunk, key_rows), i...  90.7 us
    dot_general x1, matrix products, ein(): return jnp.einsum(spec, a, b, preferred_element_type=F32)  26.7 us
  transfers between devices with their start and end apart: 3, of which 0 were waited for; matrix products, arithmetic and copies ran while one was open for 1% of the time, Pallas kernels for 44%

profile of v5, /device:TPU:0, one launch (start us, length us, event | category | flops | bytes accessed | tf_op | source)
XLA Modules:
  0.0 765.4 jit_solution(11529016967676860460)
XLA Ops:
  7.2 1.3 broadcast_in_dim.19.gain_attn.refs_7_
  8.5 1.3 broadcast_in_dim.20.gain_mlp
  9.8 1.4 multiply_sine_fusion
  11.2 103.2 %project.1 = (bf16[1024,2560]{1,0:T(8,128)(2,1)}, bf16[1024,2560]{1,0:T(8,128)(2,1)}, f32[1024,1]{1,0:T(8,128)}, f32[8,2560]{1,0:T(8,128)}, bf16[8,80,1024]{2,1,...) custom-call(bf16[1024,640]{1,0:T(8,128)(2,1)} %bitcast.21, ...), custom_call_target="tpu_custom_call" | custom-call | flops 5033164800 | bytes 20971520 | tf_op jit(solution)/shard_map/project/pallas_call | solution.py:1022
  114.3 90.7 %attend_forward.1 = (bf16[1024,2560]{1,0:T(8,128)(2,1)}, bf16[8,80,1024]{2,1,0:T(8,128)(2,1)}, f32[8,1,1024]{2,1,0:T(1,128)}) custom-call(bf16[1024,640]{1,0:T(8,128)(2,1)} %bitcast.29, bf16[8,80,1024]{2,1,0:T(8,128)(2,1)} %get-tuple-element.44.q.refs_1_, bf16[4,80,2048]{2,1,0:T(8,128)(2,1)} %get-tuple-element.45.kv.refs_2_, ...), custom_call_target="tpu_custom_call" | custom-call | flops 13421772800 | bytes 16777216 | tf_op jit(solution)/shard_map/attend_forward/pallas_call | solution.py:1152
  205.0 169.4 %feed_forward.1 = (bf16[1024,2560]{1,0:T(8,128)(2,1)}, bf16[1024,1792]{1,0:T(8,128)(2,1)}, bf16[1024,3584]{1,0:T(8,128)(2,1)}, bf16[4,1024,640]{2,1,0:T(8,128)(2...) custom-call(bf16[640,1024]{1,0:T(8,128)(2,1)} %bitcast.30, ...), custom_call_target="tpu_custom_call" | custom-call | flops 59726888960 | bytes 83886080 | tf_op jit(solution)/shard_map/feed_forward/pallas_call | solution.py:424
  374.4 26.7 %convolution_convert_fusion.refs_7_ = bf16[2560,3584]{1,0:T(8,128)(2,1)} fusion(bf16[1024,2560]{1,0:T(8,128)(2,1)} %get-tuple-element.56, bf16[1024,3584]{1,0:T(8,128)(2,1)} %get-tuple-element.57), kind=kOutput, calls=%fused_computation | convolution fusion | flops 18799656960 | bytes 30932992 | tf_op jit(solution)/shard_map/sd,sf->df/dot_general | solution.py:38
  401.2 149.1 %norm_back.1 = (f32[1024,640]{1,0:T(8,128)}, bf16[1024,2560]{1,0:T(8,128)(2,1)}, bf16[640,1024]{1,0:T(8,128)(2,1)}, f32[1,2560]{1,0:T(1,128)}, bf16[2560,1792]{1,0:T(8,128)(2,1)}) custom-call(bf16[1024,2560]{1,0:T(8,128)(2,1)} %get-tuple-element.53.refs_0_, f32[1024,1]{1,0:T(8,128)} %get-tuple-element.48.keep.refs_1_.refs_3_, ...), custom_call_target="tpu_custom_call" | custom-call | flops 12750684160 | bytes 41943040 | tf_op jit(solution)/shard_map/norm_back/pallas_call | solution.py:619
  550.4 0.0 reduce-scatter.8.cloned.1.call-start
  550.5 93.9 %attend_backward.1 = (bf16[12,80,1024]{2,1,0:T(8,128)(2,1)}, bf16[1024,640]{1,0:T(8,128)(2,1)}, f32[1,640]{1,0:T(1,128)}, bf16[2560,1600]{1,0:T(8,128)(2,1)}) custom-call(bf16[4,1024,640]{2,1,0:T(8,128)(2,1)} %get-tuple-element.52.refs_0_, bf16[8,80,1024]{2,1,0:T(8,128)(2,1)} %get-tuple-element.44.q.refs_1_, ...), custom_call_target="tpu_custom_call" | custom-call | flops 21474836480 | bytes 16777216 | tf_op jit(solution)/shard_map/attend_backward/pallas_call | solution.py:1370
  644.4 2.8 convert_bitcast_fusion
  647.2 97.1 %input_gradient.1 = (bf16[1024,640]{1,0:T(8,128)(2,1)}, f32[8,640]{1,0:T(8,128)}) custom-call(bf16[960,1024]{1,0:T(8,128)(2,1)} %bitcast.20, f32[1024,1]{1,0:T(8,128)} %get-tuple-element.65.refs_1_, f32[8,2560]{1,0:T(8,128)} %get-tuple-element.49.gain.refs_2_, f32[1024,1]{1,0:T(8,128)} %get-tuple-element.48.keep.refs_1_.refs_3_, ...), custom_call_target="tpu_custom_call" | custom-call | flops 5033164800 | bytes 20971520 | tf_op jit(solution)/shard_map/input_gradient/pallas_call | solution.py:1589
  744.3 1.3 slice.26
  746.9 0.7 divide_sqrt_fusion
  747.5 0.6 fusion.2
  748.2 1.4 slice_reduce_fusion
  749.6 2.5 fusion
  752.1 1.4 convert_select_fusion
  753.4 0.2 fusion.1
  753.6 1.3 slice_bitcast_fusion
  754.9 0.8 copy.28
  755.7 0.8 copy.27
  756.5 1.1 copy.31
  757.6 1.1 copy.32
  (16 shorter events, 0.2 us)
Async XLA Ops:
  7.2 543.3 %reduce-scatter.4.cloned.1.call-start = ((), (), s32[]{:S(2)}) async-start(), calls=%async_computation.3 | async-start | bytes 20643840 | tf_op jit(solution)/shard_map/reduce_scatter | solution.py:1662
  401.2 243.2 %reduce-scatter.6.cloned.1.call-start = ((), (), s32[]{:S(2)}) async-start(), calls=%async_computation.4 | async-start | bytes 10321920 | tf_op jit(solution)/shard_map/reduce_scatter | solution.py:1662
  550.4 201.7 %reduce-scatter.8.cloned.1.call-start = ((), (), s32[]{:S(2)}) async-start(), calls=%async_computation.5 | async-start | bytes 9584640 | tf_op jit(solution)/shard_map/reduce_scatter | solution.py:1662
  647.2 102.4 %copy-start = (bf16[320,3584]{1,0:T(8,128)(2,1)S(1)}, bf16[320,3584]{1,0:T(8,128)(2,1)}, u32[]{:S(2)}) copy-start(bf16[320,3584]{1,0:T(8,128)(2,1)} %reduce-scatter.4.cloned.1.call-done.refs_12_) | copy-start | bytes 6881284
  753.6 3.0 copy-start.1
  754.9 2.7 copy-start.2
Sparse Core Ops, SparseCore 0:
  401.3 120.7 reduce-scatter.3
  550.5 81.2 reduce-scatter.5
  644.5 73.5 reduce-scatter.7

commit v6 on v5

--- a/solution.py
+++ b/solution.py
@@ -39,8 +39,11 @@
 
 
 MESH_ID = pl.DeviceIdType.MESH
-RING = 8
 SENT = 4
+
+
+def ring_of(size):
+    return size + 4
 
 
 def add_low(a, b):
@@ -79,7 +82,7 @@
             pl.semaphore_wait(barrier, 1)
 
     def up(self, c):
-        slot = lax.rem(c, RING)
+        slot = lax.rem(c, ring_of(self.size))
         return pltpu.make_async_remote_copy(
             src_ref=self.low.at[slot],
             dst_ref=self.low.at[slot],
@@ -90,7 +93,7 @@
         )
 
     def down(self, c):
-        slot, mine = lax.rem(c, RING), lax.rem(c, SENT)
+        slot, mine = lax.rem(c, ring_of(self.size)), lax.rem(c, SENT)
         return pltpu.make_async_remote_copy(
             src_ref=self.sent.at[mine],
             dst_ref=self.high.at[slot],
@@ -107,7 +110,7 @@
 
         @pl.when((c >= 0) & (c < count))
         def _():
-            slot = lax.rem(c, RING)
+            slot = lax.rem(c, ring_of(self.size))
 
             @pl.when(bottom)
             def _():
@@ -126,7 +129,7 @@
 
         @pl.when((d >= 0) & (d < count))
         def _():
-            slot, mine = lax.rem(d, RING), lax.rem(d, SENT)
+            slot, mine = lax.rem(d, ring_of(self.size)), lax.rem(d, SENT)
 
             @pl.when(top)
             def _():
@@ -153,7 +156,7 @@
             self.down(d - 2).wait_send()
 
     def total(self, c, then):
-        slot = lax.rem(c, RING)
+        slot = lax.rem(c, ring_of(self.size))
         top = self.here == self.size - 1
 
         @pl.when(top)
@@ -165,15 +168,16 @@
             then(self.low[slot].astype(F32) + self.high[slot].astype(F32))
 
 
-def sum_scratch(hop, features):
+def sum_scratch(size, hop, features):
+    ring, dma = ring_of(size), pltpu.SemaphoreType.DMA
     return [
-        pltpu.VMEM((RING, hop, features), BF),
-        pltpu.VMEM((RING, hop, features), BF),
+        pltpu.VMEM((ring, hop, features), BF),
+        pltpu.VMEM((ring, hop, features), BF),
         pltpu.VMEM((SENT, hop, features), BF),
-        pltpu.SemaphoreType.DMA((RING,)),
-        pltpu.SemaphoreType.DMA((RING,)),
-        pltpu.SemaphoreType.DMA((SENT,)),
-        pltpu.SemaphoreType.DMA((RING,)),
+        dma((ring,)),
+        dma((ring,)),
+        dma((SENT,)),
+        dma((ring,)),
     ]
 
 
@@ -208,10 +212,12 @@
     tiles_f, tiles_d = hidden // tile_f, features // tile_d
     half_f, half_d = -(-tiles_f // 2), -(-tiles_d // 2)
     lag = size - 1 + per - 1
+    ahead, part_slots = per // 2, parts.shape[0]
     ticks = max(per * groups + lag, count + size)
 
     def part(c):
-        return parts[lax.rem(lax.div(c, per), 2), pl.ds(pl.multiple_of(lax.rem(c, per) * hop, hop), hop), :]
+        slot = lax.rem(lax.div(c, per), part_slots)
+        return parts[slot, pl.ds(pl.multiple_of(lax.rem(c, per) * hop, hop), hop), :]
 
     sums = Sums(size, count, part, low, high, sent, (low_send, low_recv, high_send, high_recv))
     loads = [
@@ -256,7 +262,7 @@
         ]
 
     def project(g):
-        at = lax.rem(g, 2)
+        at = lax.rem(g, part_slots)
         lhs = mixed[:, pl.ds(pl.multiple_of(g * chunk, chunk), chunk)]
 
         def one(j, _):
@@ -349,17 +355,17 @@
         def _():
             finish(c)
 
-        ahead = k + 2
-
-        @pl.when((lax.rem(ahead, per) == 0) & (ahead < count))
-        def _():
-            project(lax.div(ahead, per))
+        later = k + ahead
+
+        @pl.when((lax.rem(later, per) == 0) & (later < count))
+        def _():
+            project(lax.div(later, per))
 
         s = k - lag
         g, stage = lax.div(s, per), lax.rem(s, per)
         going = (s >= 0) & (g < groups)
 
-        @pl.when(going & (stage == 0))
+        @pl.when(going & (stage == 0 * per // 4))
         def _():
             @pl.when(g == 0)
             def _():
@@ -375,7 +381,7 @@
 
             inner(g, 0, half_f)
 
-        @pl.when(going & (stage == 1))
+        @pl.when(going & (stage == 1 * per // 4))
         def _():
             inner(g, half_f, tiles_f)
             for copy in save_act(g):
@@ -385,7 +391,7 @@
             def _():
                 load_cot(g + 1).start()
 
-        @pl.when(going & (stage == 2))
+        @pl.when(going & (stage == 2 * per // 4))
         def _():
             @pl.when(g > 0)
             def _():
@@ -394,7 +400,7 @@
 
             outer(g, 0, half_d)
 
-        @pl.when(going & (stage == 3))
+        @pl.when(going & (stage == 3 * per // 4))
         def _():
             outer(g, half_d, tiles_d)
             for j in range(size):
@@ -418,7 +424,6 @@
     rows, features = x.shape
     hidden = w_gate.shape[1]
     per = chunk // hop
-    assert per == 4
     anywhere, vmem = pl.BlockSpec(memory_space=pl.ANY), pl.BlockSpec(memory_space=pltpu.VMEM)
     shape = jax.ShapeDtypeStruct
     return pl.pallas_call(
@@ -435,13 +440,13 @@
             shape((rows, features // size), F32),
             shape((1, features), F32),
         ],
-        scratch_shapes=sum_scratch(hop, features)
+        scratch_shapes=sum_scratch(size, hop, features)
         + [
             pltpu.VMEM(w_out.shape, BF),
             pltpu.VMEM(w_gate.shape, BF),
             pltpu.VMEM(w_up.shape, BF),
             pltpu.VMEM(w_down.shape, BF),
-            pltpu.VMEM((2, chunk, features), BF),
+            pltpu.VMEM((-(-(per + size - 2 + per // 2) // per), chunk, features), BF),
             pltpu.VMEM((2, chunk, features), BF),
             pltpu.VMEM((2, hop, features), BF),
             pltpu.VMEM((chunk, features), BF),
@@ -627,7 +632,7 @@
             shape((1, features), F32),
             shape((features, act.shape[1]), BF),
         ],
-        scratch_shapes=sum_scratch(hop, features)
+        scratch_shapes=sum_scratch(size, hop, features)
         + [
             pltpu.VMEM(w_out.shape, BF),
             pltpu.VMEM((2, hop, features), F32),
@@ -884,21 +889,28 @@
     return lax.div(free, key_rows), lax.div(last + key_rows - 1, key_rows)
 
 
-def project_kernel(
-    size, contexts, chunk,
-    own, gain_attn, gain_mlp, cos_tab, sin_tab, mask, starts, w_query, w_key_t, w_value_t,
-    x_o, normed_o, inv_o, gain_o, query_o, kv_o, kend_o, keep_o,
+def attend_kernel(
+    size, contexts, chunk, key_rows,
+    own, own_cot, gain_pair, cos_tab, sin_tab, mask, starts, w_query, w_key_t, w_value_t,
+    x_o, normed_o, inv_o, gain_o, q, kv_o, kend, keep_o, cot_o, mixed_o, lse_o,
     xs, up_send, up_recv, down_send, down_recv, own_sem,
-    gains, full, normed, kv, wq, wk, wv,
-    gain_send, gain_recv, kv_send, kv_recv, w_sem, out_sem, kv_sem,
+    blocks, up_send_c, up_recv_c, down_send_c, down_recv_c, own_sem_c,
+    gains, full, normed, full_c, kv, wq, wk, wv, keys_in_rows, acc, mx, sm,
+    gain_send, gain_recv, kv_send, kv_recv, w_sem, out_sem, kv_sem, cot_sem,
 ):
     here, place = lax.axis_index("tensor"), lax.axis_index("context")
     rows, width = own.shape
     features = size * width
     groups = rows // chunk
     heads, kvs = w_query.shape[1] // HD, w_key_t.shape[0] // HD
+    keys, group = contexts * rows, heads // kvs
+    units = kvs * groups
     line = Gather(
         size, groups, chunk, own, xs, (up_send, up_recv, down_send, down_recv, own_sem)
+    )
+    line_c = Gather(
+        size, groups, chunk, own_cot, blocks,
+        (up_send_c, up_recv_c, down_send_c, down_recv_c, own_sem_c),
     )
     loads = [
         pltpu.make_async_copy(a, b, w_sem.at[i])
@@ -908,8 +920,7 @@
     for load in loads:
         load.start()
     gains[here] = jnp.zeros_like(gains[here])
-    gains[here, 0:1] = gain_attn[...]
-    gains[here, 1:2] = gain_mlp[...]
+    gains[here, 0:2] = gain_pair[...]
     tensor_peers, context_peers = others("tensor", size), others("context", contexts)
     greet(tensor_peers + context_peers)
 
@@ -935,6 +946,7 @@
         )
 
     line.begin()
+    line_c.load_all()
     for i in range(size - 1):
         gain_copy(i).start()
 
@@ -945,7 +957,7 @@
         start = starts[:, k : k + 1]
         inside = (position >= start) & (position < start + PIC)
         last = jnp.maximum(last, jnp.where(inside, start + PIC - 1, 0))
-    kend_o[...] = jnp.minimum(last + 1, length)
+    kend[...] = jnp.minimum(last + 1, length)
     down_rows = lax.broadcasted_iota(jnp.int32, (rows, 1), 0) + place * rows
     keep_o[...] = jnp.where(down_rows < length, 1.0, 0.0)
 
@@ -956,7 +968,7 @@
             pltpu.make_async_copy(normed, normed_o.at[part], out_sem.at[1]),
         ]
 
-    def compute(g):
+    def project(g):
         part = pl.ds(pl.multiple_of(g * chunk, chunk), chunk)
 
         @pl.when(g == 0)
@@ -990,109 +1002,29 @@
             kv_copy(g, i).start()
         query = dot(normed[...], wq[...]).T
         for h in range(heads):
-            query_o[h, :, part] = turn(query[h * HD : (h + 1) * HD], cos_t, sin_t).astype(BF)
-
-    def tick(k, _):
-        line.tick(k, compute)
-        return 0
-
-    lax.fori_loop(0, line.ticks, tick, 0)
-    for copy in save(groups - 1):
-        copy.wait()
-    for i in range(size - 1):
-        gain_copy(i).wait_send()
-    line.drain()
-    for g in range(groups):
-        for i in range(contexts - 1):
-            kv_copy(g, i).wait()
-    out = pltpu.make_async_copy(kv, kv_o, kv_sem)
-    out.start()
-    out.wait()
-
-
-def project(
-    axes, own, gain_attn, gain_mlp, cos_tab, sin_tab, mask, starts, w_query, w_key_t, w_value_t, chunk
-):
-    size, contexts = axes["tensor"], axes["context"]
-    rows, width = own.shape
-    features, groups = size * width, rows // chunk
-    heads, kvs = w_query.shape[1] // HD, w_key_t.shape[0] // HD
-    anywhere, vmem = pl.BlockSpec(memory_space=pl.ANY), pl.BlockSpec(memory_space=pltpu.VMEM)
-    shape, dma = jax.ShapeDtypeStruct, pltpu.SemaphoreType.DMA
-    return pl.pallas_call(
-        functools.partial(project_kernel, size, contexts, chunk),
-        in_specs=[anywhere] + [vmem] * 6 + [anywhere] * 3,
-        out_specs=[anywhere] * 2 + [vmem] * 3 + [anywhere] + [vmem] * 2,
-        out_shape=[
-            shape((rows, features), BF),
-            shape((rows, features), BF),
-            shape((rows, 1), F32),
-            shape((8, features), F32),
-            shape((heads, HD, rows), BF),
-            shape((2 * kvs, HD, contexts * rows), BF),
-            shape((1, rows), jnp.int32),
-            shape((rows, 1), F32),
-        ],
-        scratch_shapes=gather_scratch(size, rows, width, chunk)
-        + [
-            pltpu.VMEM((size, 8, width), F32),
-            pltpu.VMEM((chunk, features), BF),
-            pltpu.VMEM((chunk, features), BF),
-            pltpu.VMEM((2 * kvs, HD, contexts * rows), BF),
-            pltpu.VMEM(w_query.shape, BF),
-            pltpu.VMEM(w_key_t.shape, BF),
-            pltpu.VMEM(w_value_t.shape, BF),
-            dma((size - 1,)),
-            dma((size - 1,)),
-            dma((groups, max(contexts - 1, 1))),
-            dma((groups, max(contexts - 1, 1))),
-            dma((3,)),
-            dma((2,)),
-            dma,
-        ],
-        compiler_params=pltpu.CompilerParams(
-            collective_id=3, has_side_effects=True, vmem_limit_bytes=VMEM_LIMIT
-        ),
-        cost_estimate=pl.CostEstimate(
-            flops=2 * rows * features * (heads + 2 * kvs) * HD,
-            bytes_accessed=20 << 20,
-            transcendentals=rows,
-        ),
-        name="project",
-    )(own, gain_attn, gain_mlp, cos_tab, sin_tab, mask, starts, w_query, w_key_t, w_value_t)
-
-
-def attend_kernel(
-    size, chunk, key_rows,
-    own, q, kv, kend,
-    cot_o, mixed_o, lse_o,
-    blocks, up_send, up_recv, down_send, down_recv, own_sem,
-    full, keys_in_rows, acc, mx, sm, out_sem,
-):
-    rows, _ = own.shape
-    heads, kvs, keys = q.shape[0], kv.shape[0] // 2, kv.shape[2]
-    groups, group = rows // chunk, heads // kvs
-    units = kvs * groups
-    line = Gather(
-        size, groups, chunk, own, blocks, (up_send, up_recv, down_send, down_recv, own_sem)
-    )
-    line.load_all()
-    greet(others("tensor", size))
-    line.begin()
-    for h in range(kvs):
-        keys_in_rows[h] = flip(kv[h]).astype(BF)
-
-    def save(g):
-        return pltpu.make_async_copy(full, cot_o.at[pl.ds(g * chunk, chunk)], out_sem)
+            q[h, :, part] = turn(query[h * HD : (h + 1) * HD], cos_t, sin_t).astype(BF)
+
+    def save_cot(g):
+        return pltpu.make_async_copy(full_c, cot_o.at[pl.ds(g * chunk, chunk)], cot_sem)
 
     def join(g):
         @pl.when(g > 0)
         def _():
-            save(g - 1).wait()
+            save_cot(g - 1).wait()
 
         part = pl.ds(pl.multiple_of(g * chunk, chunk), chunk)
-        full[...] = jnp.concatenate([blocks[j, part, :] for j in range(size)], 1)
-        save(g).start()
+        full_c[...] = jnp.concatenate([blocks[j, part, :] for j in range(size)], 1)
+        save_cot(g).start()
+
+    save_kv = pltpu.make_async_copy(kv, kv_o, kv_sem)
+
+    def meet():
+        for g in range(groups):
+            for i in range(contexts - 1):
+                kv_copy(g, i).wait_recv()
+        save_kv.start()
+        for h in range(kvs):
+            keys_in_rows[h] = flip(kv[h]).astype(BF)
 
     def unit(u):
         pair, g = lax.div(u, groups), lax.rem(u, groups)
@@ -1128,55 +1060,105 @@
             mixed_o[pair * group + h, :, part] = (acc[h] / sm[h]).astype(BF)
             lse_o[pair * group + h, :, part] = mx[h] * SCALE2 + jnp.log2(sm[h])
 
+    turnover = line.ticks - 1
+
     def tick(k, _):
-        line.tick(k, join)
-
-        @pl.when(k < units)
-        def _():
-            unit(k)
+        @pl.when(k == turnover)
+        def _():
+            line_c.begin()
+
+        line.tick(k, project)
+
+        @pl.when(k >= turnover)
+        def _():
+            line_c.tick(k - turnover, join)
+
+        u = k - line.ticks
+
+        @pl.when(u == 0)
+        def _():
+            meet()
+
+        @pl.when((u >= 0) & (u < units))
+        def _():
+            unit(u)
 
         return 0
 
-    lax.fori_loop(0, max(line.ticks, units), tick, 0)
-    save(groups - 1).wait()
+    lax.fori_loop(0, max(turnover + line_c.ticks, line.ticks + units), tick, 0)
+    for copy in [*save(groups - 1), save_cot(groups - 1), save_kv]:
+        copy.wait()
+    for i in range(size - 1):
+        gain_copy(i).wait_send()
     line.drain()
-
-
-def attend_forward(size, own, q, kv, kend, chunk):
-    heads, _, rows = q.shape
-    kvs, keys = kv.shape[0] // 2, kv.shape[2]
-    group, width = heads // kvs, own.shape[1]
+    line_c.drain()
+    for g in range(groups):
+        for i in range(contexts - 1):
+            kv_copy(g, i).wait_send()
+
+
+def attend_forward(
+    axes, own, own_cot, gain_pair, cos_tab, sin_tab, mask, starts, w_query, w_key_t, w_value_t, chunk
+):
+    size, contexts = axes["tensor"], axes["context"]
+    rows, width = own.shape
+    features, groups = size * width, rows // chunk
+    heads, kvs = w_query.shape[1] // HD, w_key_t.shape[0] // HD
+    keys, group = contexts * rows, heads // kvs
     key_rows = min(KEY_ROWS_FWD, keys)
     anywhere, vmem = pl.BlockSpec(memory_space=pl.ANY), pl.BlockSpec(memory_space=pltpu.VMEM)
-    shape = jax.ShapeDtypeStruct
+    shape, dma = jax.ShapeDtypeStruct, pltpu.SemaphoreType.DMA
     return pl.pallas_call(
-        functools.partial(attend_kernel, size, chunk, key_rows),
-        in_specs=[anywhere] + [vmem] * 3,
-        out_specs=[anywhere] + [vmem] * 2,
+        functools.partial(attend_kernel, size, contexts, chunk, key_rows),
+        in_specs=[anywhere] * 2 + [vmem] * 5 + [anywhere] * 3,
+        out_specs=[anywhere] * 2 + [vmem] * 3 + [anywhere] + [vmem] * 2 + [anywhere] + [vmem] * 2,
         out_shape=[
-            shape((rows, size * width), BF),
+            shape((rows, features), BF),
+            shape((rows, features), BF),
+            shape((rows, 1), F32),
+            shape((8, features), F32),
+            shape((heads, HD, rows), BF),
+            shape((2 * kvs, HD, keys), BF),
+            shape((1, rows), jnp.int32),
+            shape((rows, 1), F32),
+            shape((rows, features), BF),
             shape((heads, HD, rows), BF),
             shape((heads, 1, rows), F32),
         ],
         scratch_shapes=gather_scratch(size, rows, width, chunk)
+        + gather_scratch(size, rows, width, chunk)
         + [
-            pltpu.VMEM((chunk, size * width), BF),
+            pltpu.VMEM((size, 8, width), F32),
+            pltpu.VMEM((chunk, features), BF),
+            pltpu.VMEM((chunk, features), BF),
+            pltpu.VMEM((chunk, features), BF),
+            pltpu.VMEM((2 * kvs, HD, keys), BF),
+            pltpu.VMEM(w_query.shape, BF),
+            pltpu.VMEM(w_key_t.shape, BF),
+            pltpu.VMEM(w_value_t.shape, BF),
             pltpu.VMEM((kvs, keys, HD), BF),
             pltpu.VMEM((group, HD, chunk), F32),
             pltpu.VMEM((group, 1, chunk), F32),
             pltpu.VMEM((group, 1, chunk), F32),
-            pltpu.SemaphoreType.DMA,
+            dma((size - 1,)),
+            dma((size - 1,)),
+            dma((groups, max(contexts - 1, 1))),
+            dma((groups, max(contexts - 1, 1))),
+            dma((3,)),
+            dma((2,)),
+            dma,
+            dma,
         ],
         compiler_params=pltpu.CompilerParams(
-            collective_id=5, has_side_effects=True, vmem_limit_bytes=VMEM_LIMIT
+            collective_id=3, has_side_effects=True, vmem_limit_bytes=VMEM_LIMIT
         ),
         cost_estimate=pl.CostEstimate(
-            flops=10 * heads * rows * keys * HD,
-            bytes_accessed=16 << 20,
+            flops=2 * rows * features * (heads + 2 * kvs) * HD + 10 * heads * rows * keys * HD,
+            bytes_accessed=40 << 20,
             transcendentals=heads * rows * keys,
         ),
         name="attend_forward",
-    )(own, q, kv, kend)
+    )(own, own_cot, gain_pair, cos_tab, sin_tab, mask, starts, w_query, w_key_t, w_value_t)
 
 
 def attend_back_kernel(
@@ -1205,9 +1187,6 @@
     square_o[...] = jnp.zeros_like(square_o)
     peers = others("context", contexts)
     greet(others("tensor", size) + peers)
-    for h in range(kvs):
-        keys_in_rows[h] = flip(kv[h]).astype(BF)
-        values_in_rows[h] = flip(kv[kvs + h]).astype(BF)
     loads[0].wait()
 
     def half(of):
@@ -1321,6 +1300,12 @@
 
     def tick(k, _):
         line.tick(k)
+
+        @pl.when(k == 0)
+        def _():
+            for h in range(kvs):
+                keys_in_rows[h] = flip(kv[h]).astype(BF)
+                values_in_rows[h] = flip(kv[kvs + h]).astype(BF)
 
         @pl.when(k < units)
         def _():
@@ -1417,7 +1402,7 @@
     w_query, w_key_t, w_value_t, x,
     out_o, sum_o,
     parts, ups, downs, total, up_send, up_recv, down_send, down_recv,
-    xs, wq, wk, wv, dots, dot_sum, cols, cols_in, world, square,
+    xs, whole, wq, wk, wv, dots, dot_sum, cols, cols_in, world, square,
     dot_send, dot_recv, col_send, col_recv, world_send, world_recv, w_sem, x_sem,
 ):
     size = axes["tensor"]
@@ -1462,20 +1447,24 @@
             load_x(c + 1).start()
 
         g = flip(grads[:, part]).astype(BF)
-        whole = (
+        whole[...] = (
             dot_nt(g[:, :nq], wq[...])
             + dot(g[:, nq : nq + nk], wk[...])
             + dot(g[:, nq + nk :], wv[...])
         )
+        for j in range(size):
+            parts[j, part, :] = whole[:, j * width : (j + 1) * width].astype(BF)
+
+    def add_up(c):
+        slot = lax.rem(c, 2)
+        part = pl.ds(pl.multiple_of(c * chunk, chunk), chunk)
         stream = xs[slot].astype(F32)
         square[...] += jnp.sum(stream * stream * keep[part, :], 0, keepdims=True)
-        moved = whole * (stream * inv[part, :])
+        moved = whole[...] * (stream * inv[part, :])
         rowsum = jnp.sum(moved * gain[0:1, :], 1, keepdims=True)
         dots[here, :, part] = jnp.broadcast_to(rowsum, (chunk, 128)).T[:8]
         colsum = jnp.sum(moved, 0, keepdims=True)
-        low = whole.astype(BF)
         for j in range(size):
-            parts[j, part, :] = low[:, j * width : (j + 1) * width]
             piece = jnp.where(row == 0, colsum[:, j * width : (j + 1) * width], 0.0)
 
             @pl.when(c == 0)
@@ -1546,6 +1535,10 @@
 
         line.tick(k)
 
+        @pl.when(k < groups)
+        def _():
+            add_up(k)
+
         @pl.when(k == groups)
         def _():
             exchange()
@@ -1597,6 +1590,7 @@
         scratch_shapes=scatter_scratch(size, rows, width, chunk)
         + [
             pltpu.VMEM((2, chunk, features), BF),
+            pltpu.VMEM((chunk, features), F32),
             pltpu.VMEM(w_query.shape, BF),
             pltpu.VMEM(w_key_t.shape, BF),
             pltpu.VMEM(w_value_t.shape, BF),
@@ -1661,11 +1655,23 @@
     def shard(grad):
         return lax.psum_scatter(grad, ("dp", "context"), scatter_dimension=0, tiled=True)
 
-    x_low, normed_a, inv_a, gains, query_t, both, kend, keep = project(
+    (
+        x_low,
+        normed_a,
+        inv_a,
+        gains,
+        query_t,
+        both,
+        kend,
+        keep,
+        cot,
+        mixed,
+        lse,
+    ) = attend_forward(
         axes,
         x_own,
-        gain_attn[None],
-        gain_mlp[None],
+        cotangent[0],
+        jnp.stack([gain_attn, gain_mlp]),
         cos_tab,
         sin_tab,
         valid_mask,
@@ -1675,7 +1681,6 @@
         w_value_t,
         GROUP_ROWS,
     )
-    cot, mixed, lse = attend_forward(size, cotangent[0], query_t, both, kend, GROUP_ROWS)
     normed_m, act, ggu, down_part, back_part, middle, middle_own, attn_square = feed_forward(
         size,
         mixed.reshape(heads * HD, rows),

time: 768 us -> 763 us (level)
  Pallas kernels: 703 us -> 692 us
    pallas_call x2 -> x1, Pallas kernels: 194 us -> 182 us  [attend_forward(): pl.pallas_call(functools.partial(attend_kernel, size, contexts, chunk, ke...]
  transfers between devices with their start and end apart: 3 -> 3, of which waited for: 0 -> 0; matrix products, arithmetic and copies ran while one was open for 1% -> 1% of each run, Pallas kernels for 44% -> 45%
where the time goes in v6:
time: 763 us; the launch traced here: 753 us
  Pallas kernels  692 us (91%)
  matrix products  26.7 us (3%)
  between operations  15.4 us (2%)
  local copies, waits for them, and re-layouts  12.4 us (2%)
    pallas_call x1, Pallas kernels, attend_forward(): pl.pallas_call(functools.partial(attend_kernel, size, contexts, chunk, ke...  182 us
    pallas_call x1, Pallas kernels, feed_forward(): pl.pallas_call(functools.partial(ffn_kernel, size, hop, chunk), in_specs=...  169 us
    pallas_call x1, Pallas kernels, norm_back(): pl.pallas_call(kernel, in_specs=[vmem] * 3 + [anywhere] * (4 + len(after)...  143 us
    pallas_call x1, Pallas kernels, attend_backward(): pl.pallas_call(kernel, in_specs=[anywhere] + [vmem] * 9 + [anywhere] * (2...  100 us
    pallas_call x1, Pallas kernels, input_gradient(): pl.pallas_call(kernel, in_specs=[vmem] * 10 + [anywhere] * (4 + len(after...  96.6 us
    dot_general x1, matrix products, ein(): return jnp.einsum(spec, a, b, preferred_element_type=F32)  26.7 us
  transfers between devices with their start and end apart: 3, of which 0 were waited for; matrix products, arithmetic and copies ran while one was open for 1% of the time, Pallas kernels for 45%

profile of v6, /device:TPU:0, one launch (start us, length us, event | category | flops | bytes accessed | tf_op | source)
XLA Modules:
  0.0 753.1 jit_solution(9328506402084710021)
XLA Ops:
  7.2 0.7 stack.9.refs_7_
  7.9 0.7 stack.10
  8.6 0.6 pad_maximum_fusion.gain_pair
  9.2 1.4 multiply_sine_fusion
  10.6 182.3 %attend_forward.1 = (bf16[1024,2560]{1,0:T(8,128)(2,1)}, bf16[1024,2560]{1,0:T(8,128)(2,1)}, f32[1024,1]{1,0:T(8,128)}, f32[8,2560]{1,0:T(8,128)}, bf16[8,80,102...) custom-call(bf16[1024,640]{1,0:T(8,128)(2,1)} %bitcast.21, ...), custom_call_target="tpu_custom_call" | custom-call | flops 18454937600 | bytes 41943040 | tf_op jit(solution)/shard_map/attend_forward/pallas_call | solution.py:1111
  192.9 169.3 %feed_forward.1 = (bf16[1024,2560]{1,0:T(8,128)(2,1)}, bf16[1024,1792]{1,0:T(8,128)(2,1)}, bf16[1024,3584]{1,0:T(8,128)(2,1)}, bf16[4,1024,640]{2,1,0:T(8,128)(2...) custom-call(bf16[640,1024]{1,0:T(8,128)(2,1)} %bitcast.30, ...), custom_call_target="tpu_custom_call" | custom-call | flops 59726888960 | bytes 83886080 | tf_op jit(solution)/shard_map/feed_forward/pallas_call | solution.py:429
  362.2 26.7 %convolution_convert_fusion.refs_7_ = bf16[2560,3584]{1,0:T(8,128)(2,1)} fusion(bf16[1024,2560]{1,0:T(8,128)(2,1)} %get-tuple-element.56, bf16[1024,3584]{1,0:T(8,128)(2,1)} %get-tuple-element.57), kind=kOutput, calls=%fused_computation | convolution fusion | flops 18799656960 | bytes 30932992 | tf_op jit(solution)/shard_map/sd,sf->df/dot_general | solution.py:38
  389.0 0.0 reduce-scatter.6.cloned.1.call-start
  389.1 143.4 %norm_back.1 = (f32[1024,640]{1,0:T(8,128)}, bf16[1024,2560]{1,0:T(8,128)(2,1)}, bf16[640,1024]{1,0:T(8,128)(2,1)}, f32[1,2560]{1,0:T(1,128)}, bf16[2560,1792]{1,0:T(8,128)(2,1)}) custom-call(bf16[1024,2560]{1,0:T(8,128)(2,1)} %get-tuple-element.53.refs_0_, f32[1024,1]{1,0:T(8,128)} %get-tuple-element.45.keep.refs_1_.refs_3_, ...), custom_call_target="tpu_custom_call" | custom-call | flops 12750684160 | bytes 41943040 | tf_op jit(solution)/shard_map/norm_back/pallas_call | solution.py:624
  532.5 100.0 %attend_backward.1 = (bf16[12,80,1024]{2,1,0:T(8,128)(2,1)}, bf16[1024,640]{1,0:T(8,128)(2,1)}, f32[1,640]{1,0:T(1,128)}, bf16[2560,1600]{1,0:T(8,128)(2,1)}) custom-call(bf16[4,1024,640]{2,1,0:T(8,128)(2,1)} %get-tuple-element.49.refs_0_, bf16[8,80,1024]{2,1,0:T(8,128)(2,1)} %get-tuple-element.50.refs_1_, bf16[4,80,2048]{2,1,0:T(8,128)(2,1)} %get-tuple-element.51.refs_2_, ...), custom_call_target="tpu_custom_call" | custom-call | flops 21474836480 | bytes 16777216 | tf_op jit(solution)/shard_map/attend_backward/pallas_call | solution.py:1355
  632.6 2.8 convert_bitcast_fusion
  635.4 96.6 %input_gradient.1 = (bf16[1024,640]{1,0:T(8,128)(2,1)}, f32[8,640]{1,0:T(8,128)}) custom-call(bf16[960,1024]{1,0:T(8,128)(2,1)} %bitcast.20, f32[1024,1]{1,0:T(8,128)} %get-tuple-element.65.refs_1_, f32[8,2560]{1,0:T(8,128)} %get-tuple-element.46.gain.refs_2_, f32[1024,1]{1,0:T(8,128)} %get-tuple-element.45.keep.refs_1_.refs_3_, ...), custom_call_target="tpu_custom_call" | custom-call | flops 5033164800 | bytes 20971520 | tf_op jit(solution)/shard_map/input_gradient/pallas_call | solution.py:1582
  732.0 1.3 slice.26
  734.6 0.7 divide_sqrt_fusion
  735.3 0.6 fusion.2
  735.9 1.4 slice_reduce_fusion
  737.3 2.5 fusion
  739.8 1.4 convert_select_fusion
  741.1 0.2 fusion.1
  741.3 1.3 slice_bitcast_fusion
  742.6 0.8 copy.28
  743.4 0.8 copy.27
  744.3 1.1 copy.31
  745.3 1.1 copy.32
  (18 shorter events, 0.2 us)
Async XLA Ops:
  7.2 525.3 %reduce-scatter.4.cloned.1.call-start = ((), (), s32[]{:S(2)}) async-start(), calls=%async_computation.3 | async-start | bytes 20643840 | tf_op jit(solution)/shard_map/reduce_scatter | solution.py:1656
  7.9 185.0 %copy-start.3 = (f32[1,640]{1,0:T(1,128)}, f32[1,640]{1,0:T(1,128)S(1)}, u32[]{:S(2)}) copy-start(f32[1,640]{1,0:T(1,128)S(1)} %stack.9.refs_7_) | copy-start | bytes 7684
  389.0 243.6 %reduce-scatter.6.cloned.1.call-start = ((), (), s32[]{:S(2)}) async-start(), calls=%async_computation.4 | async-start | bytes 10321920 | tf_op jit(solution)/shard_map/reduce_scatter | solution.py:1656
  532.4 207.3 %reduce-scatter.8.cloned.1.call-start = ((), (), s32[]{:S(2)}) async-start(), calls=%async_computation.5 | async-start | bytes 9584640 | tf_op jit(solution)/shard_map/reduce_scatter | solution.py:1656
  635.4 101.9 %copy-start = (bf16[320,3584]{1,0:T(8,128)(2,1)S(1)}, bf16[320,3584]{1,0:T(8,128)(2,1)}, u32[]{:S(2)}) copy-start(bf16[320,3584]{1,0:T(8,128)(2,1)} %reduce-scatter.4.cloned.1.call-done.refs_12_) | copy-start | bytes 6881284
  741.3 3.0 copy-start.1
  742.6 2.7 copy-start.2
Sparse Core Ops, SparseCore 0:
  389.1 122.2 reduce-scatter.3
  532.6 84.3 reduce-scatter.5
  632.7 71.1 reduce-scatter.7

commit v7 on v6

--- a/solution.py
+++ b/solution.py
@@ -50,9 +50,15 @@
     return (a.astype(F32) + b.astype(F32)).astype(BF)
 
 
+def partner(replicas):
+    spot = lax.axis_index("dp")
+    return [] if replicas % 2 else [{"dp": spot + 1 - 2 * lax.rem(spot, 2)}]
+
+
 class Sums:
-    def __init__(self, size, count, part, low, high, sent, sems):
-        self.size, self.count, self.part = size, count, part
+    def __init__(self, axes, count, part, low, high, sent, sems):
+        self.size, self.count, self.part = axes["tensor"], count, part
+        self.replicas = axes["dp"]
         self.low, self.high, self.sent = low, high, sent
         self.low_send, self.low_recv, self.high_send, self.high_recv = sems
         self.here = lax.axis_index("tensor")
@@ -60,6 +66,9 @@
     def barrier(self):
         here, size = self.here, self.size
         barrier = pltpu.get_barrier_semaphore()
+        pair = partner(self.replicas)
+        for peer in pair:
+            pl.semaphore_signal(barrier, inc=1, device_id=peer, device_id_type=MESH_ID)
 
         @pl.when(here > 0)
         def _():
@@ -75,11 +84,11 @@
 
         @pl.when((here > 0) & (here < size - 1))
         def _():
-            pl.semaphore_wait(barrier, 2)
+            pl.semaphore_wait(barrier, 2 + len(pair))
 
         @pl.when((here == 0) | (here == size - 1))
         def _():
-            pl.semaphore_wait(barrier, 1)
+            pl.semaphore_wait(barrier, 1 + len(pair))
 
     def up(self, c):
         slot = lax.rem(c, ring_of(self.size))
@@ -198,13 +207,14 @@
 
 
 def ffn_kernel(
-    size, hop, chunk,
+    axes, hop, chunk,
     mixed, keep, gain, w_out, w_gate, w_up, w_down, x, cot,
     normed_o, act_o, ggu_o, ffn_o, back_o, middle_o, own_o, square_o,
     low, high, sent, low_send, low_recv, high_send, high_recv,
     wo, wg, wu, wd, parts, normed, xs, cots, mids, owns, act, ggu, ffn, back, split,
     w_sem, x_sem, cot_sem, normed_sem, mid_sem, own_sem, act_sem, ffn_sem,
 ):
+    size = axes["tensor"]
     rows, features = x.shape
     hidden = w_gate.shape[1]
     count, per, groups = rows // hop, chunk // hop, rows // chunk
@@ -219,7 +229,7 @@
         slot = lax.rem(lax.div(c, per), part_slots)
         return parts[slot, pl.ds(pl.multiple_of(lax.rem(c, per) * hop, hop), hop), :]
 
-    sums = Sums(size, count, part, low, high, sent, (low_send, low_recv, high_send, high_recv))
+    sums = Sums(axes, count, part, low, high, sent, (low_send, low_recv, high_send, high_recv))
     loads = [
         pltpu.make_async_copy(a, b, w_sem.at[i])
         for i, (a, b) in enumerate(((w_out, wo), (w_gate, wg), (w_up, wu), (w_down, wd)))
@@ -420,14 +430,15 @@
         save_normed(c).wait()
 
 
-def feed_forward(size, mixed, keep, gain, w_out, w_gate, w_up, w_down, x, cot, chunk, hop):
+def feed_forward(axes, mixed, keep, gain, w_out, w_gate, w_up, w_down, x, cot, chunk, hop):
+    size = axes["tensor"]
     rows, features = x.shape
     hidden = w_gate.shape[1]
     per = chunk // hop
     anywhere, vmem = pl.BlockSpec(memory_space=pl.ANY), pl.BlockSpec(memory_space=pltpu.VMEM)
     shape = jax.ShapeDtypeStruct
     return pl.pallas_call(
-        functools.partial(ffn_kernel, size, hop, chunk),
+        functools.partial(ffn_kernel, axes, hop, chunk),
         in_specs=[vmem] * 3 + [anywhere] * 6,
         out_specs=[anywhere] * 7 + [vmem],
         out_shape=[
@@ -479,13 +490,14 @@
 
 
 def back_kernel(
-    size, hop, chunk,
+    axes, hop, chunk,
     parts, keep, gain, w_out, middle, cot, act,
     own_o, grad_low_o, mixed_o, gain_o, down_o,
     low, high, sent, low_send, low_recv, high_send, high_recv,
     wo, mids, cots, acts, owns, grads_low, tiles,
     load_sem, mid_sem, own_sem, grad_low_sem, tile_sem,
 ):
+    size = axes["tensor"]
     rows, features = middle.shape
     count, per, groups = rows // hop, chunk // hop, rows // chunk
     tile = tile_of(features, 256)
@@ -495,7 +507,7 @@
     def part(c):
         return parts[pl.ds(pl.multiple_of(c * hop, hop), hop), :]
 
-    sums = Sums(size, count, part, low, high, sent, (low_send, low_recv, high_send, high_recv))
+    sums = Sums(axes, count, part, low, high, sent, (low_send, low_recv, high_send, high_recv))
     loads = [
         pltpu.make_async_copy(a, b, load_sem.at[i])
         for i, (a, b) in enumerate(((cot, cots), (w_out, wo), (act, acts)))
@@ -612,14 +624,15 @@
         save_tile(j).wait()
 
 
-def norm_back(size, parts, keep, gain, w_out, middle, cot, act, chunk, hop, after):
+def norm_back(axes, parts, keep, gain, w_out, middle, cot, act, chunk, hop, after):
+    size = axes["tensor"]
     rows, features = middle.shape
     per = chunk // hop
     anywhere, vmem = pl.BlockSpec(memory_space=pl.ANY), pl.BlockSpec(memory_space=pltpu.VMEM)
     shape, dma = jax.ShapeDtypeStruct, pltpu.SemaphoreType.DMA
 
     def kernel(*refs):
-        back_kernel(size, hop, chunk, *refs[:7], *refs[7 + len(after) :])
+        back_kernel(axes, hop, chunk, *refs[:7], *refs[7 + len(after) :])
 
     return pl.pallas_call(
         kernel,
@@ -826,35 +839,45 @@
                 self.downs[n] = add_low(self.downs[n], self.parts[below, self.rows(n), :])
                 self.down(n, False).start()
 
-    def finish(self, total, then):
-        here = self.here
+    def close(self, c, total, then):
+        here, part = self.here, self.rows(c)
+        m, n = (self.size - 1 - here) * self.groups + c, here * self.groups + c
+        total[...] = self.parts[here, part, :].astype(F32)
+
+        @pl.when(here > 0)
+        def _():
+            self.up(m, False).wait_recv()
+            total[...] += self.ups[m].astype(F32)
+
+        @pl.when(here < self.size - 1)
+        def _():
+            self.down(n, False).wait_recv()
+            total[...] += self.downs[n].astype(F32)
+
+        then(part, total[...])
+
+    def close_early(self, k, total, then):
+        c = k - (self.count - self.groups + 2)
+
+        @pl.when((c >= 0) & (c < self.groups) & (k < self.count))
+        def _():
+            self.close(c, total, then)
+
+    def finish(self, ticks, total, then):
+        done = min(max(min(ticks, self.count) - (self.count - self.groups + 2), 0), self.groups)
 
         def last(c, _):
-            part = self.rows(c)
-            m, n = (self.size - 1 - here) * self.groups + c, here * self.groups + c
-            total[...] = self.parts[here, part, :].astype(F32)
-
-            @pl.when(here > 0)
-            def _():
-                self.up(m, False).wait_recv()
-                total[...] += self.ups[m].astype(F32)
-
-            @pl.when(here < self.size - 1)
-            def _():
-                self.down(n, False).wait_recv()
-                total[...] += self.downs[n].astype(F32)
-
-            then(part, total[...])
+            self.close(c, total, then)
             return 0
 
-        lax.fori_loop(0, self.groups, last, 0)
+        lax.fori_loop(done, self.groups, last, 0)
 
         def drain(m, _):
-            @pl.when(self.size - 1 - lax.div(m, self.groups) > here)
+            @pl.when(self.size - 1 - lax.div(m, self.groups) > self.here)
             def _():
                 self.up(m, False).wait_send()
 
-            @pl.when(lax.div(m, self.groups) < here)
+            @pl.when(lax.div(m, self.groups) < self.here)
             def _():
                 self.down(m, False).wait_send()
 
@@ -890,7 +913,7 @@
 
 
 def attend_kernel(
-    size, contexts, chunk, key_rows,
+    axes, chunk, key_rows,
     own, own_cot, gain_pair, cos_tab, sin_tab, mask, starts, w_query, w_key_t, w_value_t,
     x_o, normed_o, inv_o, gain_o, q, kv_o, kend, keep_o, cot_o, mixed_o, lse_o,
     xs, up_send, up_recv, down_send, down_recv, own_sem,
@@ -898,6 +921,7 @@
     gains, full, normed, full_c, kv, wq, wk, wv, keys_in_rows, acc, mx, sm,
     gain_send, gain_recv, kv_send, kv_recv, w_sem, out_sem, kv_sem, cot_sem,
 ):
+    size, contexts = axes["tensor"], axes["context"]
     here, place = lax.axis_index("tensor"), lax.axis_index("context")
     rows, width = own.shape
     features = size * width
@@ -922,7 +946,7 @@
     gains[here] = jnp.zeros_like(gains[here])
     gains[here, 0:2] = gain_pair[...]
     tensor_peers, context_peers = others("tensor", size), others("context", contexts)
-    greet(tensor_peers + context_peers)
+    greet(tensor_peers + context_peers + partner(axes["dp"]))
 
     def gain_copy(i):
         return pltpu.make_async_remote_copy(
@@ -1109,7 +1133,7 @@
     anywhere, vmem = pl.BlockSpec(memory_space=pl.ANY), pl.BlockSpec(memory_space=pltpu.VMEM)
     shape, dma = jax.ShapeDtypeStruct, pltpu.SemaphoreType.DMA
     return pl.pallas_call(
-        functools.partial(attend_kernel, size, contexts, chunk, key_rows),
+        functools.partial(attend_kernel, axes, chunk, key_rows),
         in_specs=[anywhere] * 2 + [vmem] * 5 + [anywhere] * 3,
         out_specs=[anywhere] * 2 + [vmem] * 3 + [anywhere] + [vmem] * 2 + [anywhere] + [vmem] * 2,
         out_shape=[
@@ -1162,7 +1186,7 @@
 
 
 def attend_back_kernel(
-    size, contexts, chunk, key_rows,
+    axes, chunk, key_rows,
     ffn, q, kv, kend, do, o, lse, cos_tab, sin_tab, middle, grad_attn, normed,
     grads_o, layer_o, square_o, weights_o,
     parts, ups, downs, total, up_send, up_recv, down_send, down_recv,
@@ -1170,6 +1194,7 @@
     grads_in, normed_in, tiles,
     kv_send, kv_recv, part_sem, tile_sem,
 ):
+    size, contexts = axes["tensor"], axes["context"]
     heads, _, rows = q.shape
     kvs, keys = kv.shape[0] // 2, kv.shape[2]
     groups, group = rows // chunk, heads // kvs
@@ -1186,7 +1211,7 @@
         load.start()
     square_o[...] = jnp.zeros_like(square_o)
     peers = others("context", contexts)
-    greet(others("tensor", size) + peers)
+    greet(others("tensor", size) + peers + partner(axes["dp"]))
     loads[0].wait()
 
     def half(of):
@@ -1298,6 +1323,10 @@
         tiles[slot] = jnp.concatenate([out, into], 1).astype(BF)
         save_tile(j).start()
 
+    def then(part, ffn_out):
+        square_o[...] += jnp.sum(ffn_out * ffn_out, 0, keepdims=True)
+        layer_o[part, :] = (middle[part, :] + ffn_out).astype(BF)
+
     def tick(k, _):
         line.tick(k)
 
@@ -1324,15 +1353,13 @@
             def _():
                 weight_tile(first + j)
 
+        line.close_early(k, total, then)
         return 0
 
-    lax.fori_loop(0, max(line.count, units + 1 + -(-tile_count // each)), tick, 0)
-
-    def then(part, ffn_out):
-        square_o[...] += jnp.sum(ffn_out * ffn_out, 0, keepdims=True)
-        layer_o[part, :] = (middle[part, :] + ffn_out).astype(BF)
-
-    line.finish(total, then)
+    ticks = max(line.count, units + 1 + -(-tile_count // each))
+    lax.fori_loop(0, ticks, tick, 0)
+
+    line.finish(ticks, total, then)
     for j in range(max(tile_count - 2, 0), tile_count):
         save_tile(j).wait()
 
@@ -1350,7 +1377,7 @@
     slots = max(contexts - 1, 1)
 
     def kernel(*refs):
-        attend_back_kernel(size, contexts, chunk, key_rows, *refs[:12], *refs[12 + len(after) :])
+        attend_back_kernel(axes, chunk, key_rows, *refs[:12], *refs[12 + len(after) :])
 
     return pl.pallas_call(
         kernel,
@@ -1528,36 +1555,38 @@
         for i in range(replicas - 1):
             world_copy(i).start()
 
-    def tick(k, _):
-        @pl.when(k < groups)
-        def _():
-            compute(k)
-
-        line.tick(k)
-
-        @pl.when(k < groups)
-        def _():
-            add_up(k)
-
-        @pl.when(k == groups)
-        def _():
-            exchange()
-
-        @pl.when(k == groups + 3)
-        def _():
-            spread()
-
-        return 0
-
-    lax.fori_loop(0, max(line.count, groups + 4), tick, 0)
-
     def then(part, grad):
         through = grad * gain_own[...] - x_own[part, :].astype(F32) * inv[part, :] * (
             dot_sum[:, part].T[:, :1] / features
         )
         out_o[part, :] = (grad_own[part, :] + inv[part, :] * through).astype(BF)
 
-    line.finish(total, then)
+    def tick(k, _):
+        @pl.when(k < groups)
+        def _():
+            compute(k)
+
+        line.tick(k)
+
+        @pl.when(k < groups)
+        def _():
+            add_up(k)
+
+        @pl.when(k == groups)
+        def _():
+            exchange()
+
+        @pl.when(k == groups + 3)
+        def _():
+            spread()
+
+        line.close_early(k, total, then)
+        return 0
+
+    ticks = max(line.count, groups + 4)
+    lax.fori_loop(0, ticks, tick, 0)
+
+    line.finish(ticks, total, then)
     for i in range(replicas - 1):
         world_copy(i).wait()
     everything = world[0]
@@ -1682,7 +1711,7 @@
         GROUP_ROWS,
     )
     normed_m, act, ggu, down_part, back_part, middle, middle_own, attn_square = feed_forward(
-        size,
+        axes,
         mixed.reshape(heads * HD, rows),
         keep,
         gains,
@@ -1699,7 +1728,7 @@
     ggu_sum = shard(grad_ggu)
 
     grad_own, grad_attn, grad_mixed, gain_m_rows, grad_down = norm_back(
-        size, back_part, keep, gains, w_out, middle, cot, act, GROUP_ROWS, HOP_ROWS, (grad_ggu,)
+        axes, back_part, keep, gains, w_out, middle, cot, act, GROUP_ROWS, HOP_ROWS, (grad_ggu,)
     )
     down_sum = shard(grad_down)
     grads, layer_out, ffn_square, grad_rest = attend_backward(

time: 763 us -> 772 us (1.012)
  Pallas kernels: 692 us -> 703 us
  transfers between devices with their start and end apart: 3 -> 3, of which waited for: 0 -> 0; matrix products, arithmetic and copies ran while one was open for 1% -> 1% of each run, Pallas kernels for 45% -> 46%
where the time goes in v7:
time: 772 us; the launch traced here: 764 us
  Pallas kernels  703 us (91%)
  matrix products  26.7 us (3%)
  between operations  15.4 us (2%)
  local copies, waits for them, and re-layouts  12.4 us (2%)
    pallas_call x1, Pallas kernels, attend_forward(): pl.pallas_call(functools.partial(attend_kernel, axes, chunk, key_rows), i...  182 us
    pallas_call x1, Pallas kernels, feed_forward(): pl.pallas_call(functools.partial(ffn_kernel, axes, hop, chunk), in_specs=...  171 us
    pallas_call x1, Pallas kernels, norm_back(): pl.pallas_call(kernel, in_specs=[vmem] * 3 + [anywhere] * (4 + len(after)...  144 us
    pallas_call x1, Pallas kernels, attend_backward(): pl.pallas_call(kernel, in_specs=[anywhere] + [vmem] * 9 + [anywhere] * (2...  108 us
    pallas_call x1, Pallas kernels, input_gradient(): pl.pallas_call(kernel, in_specs=[vmem] * 10 + [anywhere] * (4 + len(after...  98.1 us
    dot_general x1, matrix products, ein(): return jnp.einsum(spec, a, b, preferred_element_type=F32)  26.7 us
  transfers between devices with their start and end apart: 3, of which 0 were waited for; matrix products, arithmetic and copies ran while one was open for 1% of the time, Pallas kernels for 46%

profile of v7, /device:TPU:0, one launch (start us, length us, event | category | flops | bytes accessed | tf_op | source)
XLA Modules:
  0.0 764.4 jit_solution(12426289828716320373)
XLA Ops:
  7.2 0.7 stack.9.refs_7_
  7.9 0.7 stack.10
  8.6 0.6 pad_maximum_fusion.gain_pair
  9.2 1.4 multiply_sine_fusion
  10.6 182.3 %attend_forward.1 = (bf16[1024,2560]{1,0:T(8,128)(2,1)}, bf16[1024,2560]{1,0:T(8,128)(2,1)}, f32[1024,1]{1,0:T(8,128)}, f32[8,2560]{1,0:T(8,128)}, bf16[8,80,102...) custom-call(bf16[1024,640]{1,0:T(8,128)(2,1)} %bitcast.21, ...), custom_call_target="tpu_custom_call" | custom-call | flops 18454937600 | bytes 41943040 | tf_op jit(solution)/shard_map/attend_forward/pallas_call | solution.py:1135
  192.9 171.3 %feed_forward.1 = (bf16[1024,2560]{1,0:T(8,128)(2,1)}, bf16[1024,1792]{1,0:T(8,128)(2,1)}, bf16[1024,3584]{1,0:T(8,128)(2,1)}, bf16[4,1024,640]{2,1,0:T(8,128)(2...) custom-call(bf16[640,1024]{1,0:T(8,128)(2,1)} %bitcast.30, ...), custom_call_target="tpu_custom_call" | custom-call | flops 59726888960 | bytes 83886080 | tf_op jit(solution)/shard_map/feed_forward/pallas_call | solution.py:440
  364.2 26.7 %convolution_convert_fusion.refs_7_ = bf16[2560,3584]{1,0:T(8,128)(2,1)} fusion(bf16[1024,2560]{1,0:T(8,128)(2,1)} %get-tuple-element.56, bf16[1024,3584]{1,0:T(8,128)(2,1)} %get-tuple-element.57), kind=kOutput, calls=%fused_computation | convolution fusion | flops 18799656960 | bytes 30932992 | tf_op jit(solution)/shard_map/sd,sf->df/dot_general | solution.py:38
  391.0 0.0 reduce-scatter.6.cloned.1.call-start
  391.0 143.5 %norm_back.1 = (f32[1024,640]{1,0:T(8,128)}, bf16[1024,2560]{1,0:T(8,128)(2,1)}, bf16[640,1024]{1,0:T(8,128)(2,1)}, f32[1,2560]{1,0:T(1,128)}, bf16[2560,1792]{1,0:T(8,128)(2,1)}) custom-call(bf16[1024,2560]{1,0:T(8,128)(2,1)} %get-tuple-element.53.refs_0_, f32[1024,1]{1,0:T(8,128)} %get-tuple-element.45.keep.refs_1_.refs_3_, ...), custom_call_target="tpu_custom_call" | custom-call | flops 12750684160 | bytes 41943040 | tf_op jit(solution)/shard_map/norm_back/pallas_call | solution.py:637
  534.7 107.6 %attend_backward.1 = (bf16[12,80,1024]{2,1,0:T(8,128)(2,1)}, bf16[1024,640]{1,0:T(8,128)(2,1)}, f32[1,640]{1,0:T(1,128)}, bf16[2560,1600]{1,0:T(8,128)(2,1)}) custom-call(bf16[4,1024,640]{2,1,0:T(8,128)(2,1)} %get-tuple-element.49.refs_0_, bf16[8,80,1024]{2,1,0:T(8,128)(2,1)} %get-tuple-element.50.refs_1_, bf16[4,80,2048]{2,1,0:T(8,128)(2,1)} %get-tuple-element.51.refs_2_, ...), custom_call_target="tpu_custom_call" | custom-call | flops 21474836480 | bytes 16777216 | tf_op jit(solution)/shard_map/attend_backward/pallas_call | solution.py:1382
  642.3 2.8 convert_bitcast_fusion
  645.1 98.1 %input_gradient.1 = (bf16[1024,640]{1,0:T(8,128)(2,1)}, f32[8,640]{1,0:T(8,128)}) custom-call(bf16[960,1024]{1,0:T(8,128)(2,1)} %bitcast.20, f32[1024,1]{1,0:T(8,128)} %get-tuple-element.65.refs_1_, f32[8,2560]{1,0:T(8,128)} %get-tuple-element.46.gain.refs_2_, f32[1024,1]{1,0:T(8,128)} %get-tuple-element.45.keep.refs_1_.refs_3_, ...), custom_call_target="tpu_custom_call" | custom-call | flops 5033164800 | bytes 20971520 | tf_op jit(solution)/shard_map/input_gradient/pallas_call | solution.py:1611
  743.2 1.3 slice.26
  745.8 0.7 divide_sqrt_fusion
  746.5 0.6 fusion.2
  747.1 1.4 slice_reduce_fusion
  748.5 2.5 fusion
  751.0 1.4 convert_select_fusion
  752.4 0.2 fusion.1
  752.5 1.3 slice_bitcast_fusion
  753.8 0.8 copy.28
  754.6 0.8 copy.27
  755.5 1.1 copy.31
  756.5 1.1 copy.32
  (18 shorter events, 0.2 us)
Async XLA Ops:
  7.2 527.5 %reduce-scatter.4.cloned.1.call-start = ((), (), s32[]{:S(2)}) async-start(), calls=%async_computation.3 | async-start | bytes 20643840 | tf_op jit(solution)/shard_map/reduce_scatter | solution.py:1685
  7.9 185.0 %copy-start.3 = (f32[1,640]{1,0:T(1,128)}, f32[1,640]{1,0:T(1,128)S(1)}, u32[]{:S(2)}) copy-start(f32[1,640]{1,0:T(1,128)S(1)} %stack.9.refs_7_) | copy-start | bytes 7684
  391.0 251.3 %reduce-scatter.6.cloned.1.call-start = ((), (), s32[]{:S(2)}) async-start(), calls=%async_computation.4 | async-start | bytes 10321920 | tf_op jit(solution)/shard_map/reduce_scatter | solution.py:1685
  534.6 216.4 %reduce-scatter.8.cloned.1.call-start = ((), (), s32[]{:S(2)}) async-start(), calls=%async_computation.5 | async-start | bytes 9584640 | tf_op jit(solution)/shard_map/reduce_scatter | solution.py:1685
  645.1 103.4 %copy-start = (bf16[320,3584]{1,0:T(8,128)(2,1)S(1)}, bf16[320,3584]{1,0:T(8,128)(2,1)}, u32[]{:S(2)}) copy-start(bf16[320,3584]{1,0:T(8,128)(2,1)} %reduce-scatter.4.cloned.1.call-done.refs_12_) | copy-start | bytes 6881284
  752.5 3.0 copy-start.1
  753.8 2.7 copy-start.2
Sparse Core Ops, SparseCore 0:
  391.1 122.6 reduce-scatter.3
  534.7 93.0 reduce-scatter.5
  642.4 73.1 reduce-scatter.7

commit v8 on v6

--- a/solution.py
+++ b/solution.py
@@ -19,7 +19,7 @@
 GROUP_ROWS = 256
 HOP_ROWS = 64
 VMEM_LIMIT = 60 << 20
-KEY_ROWS_FWD = 1024
+KEY_ROWS_FWD = 512
 KEY_ROWS_BWD = 512
 
 epsilon = 1e-05
@@ -155,17 +155,10 @@
         def _():
             self.down(d - 2).wait_send()
 
-    def total(self, c, then):
+    def total(self, c):
         slot = lax.rem(c, ring_of(self.size))
-        top = self.here == self.size - 1
-
-        @pl.when(top)
-        def _():
-            then(self.low[slot].astype(F32))
-
-        @pl.when(jnp.logical_not(top))
-        def _():
-            then(self.low[slot].astype(F32) + self.high[slot].astype(F32))
+        high = jnp.where(self.here == self.size - 1, 0.0, self.high[slot].astype(F32))
+        return self.low[slot].astype(F32) + high
 
 
 def sum_scratch(size, hop, features):
@@ -300,12 +293,9 @@
 
         kept = keep[pl.ds(pl.multiple_of(c * hop, hop), hop), :]
 
-        def then(total):
-            out = kept * total
-            square_o[...] += jnp.sum(out * out, 0, keepdims=True)
-            mids[slot] = xs[slot].astype(F32) + out
-
-        sums.total(c, then)
+        out = kept * sums.total(c)
+        square_o[...] += jnp.sum(out * out, 0, keepdims=True)
+        mids[slot] = xs[slot].astype(F32) + out
         mid = mids[slot]
         own_columns(size, mid, lambda piece: owns.__setitem__(slot, piece))
         save_own(c).start()
@@ -365,7 +355,9 @@
         g, stage = lax.div(s, per), lax.rem(s, per)
         going = (s >= 0) & (g < groups)
 
-        @pl.when(going & (stage == 0 * per // 4))
+        first, second, third, fourth = (stage == i * per // 4 for i in range(4))
+
+        @pl.when(going & first)
         def _():
             @pl.when(g == 0)
             def _():
@@ -379,11 +371,12 @@
                 for copy in save_act(g - 1):
                     copy.wait()
 
-            inner(g, 0, half_f)
-
-        @pl.when(going & (stage == 1 * per // 4))
-        def _():
-            inner(g, half_f, tiles_f)
+        @pl.when(going & (first | second))
+        def _():
+            inner(g, jnp.where(first, 0, half_f), jnp.where(first, half_f, tiles_f))
+
+        @pl.when(going & second)
+        def _():
             for copy in save_act(g):
                 copy.start()
 
@@ -391,18 +384,17 @@
             def _():
                 load_cot(g + 1).start()
 
-        @pl.when(going & (stage == 2 * per // 4))
-        def _():
-            @pl.when(g > 0)
-            def _():
-                for copy in save_ffn(g - 1):
-                    copy.wait()
-
-            outer(g, 0, half_d)
-
-        @pl.when(going & (stage == 3 * per // 4))
-        def _():
-            outer(g, half_d, tiles_d)
+        @pl.when(going & third & (g > 0))
+        def _():
+            for copy in save_ffn(g - 1):
+                copy.wait()
+
+        @pl.when(going & (third | fourth))
+        def _():
+            outer(g, jnp.where(third, 0, half_d), jnp.where(third, half_d, tiles_d))
+
+        @pl.when(going & fourth)
+        def _():
             for j in range(size):
                 split[j] = ffn[:, j * (features // size) : (j + 1) * (features // size)]
             for copy in save_ffn(g):
@@ -551,13 +543,11 @@
         inv = lax.rsqrt(jnp.sum(mid * mid, 1, keepdims=True) / features + epsilon)
         hat = mid * inv
 
-        def then(total):
-            gain_o[...] += jnp.sum(total * hat, 0, keepdims=True)
-            weighted = total * gain[1:2, :]
-            mean = jnp.sum(weighted * hat, 1, keepdims=True) / features
-            mids[slot] = cots[chunk_rows, :].astype(F32) + inv * (weighted - hat * mean)
-
-        sums.total(c, then)
+        total = sums.total(c)
+        gain_o[...] += jnp.sum(total * hat, 0, keepdims=True)
+        weighted = total * gain[1:2, :]
+        mean = jnp.sum(weighted * hat, 1, keepdims=True) / features
+        mids[slot] = cots[chunk_rows, :].astype(F32) + inv * (weighted - hat * mean)
         grad = mids[slot]
         own_columns(size, grad, lambda piece: owns.__setitem__(slot, piece))
         grads_low[pl.ds(pl.multiple_of(lax.rem(c, per) * hop, hop), hop), :] = (kept * grad).astype(

time: 763 us -> 755 us (0.990)
  no operation moved by 1% of the time
where the time goes in v8:
time: 755 us; the launch traced here: 747 us
  Pallas kernels  685 us (91%)
  matrix products  26.9 us (4%)
  between operations  15.6 us (2%)
  local copies, waits for them, and re-layouts  12.4 us (2%)
    pallas_call x1, Pallas kernels, attend_forward(): pl.pallas_call(functools.partial(attend_kernel, size, contexts, chunk, ke...  182 us
    pallas_call x1, Pallas kernels, feed_forward(): pl.pallas_call(functools.partial(ffn_kernel, size, hop, chunk), in_specs=...  169 us
    pallas_call x1, Pallas kernels, norm_back(): pl.pallas_call(kernel, in_specs=[vmem] * 3 + [anywhere] * (4 + len(after)...  140 us
    pallas_call x1, Pallas kernels, input_gradient(): pl.pallas_call(kernel, in_specs=[vmem] * 10 + [anywhere] * (4 + len(after...  97.2 us
    pallas_call x1, Pallas kernels, attend_backward(): pl.pallas_call(kernel, in_specs=[anywhere] + [vmem] * 9 + [anywhere] * (2...  97 us
    dot_general x1, matrix products, ein(): return jnp.einsum(spec, a, b, preferred_element_type=F32)  26.9 us
  transfers between devices with their start and end apart: 3, of which 0 were waited for; matrix products, arithmetic and copies ran while one was open for 1% of the time, Pallas kernels for 45%

profile of v8, /device:TPU:0, one launch (start us, length us, event | category | flops | bytes accessed | tf_op | source)
XLA Modules:
  0.0 746.8 jit_solution(10533503509492962075)
XLA Ops:
  7.2 0.7 stack.9.refs_7_
  7.9 0.7 stack.10
  8.6 0.6 pad_maximum_fusion.gain_pair
  9.2 1.4 multiply_sine_fusion
  10.6 182.3 %attend_forward.1 = (bf16[1024,2560]{1,0:T(8,128)(2,1)}, bf16[1024,2560]{1,0:T(8,128)(2,1)}, f32[1024,1]{1,0:T(8,128)}, f32[8,2560]{1,0:T(8,128)}, bf16[8,80,102...) custom-call(bf16[1024,640]{1,0:T(8,128)(2,1)} %bitcast.21, ...), custom_call_target="tpu_custom_call" | custom-call | flops 18454937600 | bytes 41943040 | tf_op jit(solution)/shard_map/attend_forward/pallas_call | solution.py:1101
  192.9 168.8 %feed_forward.1 = (bf16[1024,2560]{1,0:T(8,128)(2,1)}, bf16[1024,1792]{1,0:T(8,128)(2,1)}, bf16[1024,3584]{1,0:T(8,128)(2,1)}, bf16[4,1024,640]{2,1,0:T(8,128)(2...) custom-call(bf16[640,1024]{1,0:T(8,128)(2,1)} %bitcast.30, ...), custom_call_target="tpu_custom_call" | custom-call | flops 59726888960 | bytes 83886080 | tf_op jit(solution)/shard_map/feed_forward/pallas_call | solution.py:421
  361.7 26.9 %convolution_convert_fusion.refs_7_ = bf16[2560,3584]{1,0:T(8,128)(2,1)} fusion(bf16[1024,2560]{1,0:T(8,128)(2,1)} %get-tuple-element.56, bf16[1024,3584]{1,0:T(8,128)(2,1)} %get-tuple-element.57), kind=kOutput, calls=%fused_computation | convolution fusion | flops 18799656960 | bytes 30932992 | tf_op jit(solution)/shard_map/sd,sf->df/dot_general | solution.py:38
  388.6 0.0 reduce-scatter.6.cloned.1.call-start
  388.7 139.6 %norm_back.1 = (f32[1024,640]{1,0:T(8,128)}, bf16[1024,2560]{1,0:T(8,128)(2,1)}, bf16[640,1024]{1,0:T(8,128)(2,1)}, f32[1,2560]{1,0:T(1,128)}, bf16[2560,1792]{1,0:T(8,128)(2,1)}) custom-call(bf16[1024,2560]{1,0:T(8,128)(2,1)} %get-tuple-element.53.refs_0_, f32[1024,1]{1,0:T(8,128)} %get-tuple-element.45.keep.refs_1_.refs_3_, ...), custom_call_target="tpu_custom_call" | custom-call | flops 12750684160 | bytes 41943040 | tf_op jit(solution)/shard_map/norm_back/pallas_call | solution.py:614
  528.4 97.0 %attend_backward.1 = (bf16[12,80,1024]{2,1,0:T(8,128)(2,1)}, bf16[1024,640]{1,0:T(8,128)(2,1)}, f32[1,640]{1,0:T(1,128)}, bf16[2560,1600]{1,0:T(8,128)(2,1)}) custom-call(bf16[4,1024,640]{2,1,0:T(8,128)(2,1)} %get-tuple-element.49.refs_0_, bf16[8,80,1024]{2,1,0:T(8,128)(2,1)} %get-tuple-element.50.refs_1_, bf16[4,80,2048]{2,1,0:T(8,128)(2,1)} %get-tuple-element.51.refs_2_, ...), custom_call_target="tpu_custom_call" | custom-call | flops 21474836480 | bytes 16777216 | tf_op jit(solution)/shard_map/attend_backward/pallas_call | solution.py:1345
  625.5 2.8 convert_bitcast_fusion
  628.3 97.2 %input_gradient.1 = (bf16[1024,640]{1,0:T(8,128)(2,1)}, f32[8,640]{1,0:T(8,128)}) custom-call(bf16[960,1024]{1,0:T(8,128)(2,1)} %bitcast.20, f32[1024,1]{1,0:T(8,128)} %get-tuple-element.65.refs_1_, f32[8,2560]{1,0:T(8,128)} %get-tuple-element.46.gain.refs_2_, f32[1024,1]{1,0:T(8,128)} %get-tuple-element.45.keep.refs_1_.refs_3_, ...), custom_call_target="tpu_custom_call" | custom-call | flops 5033164800 | bytes 20971520 | tf_op jit(solution)/shard_map/input_gradient/pallas_call | solution.py:1572
  725.5 1.3 slice.26
  728.0 0.7 divide_sqrt_fusion
  728.7 0.6 fusion.2
  729.3 1.4 slice_reduce_fusion
  730.7 2.5 fusion
  733.2 1.4 convert_select_fusion
  734.6 0.2 fusion.1
  734.8 1.3 slice_bitcast_fusion
  736.0 0.8 copy.28
  736.9 0.8 copy.27
  737.7 1.1 copy.31
  738.8 1.1 copy.32
  (18 shorter events, 0.2 us)
Async XLA Ops:
  7.2 521.2 %reduce-scatter.4.cloned.1.call-start = ((), (), s32[]{:S(2)}) async-start(), calls=%async_computation.3 | async-start | bytes 20643840 | tf_op jit(solution)/shard_map/reduce_scatter | solution.py:1646
  7.9 185.0 %copy-start.3 = (f32[1,640]{1,0:T(1,128)}, f32[1,640]{1,0:T(1,128)S(1)}, u32[]{:S(2)}) copy-start(f32[1,640]{1,0:T(1,128)S(1)} %stack.9.refs_7_) | copy-start | bytes 7684
  388.6 236.8 %reduce-scatter.6.cloned.1.call-start = ((), (), s32[]{:S(2)}) async-start(), calls=%async_computation.4 | async-start | bytes 10321920 | tf_op jit(solution)/shard_map/reduce_scatter | solution.py:1646
  528.3 204.9 %reduce-scatter.8.cloned.1.call-start = ((), (), s32[]{:S(2)}) async-start(), calls=%async_computation.5 | async-start | bytes 9584640 | tf_op jit(solution)/shard_map/reduce_scatter | solution.py:1646
  628.3 102.5 %copy-start = (bf16[320,3584]{1,0:T(8,128)(2,1)S(1)}, bf16[320,3584]{1,0:T(8,128)(2,1)}, u32[]{:S(2)}) copy-start(bf16[320,3584]{1,0:T(8,128)(2,1)} %reduce-scatter.4.cloned.1.call-done.refs_12_) | copy-start | bytes 6881284
  734.8 3.0 copy-start.1
  736.0 2.7 copy-start.2
Sparse Core Ops, SparseCore 0:
  388.8 122.5 reduce-scatter.3
  528.4 85.1 reduce-scatter.5
  625.6 75.2 reduce-scatter.7

commit v9 on v8

--- a/solution.py
+++ b/solution.py
@@ -205,7 +205,7 @@
     tiles_f, tiles_d = hidden // tile_f, features // tile_d
     half_f, half_d = -(-tiles_f // 2), -(-tiles_d // 2)
     lag = size - 1 + per - 1
-    ahead, part_slots = per // 2, parts.shape[0]
+    ahead, part_slots = 3 * per // 4, parts.shape[0]
     ticks = max(per * groups + lag, count + size)
 
     def part(c):
@@ -438,7 +438,7 @@
             pltpu.VMEM(w_gate.shape, BF),
             pltpu.VMEM(w_up.shape, BF),
             pltpu.VMEM(w_down.shape, BF),
-            pltpu.VMEM((-(-(per + size - 2 + per // 2) // per), chunk, features), BF),
+            pltpu.VMEM((-(-(per + size - 2 + 3 * per // 4) // per), chunk, features), BF),
             pltpu.VMEM((2, chunk, features), BF),
             pltpu.VMEM((2, hop, features), BF),
             pltpu.VMEM((chunk, features), BF),

time: 755 us -> 751 us (level)
  no operation moved by 1% of the time
where the time goes in v9:
time: 751 us; the launch traced here: 743 us
  Pallas kernels  681 us (91%)
  matrix products  26.9 us (4%)
  between operations  15.6 us (2%)
  local copies, waits for them, and re-layouts  12.4 us (2%)
    pallas_call x1, Pallas kernels, attend_forward(): pl.pallas_call(functools.partial(attend_kernel, size, contexts, chunk, ke...  182 us
    pallas_call x1, Pallas kernels, feed_forward(): pl.pallas_call(functools.partial(ffn_kernel, size, hop, chunk), in_specs=...  166 us
    pallas_call x1, Pallas kernels, norm_back(): pl.pallas_call(kernel, in_specs=[vmem] * 3 + [anywhere] * (4 + len(after)...  139 us
    pallas_call x1, Pallas kernels, attend_backward(): pl.pallas_call(kernel, in_specs=[anywhere] + [vmem] * 9 + [anywhere] * (2...  98.3 us
    pallas_call x1, Pallas kernels, input_gradient(): pl.pallas_call(kernel, in_specs=[vmem] * 10 + [anywhere] * (4 + len(after...  95.9 us
    dot_general x1, matrix products, ein(): return jnp.einsum(spec, a, b, preferred_element_type=F32)  26.9 us
  transfers between devices with their start and end apart: 3, of which 0 were waited for; matrix products, arithmetic and copies ran while one was open for 1% of the time, Pallas kernels for 45%

profile of v9, /device:TPU:0, one launch (start us, length us, event | category | flops | bytes accessed | tf_op | source)
XLA Modules:
  0.0 743.0 jit_solution(11265620150761948666)
XLA Ops:
  7.2 0.7 stack.9.refs_7_
  7.9 0.7 stack.10
  8.6 0.6 pad_maximum_fusion.gain_pair
  9.2 1.4 multiply_sine_fusion
  10.6 182.3 %attend_forward.1 = (bf16[1024,2560]{1,0:T(8,128)(2,1)}, bf16[1024,2560]{1,0:T(8,128)(2,1)}, f32[1024,1]{1,0:T(8,128)}, f32[8,2560]{1,0:T(8,128)}, bf16[8,80,102...) custom-call(bf16[1024,640]{1,0:T(8,128)(2,1)} %bitcast.21, ...), custom_call_target="tpu_custom_call" | custom-call | flops 18454937600 | bytes 41943040 | tf_op jit(solution)/shard_map/attend_forward/pallas_call | solution.py:1101
  192.9 166.1 %feed_forward.1 = (bf16[1024,2560]{1,0:T(8,128)(2,1)}, bf16[1024,1792]{1,0:T(8,128)(2,1)}, bf16[1024,3584]{1,0:T(8,128)(2,1)}, bf16[4,1024,640]{2,1,0:T(8,128)(2...) custom-call(bf16[640,1024]{1,0:T(8,128)(2,1)} %bitcast.30, ...), custom_call_target="tpu_custom_call" | custom-call | flops 59726888960 | bytes 83886080 | tf_op jit(solution)/shard_map/feed_forward/pallas_call | solution.py:421
  359.1 26.9 %convolution_convert_fusion.refs_7_ = bf16[2560,3584]{1,0:T(8,128)(2,1)} fusion(bf16[1024,2560]{1,0:T(8,128)(2,1)} %get-tuple-element.56, bf16[1024,3584]{1,0:T(8,128)(2,1)} %get-tuple-element.57), kind=kOutput, calls=%fused_computation | convolution fusion | flops 18799656960 | bytes 30932992 | tf_op jit(solution)/shard_map/sd,sf->df/dot_general | solution.py:38
  386.0 138.6 %norm_back.1 = (f32[1024,640]{1,0:T(8,128)}, bf16[1024,2560]{1,0:T(8,128)(2,1)}, bf16[640,1024]{1,0:T(8,128)(2,1)}, f32[1,2560]{1,0:T(1,128)}, bf16[2560,1792]{1,0:T(8,128)(2,1)}) custom-call(bf16[1024,2560]{1,0:T(8,128)(2,1)} %get-tuple-element.53.refs_0_, f32[1024,1]{1,0:T(8,128)} %get-tuple-element.45.keep.refs_1_.refs_3_, ...), custom_call_target="tpu_custom_call" | custom-call | flops 12750684160 | bytes 41943040 | tf_op jit(solution)/shard_map/norm_back/pallas_call | solution.py:614
  524.7 0.0 reduce-scatter.8.cloned.1.call-start
  524.7 98.3 %attend_backward.1 = (bf16[12,80,1024]{2,1,0:T(8,128)(2,1)}, bf16[1024,640]{1,0:T(8,128)(2,1)}, f32[1,640]{1,0:T(1,128)}, bf16[2560,1600]{1,0:T(8,128)(2,1)}) custom-call(bf16[4,1024,640]{2,1,0:T(8,128)(2,1)} %get-tuple-element.49.refs_0_, bf16[8,80,1024]{2,1,0:T(8,128)(2,1)} %get-tuple-element.50.refs_1_, bf16[4,80,2048]{2,1,0:T(8,128)(2,1)} %get-tuple-element.51.refs_2_, ...), custom_call_target="tpu_custom_call" | custom-call | flops 21474836480 | bytes 16777216 | tf_op jit(solution)/shard_map/attend_backward/pallas_call | solution.py:1345
  623.1 2.8 convert_bitcast_fusion
  625.8 95.9 %input_gradient.1 = (bf16[1024,640]{1,0:T(8,128)(2,1)}, f32[8,640]{1,0:T(8,128)}) custom-call(bf16[960,1024]{1,0:T(8,128)(2,1)} %bitcast.20, f32[1024,1]{1,0:T(8,128)} %get-tuple-element.65.refs_1_, f32[8,2560]{1,0:T(8,128)} %get-tuple-element.46.gain.refs_2_, f32[1024,1]{1,0:T(8,128)} %get-tuple-element.45.keep.refs_1_.refs_3_, ...), custom_call_target="tpu_custom_call" | custom-call | flops 5033164800 | bytes 20971520 | tf_op jit(solution)/shard_map/input_gradient/pallas_call | solution.py:1572
  721.7 1.3 slice.26
  724.3 0.7 divide_sqrt_fusion
  725.0 0.6 fusion.2
  725.6 1.4 slice_reduce_fusion
  727.0 2.5 fusion
  729.5 1.4 convert_select_fusion
  730.9 0.2 fusion.1
  731.0 1.3 slice_bitcast_fusion
  732.3 0.8 copy.28
  733.1 0.8 copy.27
  734.0 1.1 copy.31
  735.0 1.1 copy.32
  (18 shorter events, 0.2 us)
Async XLA Ops:
  7.2 517.5 %reduce-scatter.4.cloned.1.call-start = ((), (), s32[]{:S(2)}) async-start(), calls=%async_computation.3 | async-start | bytes 20643840 | tf_op jit(solution)/shard_map/reduce_scatter | solution.py:1646
  7.9 185.0 %copy-start.3 = (f32[1,640]{1,0:T(1,128)}, f32[1,640]{1,0:T(1,128)S(1)}, u32[]{:S(2)}) copy-start(f32[1,640]{1,0:T(1,128)S(1)} %stack.9.refs_7_) | copy-start | bytes 7684
  386.0 237.1 %reduce-scatter.6.cloned.1.call-start = ((), (), s32[]{:S(2)}) async-start(), calls=%async_computation.4 | async-start | bytes 10321920 | tf_op jit(solution)/shard_map/reduce_scatter | solution.py:1646
  524.7 204.8 %reduce-scatter.8.cloned.1.call-start = ((), (), s32[]{:S(2)}) async-start(), calls=%async_computation.5 | async-start | bytes 9584640 | tf_op jit(solution)/shard_map/reduce_scatter | solution.py:1646
  625.8 101.1 %copy-start = (bf16[320,3584]{1,0:T(8,128)(2,1)S(1)}, bf16[320,3584]{1,0:T(8,128)(2,1)}, u32[]{:S(2)}) copy-start(bf16[320,3584]{1,0:T(8,128)(2,1)} %reduce-scatter.4.cloned.1.call-done.refs_12_) | copy-start | bytes 6881284
  731.0 3.0 copy-start.1
  732.3 2.7 copy-start.2
Sparse Core Ops, SparseCore 0:
  386.1 123.5 reduce-scatter.3
  524.8 86.8 reduce-scatter.5
  623.1 73.7 reduce-scatter.7
